TPU v7x, 32 devices: a whole 2x2x4 slice. The times are simulated.
32 devices in a mesh: dp: 8 (over z, x), rows: 4 (over y, core).
Axes of the slice: x: 2, y: 2, z: 4, core: 2. Of those that a mesh axis runs over, the one named last changes fastest.
Arguments:
- activations: bfloat16 [16384, 8192], P('dp', 'rows'), may hold values from -6 to 6
- key_grads: bfloat16 [16384, 1024], P('dp'), may hold values from -0.125 to 0.125
- momentum: float32 [8, 8192, 1024], P('dp', 'rows'), may hold values from -6 to 6
- basis: float32 [1024, 128], replicated, may hold values from -0.1875 to 0.1875
Outputs:
- new_momentum: float32 [8, 8192, 1024], P('dp', 'rows')
- new_basis: float32 [1024, 128], P('rows')
- update: bfloat16 [8192, 1024], P(('rows', 'dp'))
All inputs are finite; a program needn't handle non-finite values.
Results may differ from a plain program's by a relative error of at most 0.0015.
Values sent between devices are 32-bit elements; how exact they have to be, the bound alone decides.
No kernel may reach another device: no remote copies, remote signals or barrier semaphores. Data moves between devices by JAX's collectives and lax.ppermute only.
A program may use at most 64 MiB of HBM per device.

v0:
```python
import math

import jax
import jax.numpy as jnp
from jax import lax
from jax.sharding import PartitionSpec as P

D = 8192
KV = 1024
RANK = 128


def body(activations, key_grads, momentum, basis):
    high = lax.Precision.HIGHEST
    n_dp = lax.axis_size("dp")
    n_rows = lax.axis_size("rows")
    grad = lax.dot_general(
        activations, key_grads, (((0,), (0,)), ((), ())), preferred_element_type=jnp.float32
    )
    blended = momentum[0] + grad
    local_rows = blended.shape[0]
    own_count = local_rows // n_dp
    sketch = jnp.dot(blended, basis, precision=high)
    total = lax.psum(sketch, "dp") / n_dp
    gram = lax.psum(jnp.dot(total.T, total, precision=high), "rows")
    lower = jnp.linalg.cholesky(gram)
    ortho = lax.linalg.triangular_solve(lower, total, left_side=False, lower=True, transpose_a=True)
    own_rows = lax.dynamic_slice_in_dim(ortho, lax.axis_index("dp") * own_count, own_count, 0)
    partial_coeff = lax.dot_general(
        blended, ortho, (((0,), (0,)), ((), ())), precision=high, preferred_element_type=jnp.float32
    )
    row_total = lax.psum(partial_coeff, "rows")
    coeff = lax.psum(row_total, "dp") / n_dp
    feedback = lax.dot_general(
        ortho, coeff, (((1,), (1,)), ((), ())), precision=high, preferred_element_type=jnp.float32
    )
    new_momentum = (blended - 0.2 * feedback)[None]
    col_norm = jnp.sqrt(jnp.sum(coeff * coeff, axis=0) + 1e-06)
    normed = coeff / col_norm
    basis_rows = normed.shape[0] // n_rows
    new_basis = lax.dynamic_slice_in_dim(normed, lax.axis_index("rows") * basis_rows, basis_rows, 0)
    scale = math.sqrt(D * KV / RANK)
    update = scale * lax.dot_general(
        own_rows,
        normed,
        (((1,), (1,)), ((), ())),
        precision=high,
        preferred_element_type=jnp.float32,
    )
    return (new_momentum, new_basis, update.astype(jnp.bfloat16))


def solution(mesh):
    in_specs = (P("dp", "rows"), P("dp", None), P("dp", "rows", None), P())
    out_specs = (P("dp", "rows", None), P("rows", None), P(("rows", "dp"), None))
    return jax.shard_map(body, mesh=mesh, in_specs=in_specs, out_specs=out_specs, check_vma=False)
```

profile of v0, /device:TPU:0, one launch (start us, length us, event | category | flops | bytes accessed | tf_op | source)
XLA Modules:
  0.0 322.8 jit_solution(4011536179580406112)
XLA Ops:
  7.2 0.0 copy-start
  7.2 0.0 all-reduce.5.cloned.1.call-start
  7.2 13.9 %bitcast_add_fusion = f32[2048,1024]{1,0:T(8,128)S(1)} fusion(f32[1,2048,1024]{2,1,0:T(8,128)} %param.6, bf16[2048,2048]{1,0:T(8,128)(2,1)} %param.4, bf16[2048,1024]{1,0:T(8,128)(2,1)} %param.5), kind=kOutput, calls=%fused_computation | convolution fusion | flops 8592031744 | bytes 29360128 | tf_op jit(solution)/shard_map/dot_general | solution.py:17
  21.1 0.0 copy-start.1
  21.1 3.4 %copy-done.1 = f32[2048,1024]{1,0:T(8,128)} copy-done((f32[2048,1024]{1,0:T(8,128)}, f32[2048,1024]{1,0:T(8,128)S(1)}, u32[]{:S(2)}) %copy-start.1) | copy-done | bytes 8388632
  24.5 0.0 copy-done
  24.5 7.8 %fusion.17 = f32[2048,128]{1,0:T(8,128)} fusion(f32[2048,1024]{1,0:T(8,128)S(1)} %bitcast_add_fusion, f32[1024,128]{1,0:T(8,128)S(1)} %copy-done), kind=kOutput, calls=%fused_computation.30 | convolution fusion | flops 3221225472 | bytes 9961472 | tf_op jit(solution)/shard_map/dot_general | solution.py:23
  32.3 0.0 all-reduce.5.cloned.1.call-update
  32.3 0.2 all-reduce.7.cloned.1.call-start
  32.6 80.6 %all-reduce.5.cloned.1.call-done = f32[2048,128]{1,0:T(8,128)} async-done(((f32[2048,128]{1,0:T(8,128)}), f32[2048,128]{1,0:T(8,128)}) %all-reduce.5.cloned.1.call-update) | async-done | bytes 1048592 | tf_op jit(solution)/shard_map/psum | solution.py:24
  113.2 4.0 %fusion.3 = f32[128,128]{0,1:T(8,128)} fusion(f32[2048,128]{1,0:T(8,128)} %all-reduce.5.cloned.1.call-done), kind=kOutput, calls=%fused_computation.6 | convolution fusion | flops 402915328 | bytes 1114112 | tf_op jit(solution)/shard_map/dot_general | solution.py:25
  117.2 0.0 all-reduce.7.cloned.1.call-update
  117.2 0.0 all-reduce.9.cloned.1.call-start
  117.3 30.8 %all-reduce.7.cloned.1.call-done = f32[128,128]{0,1:T(8,128)} async-done(((f32[128,128]{0,1:T(8,128)}), f32[128,128]{0,1:T(8,128)}) %all-reduce.7.cloned.1.call-update) | async-done | bytes 65552 | tf_op jit(solution)/shard_map/psum | solution.py:25
  148.0 0.9 copy.8
  149.0 0.9 fusion.12
  149.8 11.7 %cholesky.16 = f32[128,128]{1,0:T(8,128)S(1)} custom-call(f32[128,128]{1,0:T(8,128)S(1)} %fusion.12), custom_call_target="Cholesky" | custom-call | tf_op jit(solution)/shard_map/jit(cholesky)/cholesky | solution.py:26
  161.6 0.6 compare_reduce_fusion
  162.2 0.7 fusion.10
  162.9 9.8 %custom-call.6 = f32[1,128,128]{1,2,0:T(8,128)S(1)} custom-call(f32[1,128,128]{2,1,0:T(8,128)S(1)} %fusion.10), custom_call_target="InvertDiagBlocksLowerTriangular" | custom-call | tf_op jit(solution)/shard_map/triangular_solve | solution.py:27
  172.7 2.2 fusion.1
  174.9 16.4 %fusion.18 = f32[1024,128]{1,0:T(8,128)} fusion(f32[2048,1024]{1,0:T(8,128)} %copy-done.1, f32[2048,128]{1,0:T(8,128)S(1)} %fusion.1), kind=kOutput, calls=%fused_computation.31 | convolution fusion | flops 3221225472 | bytes 9961472 | tf_op jit(solution)/shard_map/dot_general | solution.py:29
  191.3 0.0 all-reduce.9.cloned.1.call-update
  191.4 0.0 all-reduce.11.cloned.1.call-start
  191.4 33.3 %all-reduce.9.cloned.1.call-done = f32[1024,128]{1,0:T(8,128)} async-done(((f32[1024,128]{1,0:T(8,128)}), f32[1024,128]{1,0:T(8,128)}) %all-reduce.9.cloned.1.call-update) | async-done | bytes 524304 | tf_op jit(solution)/shard_map/psum | solution.py:32
  224.7 0.0 all-reduce.11.cloned.1.call-update
  224.7 75.6 %all-reduce.11.cloned.1.call-done = f32[1024,128]{1,0:T(8,128)} async-done(((f32[1024,128]{1,0:T(8,128)}), f32[1024,128]{1,0:T(8,128)}) %all-reduce.11.cloned.1.call-update) | async-done | bytes 524304 | tf_op jit(solution)/shard_map/psum | solution.py:33
  300.4 1.2 multiply_reduce_fusion
  301.6 1.1 multiply_divide_fusion
  302.7 1.8 fusion
  304.4 0.7 constant_dynamic-slice_fusion
  305.1 11.2 %subtract_bitcast_fusion = f32[1,2048,1024]{2,1,0:T(8,128)} fusion(f32[2048,1024]{1,0:T(8,128)} %copy-done.1, f32[2048,128]{1,0:T(8,128)S(1)} %fusion.1, f32[1024,128]{1,0:T(8,128)} %all-reduce.11.cloned.1.call-done), kind=kOutput, calls=%fused_computation.1 | convolution fusion | flops 3225550848 | bytes 18350080 | tf_op jit(solution)/shard_map/dot_general | solution.py:34
  (2 shorter events, 0.0 us)
Async XLA Ops:
  7.2 17.4 %copy-start = (f32[1024,128]{1,0:T(8,128)S(1)}, f32[1024,128]{1,0:T(8,128)}, u32[]{:S(2)}) copy-start(f32[1024,128]{1,0:T(8,128)} %param.7) | copy-start | bytes 1572868
  7.2 106.0 %all-reduce.5.cloned.1.call-start = ((), (), s32[]{:S(2)}) async-start(), calls=%async_computation | async-start | bytes 2097152 | tf_op jit(solution)/shard_map/psum | solution.py:24
  21.1 3.4 %copy-start.1 = (f32[2048,1024]{1,0:T(8,128)}, f32[2048,1024]{1,0:T(8,128)S(1)}, u32[]{:S(2)}) copy-start(f32[2048,1024]{1,0:T(8,128)S(1)} %bitcast_add_fusion) | copy-start | bytes 25165828
  32.3 115.7 %all-reduce.7.cloned.1.call-start = ((), (), s32[]{:S(2)}) async-start(), calls=%async_computation.1 | async-start | bytes 131072 | tf_op jit(solution)/shard_map/psum | solution.py:25
  117.2 107.5 %all-reduce.9.cloned.1.call-start = ((), (), s32[]{:S(2)}) async-start(), calls=%async_computation.2 | async-start | bytes 1048576 | tf_op jit(solution)/shard_map/psum | solution.py:32
  191.4 109.0 %all-reduce.11.cloned.1.call-start = ((), (), s32[]{:S(2)}) async-start(), calls=%async_computation.3 | async-start | bytes 1048576 | tf_op jit(solution)/shard_map/psum | solution.py:33
Sparse Core Ops, SparseCore 0:
  32.5 80.6 all-reduce.4
  117.3 30.6 all-reduce.6
  191.5 33.1 all-reduce.8
  228.0 72.3 all-reduce.10
where the time goes:
time: 323 us
  waiting for transfers between devices  220 us (68%)
  matrix products  57.3 us (18%)
  other arithmetic  26 us (8%)
  between operations  13.8 us (4%)
  local copies, waits for them, and re-layouts  4.99 us (2%)
    psum x1, waiting for transfers between devices, body(): total = lax.psum(sketch, 'dp') / n_dp  80.6 us
    psum x1, waiting for transfers between devices, body(): coeff = lax.psum(row_total, 'dp') / n_dp  75.6 us
    psum x1, waiting for transfers between devices, body(): row_total = lax.psum(partial_coeff, 'rows')  33.3 us
    psum x1, waiting for transfers between devices, body(): gram = lax.psum(jnp.dot(total.T, total, precision=high), 'rows')  30.8 us
    dot_general x1, matrix products, body(): lax.dot_general(blended, ortho, (((0,), (0,)), ((), ())), precision=high,...  16.4 us
    dot_general x1, matrix products, body(): lax.dot_general(activations, key_grads, (((0,), (0,)), ((), ())), preferr...  13.9 us
    another operation x3, other arithmetic, body(): lower = jnp.linalg.cholesky(gram)  12.4 us
    dot_general x1, matrix products, body(): lax.dot_general(ortho, coeff, (((1,), (1,)), ((), ())), precision=high, p...  11.2 us
  transfers between devices with their start and end apart: 4, of which 4 were waited for; matrix products, arithmetic and copies ran while one was open for 0% of the time, Pallas kernels for 0%

commit v1 on v0

v1 whole, which is shorter than its diff:
```python
import math

import jax
import jax.numpy as jnp
from jax import lax
from jax.sharding import PartitionSpec as P

HIGH = lax.Precision.HIGH
HIGHEST = lax.Precision.HIGHEST


def swap(value, axis, mask):
    count = lax.axis_size(axis)
    return lax.ppermute(value, axis, [(i, i ^ mask) for i in range(count)])


def bits_of(count):
    return [1 << b for b in range(count.bit_length() - 1)]


def halve(value, axis, mask):
    half = value.shape[0] // 2
    bit = jnp.where((lax.axis_index(axis) & mask) != 0, 1, 0)
    keep = lax.dynamic_slice_in_dim(value, bit * half, half, 0)
    give = lax.dynamic_slice_in_dim(value, (1 - bit) * half, half, 0)
    return keep + swap(give, axis, mask)


def double(value, axis, mask):
    other = swap(value, axis, mask)
    mine_first = (lax.axis_index(axis) & mask) == 0
    return jnp.concatenate([jnp.where(mine_first, value, other), jnp.where(mine_first, other, value)], 0)


def body(activations, key_grads, momentum, basis):
    n_dp = lax.axis_size("dp")
    n_rows = lax.axis_size("rows")
    dp = lax.axis_index("dp")
    grad = lax.dot_general(
        activations, key_grads, (((0,), (0,)), ((), ())), preferred_element_type=jnp.float32
    )
    blended = momentum[0] + grad
    local_rows = blended.shape[0]
    kv = blended.shape[1]
    rank = basis.shape[1]
    sketch = jnp.dot(blended, basis, precision=HIGH)

    group = min(4, n_dp)
    low = dp & (group - 1)
    block = local_rows // group
    parts = [lax.dynamic_slice_in_dim(sketch, (low ^ s) * block, block, 0) for s in range(group)]
    own = parts[0]
    for s in range(group - 1, 0, -1):
        own = own + swap(parts[s], "dp", s)
    for mask in bits_of(n_dp):
        if mask >= group:
            own = own + swap(own, "dp", mask)
    own = own / n_dp
    total = jnp.zeros((local_rows, rank), jnp.float32)
    total = lax.dynamic_update_slice_in_dim(total, own, low * block, 0)
    for s in range(group - 1, 0, -1):
        total = lax.dynamic_update_slice_in_dim(total, swap(own, "dp", s), (low ^ s) * block, 0)

    right = lax.dot_general(
        blended, total, (((0,), (0,)), ((), ())), precision=HIGH, preferred_element_type=jnp.float32
    ) / n_dp
    gram = lax.dot_general(
        own, own, (((0,), (0,)), ((), ())), precision=HIGHEST, preferred_element_type=jnp.float32
    ) * (group / n_dp)
    both = jnp.concatenate([right, gram], 0)
    steps = [("rows", m) for m in bits_of(n_rows)] + [("dp", 1)]
    for axis, mask in steps:
        both = halve(both, axis, mask)
    for mask in bits_of(n_dp)[1:]:
        both = both + swap(both, "dp", mask)
    for axis, mask in steps[::-1]:
        both = double(both, axis, mask)
    right, gram = both[:kv], both[kv:]

    lower = jnp.linalg.cholesky(gram)
    inverse = lax.linalg.triangular_solve(lower, jnp.eye(rank, dtype=jnp.float32), left_side=True, lower=True)
    coeff = lax.dot_general(right, inverse, (((1,), (1,)), ((), ())), precision=HIGHEST)
    middle = jnp.dot(coeff, inverse, precision=HIGHEST)
    feedback = lax.dot_general(
        total, middle, (((1,), (1,)), ((), ())), precision=HIGH, preferred_element_type=jnp.float32
    )
    new_momentum = (blended - 0.2 * feedback)[None]
    col_norm = jnp.sqrt(jnp.sum(coeff * coeff, axis=0) + 1e-06)
    normed = coeff / col_norm
    basis_rows = kv // n_rows
    new_basis = lax.dynamic_slice_in_dim(normed, lax.axis_index("rows") * basis_rows, basis_rows, 0)
    own_count = local_rows // n_dp
    own_rows = lax.dynamic_slice_in_dim(total, dp * own_count, own_count, 0)
    own_ortho = lax.dot_general(own_rows, inverse, (((1,), (1,)), ((), ())), precision=HIGHEST)
    scale = math.sqrt(local_rows * n_rows * kv / rank)
    update = scale * lax.dot_general(
        own_ortho, normed, (((1,), (1,)), ((), ())), precision=HIGHEST, preferred_element_type=jnp.float32
    )
    return (new_momentum, new_basis, update.astype(jnp.bfloat16))


def solution(mesh):
    in_specs = (P("dp", "rows"), P("dp", None), P("dp", "rows", None), P())
    out_specs = (P("dp", "rows", None), P("rows", None), P(("rows", "dp"), None))
    return jax.shard_map(body, mesh=mesh, in_specs=in_specs, out_specs=out_specs, check_vma=False)
```

time: 323 us -> 149 us (0.46)
  waiting for transfers between devices: 220 us -> 62.5 us
  matrix products: 57.3 us -> 35.9 us
  starting transfers between devices: 0.34 us -> 20.6 us
  between operations: 13.8 us -> 0.94 us
    psum x4 -> x0, waiting for transfers between devices: 220 us -> none  [the longest x1 80.6 us: body(): total = lax.psum(sketch, 'dp') / n_dp]
    ppermute x0 -> x15, waiting for transfers between devices: none -> 62.5 us  [swap(): return lax.ppermute(value, axis, [(i, i ^ mask) for i in range(count)])]
    ppermute x0 -> x15, starting transfers between devices: none -> 20.6 us  [swap(): return lax.ppermute(value, axis, [(i, i ^ mask) for i in range(count)])]
    dot_general x5 -> x8, matrix products: 41.2 us -> 21.5 us  [the longest x1 8.16 us: body(): lax.dot_general(total, middle, (((1,), (1,)), ((), ())), precision=HIGH,...]
  transfers between devices with their start and end apart: 4 -> 15, of which waited for: 4 -> 13; matrix products, arithmetic and copies ran while one was open for 0% -> 0% of each run, Pallas kernels for 0% -> 0%
where the time goes in v1:
time: 149 us
  waiting for transfers between devices  62.5 us (42%)
  matrix products  35.9 us (24%)
  other arithmetic  24.5 us (16%)
  starting transfers between devices  20.6 us (14%)
  local copies, waits for them, and re-layouts  4.75 us (3%)
    ppermute x15, waiting for transfers between devices, swap(): return lax.ppermute(value, axis, [(i, i ^ mask) for i in range(count)])  62.5 us
    ppermute x15, starting transfers between devices, swap(): return lax.ppermute(value, axis, [(i, i ^ mask) for i in range(count)])  20.6 us
    dot_general x1, matrix products, body(): lax.dot_general(activations, key_grads, (((0,), (0,)), ((), ())), preferr...  14.1 us
    another operation x3, other arithmetic, body(): lower = jnp.linalg.cholesky(gram)  12.6 us
    another operation x2, other arithmetic, body(): lax.linalg.triangular_solve(lower, jnp.eye(rank, dtype=jnp.float32), left...  10.5 us
    dot_general x1, matrix products, body(): lax.dot_general(total, middle, (((1,), (1,)), ((), ())), precision=HIGH,...  8.16 us
    dot_general x1, matrix products, body(): lax.dot_general(blended, total, (((0,), (0,)), ((), ())), precision=HIGH,...  5.62 us
    dot_general x1, matrix products, body(): sketch = jnp.dot(blended, basis, precision=HIGH)  3.43 us
  transfers between devices with their start and end apart: 15, of which 13 were waited for; matrix products, arithmetic and copies ran while one was open for 0% of the time, Pallas kernels for 0%

profile of v1, /device:TPU:0, one launch (start us, length us, event | category | flops | bytes accessed | tf_op | source)
XLA Modules:
  0.0 149.1 jit_solution(17722157733989125989)
XLA Ops:
  0.7 14.1 %bitcast_add_fusion = f32[2048,1024]{1,0:T(8,128)S(1)} fusion(f32[1,2048,1024]{2,1,0:T(8,128)} %param.6, bf16[2048,2048]{1,0:T(8,128)(2,1)} %param.4, bf16[2048,1024]{1,0:T(8,128)(2,1)} %param.5), kind=kOutput, calls=%fused_computation | convolution fusion | flops 8592031744 | bytes 29360128 | tf_op jit(solution)/shard_map/dot_general | solution.py:39
  14.8 3.4 %copy-done.1 = f32[2048,1024]{1,0:T(8,128)} copy-done((f32[2048,1024]{1,0:T(8,128)}, f32[2048,1024]{1,0:T(8,128)S(1)}, u32[]{:S(2)}) %copy-start.1) | copy-done | bytes 8388632
  18.2 3.4 %fusion.14 = f32[2048,128]{1,0:T(8,128)S(1)} fusion(f32[2048,1024]{1,0:T(8,128)S(1)} %bitcast_add_fusion, f32[1024,128]{1,0:T(8,128)S(1)} %copy-done), kind=kOutput, calls=%fused_computation.55 | convolution fusion | flops 1610612736 | bytes 9961472 | tf_op jit(solution)/shard_map/dot_general | solution.py:46
  21.7 4.0 %collective-permute-start = (f32[512,128]{1,0:T(8,128)S(1)}, f32[512,128]{1,0:T(8,128)S(1)}, u32[]{:S(2)}, u32[]{:S(2)}) collective-permute-start(f32[512,128]{1,0:T(8,128)S(1)} %get-tuple-element.5), channel_id=1, source_target_pairs={{0,12},{4,8},{8,4},{12,0},{16,28},{20,24},{24,20},{28,16},{1,13},{... | collective-permute-start | bytes 786440 | tf_op jit(solution)/shard_map/ppermute | solution.py:14
  25.7 0.4 collective-permute-start.1
  26.1 0.2 collective-permute-start.2
  26.3 6.5 %collective-permute-done = f32[512,128]{1,0:T(8,128)S(1)} collective-permute-done((f32[512,128]{1,0:T(8,128)S(1)}, f32[512,128]{1,0:T(8,128)S(1)}, u32[]{:S(2)}, u32[]{:S(2)}) %collective-permute-start) | collective-permute-done | bytes 262176 | tf_op jit(solution)/shard_map/ppermute | solution.py:14
  32.8 5.0 %collective-permute-done.1 = f32[512,128]{1,0:T(8,128)S(1)} collective-permute-done((f32[512,128]{1,0:T(8,128)S(1)}, f32[512,128]{1,0:T(8,128)S(1)}, u32[]{:S(2)}, u32[]{:S(2)}) %collective-permute-start.1) | collective-permute-done | bytes 262176 | tf_op jit(solution)/shard_map/ppermute | solution.py:14
  37.9 2.7 %collective-permute-start.3 = (f32[512,128]{1,0:T(8,128)S(1)}, f32[512,128]{1,0:T(8,128)S(1)}, u32[]{:S(2)}, u32[]{:S(2)}) collective-permute-start(f32[512,128]{1,0:T(8,128)S(1)} %add_add_fusion), channel_id=1, source_target_pairs={{0,16},{4,20},{8,24},{12,28},{16,0},{20,4},{24,8},{28,12},{1,17},{... | collective-permute-start | bytes 786440 | tf_op jit(solution)/shard_map/ppermute | solution.py:14
  40.5 12.0 %collective-permute-done.3 = f32[512,128]{1,0:T(8,128)S(1)} collective-permute-done((f32[512,128]{1,0:T(8,128)S(1)}, f32[512,128]{1,0:T(8,128)S(1)}, u32[]{:S(2)}, u32[]{:S(2)}) %collective-permute-start.3) | collective-permute-done | bytes 262176 | tf_op jit(solution)/shard_map/ppermute | solution.py:14
  52.7 1.7 %collective-permute-start.4 = (f32[512,128]{1,0:T(8,128)S(1)}, f32[512,128]{1,0:T(8,128)S(1)}, u32[]{:S(2)}, u32[]{:S(2)}) collective-permute-start(f32[512,128]{1,0:T(8,128)S(1)} %get-tuple-element.4), channel_id=1, source_target_pairs={{0,12},{4,8},{8,4},{12,0},{16,28},{20,24},{24,20},{28,16},{1,13},{... | collective-permute-start | bytes 786440 | tf_op jit(solution)/shard_map/ppermute | solution.py:14
  54.4 1.4 collective-permute-start.5
  55.8 0.5 collective-permute-start.6
  56.2 0.6 convolution_multiply_fusion.2
  56.9 6.0 %collective-permute-done.4 = f32[512,128]{1,0:T(8,128)S(1)} collective-permute-done((f32[512,128]{1,0:T(8,128)S(1)}, f32[512,128]{1,0:T(8,128)S(1)}, u32[]{:S(2)}, u32[]{:S(2)}) %collective-permute-start.4) | collective-permute-done | bytes 262176 | tf_op jit(solution)/shard_map/ppermute | solution.py:14
  63.0 3.8 %collective-permute-done.5 = f32[512,128]{1,0:T(8,128)S(1)} collective-permute-done((f32[512,128]{1,0:T(8,128)S(1)}, f32[512,128]{1,0:T(8,128)S(1)}, u32[]{:S(2)}, u32[]{:S(2)}) %collective-permute-start.5) | collective-permute-done | bytes 262176 | tf_op jit(solution)/shard_map/ppermute | solution.py:14
  66.8 5.6 %convolution_multiply_fusion.1 = f32[1024,128]{0,1:T(8,128)S(1)} fusion(f32[2048,1024]{1,0:T(8,128)} %copy-done.1, f32[2048,128]{1,0:T(8,128)S(1)} %constant_dynamic-update-slice_fusion), kind=kOutput, calls=%fused_computation.4 | convolution fusion | flops 1610743808 | bytes 9961472 | tf_op jit(solution)/shard_map/dot_general | solution.py:64
  72.5 0.2 fusion.3
  72.8 1.6 %collective-permute-done.7 = f32[576,128]{0,1:T(8,128)S(1)} collective-permute-done((f32[576,128]{0,1:T(8,128)S(1)}, f32[576,128]{0,1:T(8,128)S(1)}, u32[]{:S(2)}, u32[]{:S(2)}) %collective-permute-start.7) | collective-permute-done | bytes 294944 | tf_op jit(solution)/shard_map/ppermute | solution.py:14
  74.4 0.2 fusion.5
  74.7 0.1 constant_dynamic-slice_fusion.2
  74.8 1.6 %collective-permute-start.8 = (f32[288,128]{0,1:T(8,128)S(1)}, f32[288,128]{0,1:T(8,128)S(1)}, u32[]{:S(2)}, u32[]{:S(2)}) collective-permute-start(f32[288,128]{0,1:T(8,128)S(1)} %constant_dynamic-slice_fusion.2), channel_id=1, source_target_pairs={{0,2},{1,3},{2,0},{3,1},{4,6},{5,7},{6,4},{7,5},{8,10},{9,11},{10,... | collective-permute-start | bytes 442376 | tf_op jit(solution)/shard_map/ppermute | solution.py:14
  76.4 5.4 %collective-permute-done.8 = f32[288,128]{0,1:T(8,128)S(1)} collective-permute-done((f32[288,128]{0,1:T(8,128)S(1)}, f32[288,128]{0,1:T(8,128)S(1)}, u32[]{:S(2)}, u32[]{:S(2)}) %collective-permute-start.8) | collective-permute-done | bytes 147488 | tf_op jit(solution)/shard_map/ppermute | solution.py:14
  81.8 0.1 dynamic-slice_add_fusion
  81.9 0.1 constant_dynamic-slice_fusion.1
  82.0 1.4 collective-permute-start.9
  83.5 3.6 %collective-permute-done.9 = f32[144,128]{0,1:T(8,128)S(1)} collective-permute-done((f32[144,128]{0,1:T(8,128)S(1)}, f32[144,128]{0,1:T(8,128)S(1)}, u32[]{:S(2)}, u32[]{:S(2)}) %collective-permute-start.9) | collective-permute-done | bytes 73760 | tf_op jit(solution)/shard_map/ppermute | solution.py:14
  87.2 1.6 %collective-permute-start.10 = (f32[144,128]{0,1:T(8,128)S(1)}, f32[144,128]{0,1:T(8,128)S(1)}, u32[]{:S(2)}, u32[]{:S(2)}) collective-permute-start(f32[144,128]{0,1:T(8,128)S(1)} %dynamic-slice_add_fusion.1), channel_id=1, source_target_pairs={{0,8},{4,12},{8,0},{12,4},{16,24},{20,28},{24,16},{28,20},{1,9},{5... | collective-permute-start | bytes 221192 | tf_op jit(solution)/shard_map/ppermute | solution.py:14
  88.8 3.4 %collective-permute-done.10 = f32[144,128]{0,1:T(8,128)S(1)} collective-permute-done((f32[144,128]{0,1:T(8,128)S(1)}, f32[144,128]{0,1:T(8,128)S(1)}, u32[]{:S(2)}, u32[]{:S(2)}) %collective-permute-start.10) | collective-permute-done | bytes 73760 | tf_op jit(solution)/shard_map/ppermute | solution.py:14
  92.2 3.3 %collective-permute-start.11 = (f32[144,128]{0,1:T(8,128)S(1)}, f32[144,128]{0,1:T(8,128)S(1)}, u32[]{:S(2)}, u32[]{:S(2)}) collective-permute-start(f32[144,128]{0,1:T(8,128)S(1)} %add.109), channel_id=1, source_target_pairs={{0,16},{4,20},{8,24},{12,28},{16,0},{20,4},{24,8},{28,12},{1,17},{... | collective-permute-start | bytes 221192 | tf_op jit(solution)/shard_map/ppermute | solution.py:14
  95.6 4.4 %collective-permute-done.11 = f32[144,128]{0,1:T(8,128)S(1)} collective-permute-done((f32[144,128]{0,1:T(8,128)S(1)}, f32[144,128]{0,1:T(8,128)S(1)}, u32[]{:S(2)}, u32[]{:S(2)}) %collective-permute-start.11) | collective-permute-done | bytes 73760 | tf_op jit(solution)/shard_map/ppermute | solution.py:14
  100.0 4.9 %collective-permute-done.12 = f32[144,128]{0,1:T(8,128)S(1)} collective-permute-done((f32[144,128]{0,1:T(8,128)S(1)}, f32[144,128]{0,1:T(8,128)S(1)}, u32[]{:S(2)}, u32[]{:S(2)}) %collective-permute-start.12) | collective-permute-done | bytes 73760 | tf_op jit(solution)/shard_map/ppermute | solution.py:14
  105.1 1.6 %collective-permute-start.13 = (f32[288,128]{0,1:T(8,128)S(1)}, f32[288,128]{0,1:T(8,128)S(1)}, u32[]{:S(2)}, u32[]{:S(2)}) collective-permute-start(f32[288,128]{0,1:T(8,128)S(1)} %pad_maximum_fusion.3), channel_id=1, source_target_pairs={{0,2},{1,3},{2,0},{3,1},{4,6},{5,7},{6,4},{7,5},{8,10},{9,11},{10,... | collective-permute-start | bytes 442376 | tf_op jit(solution)/shard_map/ppermute | solution.py:14
  106.7 4.2 %collective-permute-done.13 = f32[288,128]{0,1:T(8,128)S(1)} collective-permute-done((f32[288,128]{0,1:T(8,128)S(1)}, f32[288,128]{0,1:T(8,128)S(1)}, u32[]{:S(2)}, u32[]{:S(2)}) %collective-permute-start.13) | collective-permute-done | bytes 147488 | tf_op jit(solution)/shard_map/ppermute | solution.py:14
  110.9 0.1 pad_maximum_fusion.2
  111.1 1.6 %collective-permute-done.14 = f32[576,128]{0,1:T(8,128)S(1)} collective-permute-done((f32[576,128]{0,1:T(8,128)S(1)}, f32[576,128]{0,1:T(8,128)S(1)}, u32[]{:S(2)}, u32[]{:S(2)}) %collective-permute-start.14) | collective-permute-done | bytes 294944 | tf_op jit(solution)/shard_map/ppermute | solution.py:14
  112.8 0.1 broadcast_select_fusion.1
  113.2 11.9 %cholesky.17 = f32[128,128]{1,0:T(8,128)S(1)} custom-call(f32[128,128]{1,0:T(8,128)S(1)} %fusion.11), custom_call_target="Cholesky" | custom-call | tf_op jit(solution)/shard_map/jit(cholesky)/cholesky | solution.py:80
  125.1 0.6 compare_reduce_fusion
  125.7 0.7 fusion.8
  126.4 9.8 %custom-call.6 = f32[1,128,128]{1,2,0:T(8,128)S(1)} custom-call(f32[1,128,128]{2,1,0:T(8,128)S(1)} %fusion.8), custom_call_target="InvertDiagBlocksLowerTriangular" | custom-call | tf_op jit(solution)/shard_map/triangular_solve | solution.py:81
  136.2 0.2 fusion.9
  136.5 0.3 fusion.6
  136.7 1.1 multiply_reduce_fusion
  137.9 0.6 fusion.15
  138.5 1.8 %fusion = bf16[256,1024]{1,0:T(8,128)(2,1)} fusion(f32[256,128]{1,0:T(8,128)S(1)} %fusion.6, f32[1024,128]{1,0:T(8,128)S(1)} %broadcast_divide_fusion), kind=kOutput, calls=%fused_computation.3 | convolution fusion | flops 403177472 | bytes 1179648 | tf_op jit(solution)/shard_map/dot_general | solution.py:96
  140.3 0.7 constant_dynamic-slice_fusion
  140.9 8.2 %subtract_bitcast_fusion = f32[1,2048,1024]{2,1,0:T(8,128)} fusion(f32[2048,1024]{1,0:T(8,128)} %copy-done.1, f32[2048,128]{1,0:T(8,128)S(1)} %constant_dynamic-update-slice_fusion, f32[1024,128]{1,0:T(8,128)S(1)} %fusion.15), kind=kOutput, calls=%fused_computation.1 | convolution fusion | flops 1614807040 | bytes 18350080 | tf_op jit(solution)/shard_map/dot_general | solution.py:84
  (28 shorter events, 1.3 us)
Async XLA Ops:
  0.6 17.5 %copy-start = (f32[1024,128]{1,0:T(8,128)S(1)}, f32[1024,128]{1,0:T(8,128)}, u32[]{:S(2)}) copy-start(f32[1024,128]{1,0:T(8,128)} %param.7) | copy-start | bytes 1572868
  14.7 3.4 %copy-start.1 = (f32[2048,1024]{1,0:T(8,128)}, f32[2048,1024]{1,0:T(8,128)S(1)}, u32[]{:S(2)}) copy-start(f32[2048,1024]{1,0:T(8,128)S(1)} %bitcast_add_fusion) | copy-start | bytes 25165828
  21.7 11.2 %collective-permute-start = (f32[512,128]{1,0:T(8,128)S(1)}, f32[512,128]{1,0:T(8,128)S(1)}, u32[]{:S(2)}, u32[]{:S(2)}) collective-permute-start(f32[512,128]{1,0:T(8,128)S(1)} %get-tuple-element.5), channel_id=1, source_target_pairs={{0,12},{4,8},{8,4},{12,0},{16,28},{20,24},{24,20},{28,16},{1,13},{... | collective-permute-start | bytes 786440 | tf_op jit(solution)/shard_map/ppermute | solution.py:14
  25.7 12.1 %collective-permute-start.1 = (f32[512,128]{1,0:T(8,128)S(1)}, f32[512,128]{1,0:T(8,128)S(1)}, u32[]{:S(2)}, u32[]{:S(2)}) collective-permute-start(f32[512,128]{1,0:T(8,128)S(1)} %get-tuple-element.7), channel_id=1, source_target_pairs={{0,8},{4,12},{8,0},{12,4},{16,24},{20,28},{24,16},{28,20},{1,9},{5... | collective-permute-start | bytes 786440 | tf_op jit(solution)/shard_map/ppermute | solution.py:14
  26.1 11.7 %collective-permute-start.2 = (f32[512,128]{1,0:T(8,128)S(1)}, f32[512,128]{1,0:T(8,128)S(1)}, u32[]{:S(2)}, u32[]{:S(2)}) collective-permute-start(f32[512,128]{1,0:T(8,128)S(1)} %get-tuple-element.6), channel_id=1, source_target_pairs={{0,4},{4,0},{8,12},{12,8},{16,20},{20,16},{24,28},{28,24},{1,5},{5... | collective-permute-start | bytes 786440 | tf_op jit(solution)/shard_map/ppermute | solution.py:14
  37.9 14.7 %collective-permute-start.3 = (f32[512,128]{1,0:T(8,128)S(1)}, f32[512,128]{1,0:T(8,128)S(1)}, u32[]{:S(2)}, u32[]{:S(2)}) collective-permute-start(f32[512,128]{1,0:T(8,128)S(1)} %add_add_fusion), channel_id=1, source_target_pairs={{0,16},{4,20},{8,24},{12,28},{16,0},{20,4},{24,8},{28,12},{1,17},{... | collective-permute-start | bytes 786440 | tf_op jit(solution)/shard_map/ppermute | solution.py:14
  52.7 10.2 %collective-permute-start.4 = (f32[512,128]{1,0:T(8,128)S(1)}, f32[512,128]{1,0:T(8,128)S(1)}, u32[]{:S(2)}, u32[]{:S(2)}) collective-permute-start(f32[512,128]{1,0:T(8,128)S(1)} %get-tuple-element.4), channel_id=1, source_target_pairs={{0,12},{4,8},{8,4},{12,0},{16,28},{20,24},{24,20},{28,16},{1,13},{... | collective-permute-start | bytes 786440 | tf_op jit(solution)/shard_map/ppermute | solution.py:14
  54.4 12.4 %collective-permute-start.5 = (f32[512,128]{1,0:T(8,128)S(1)}, f32[512,128]{1,0:T(8,128)S(1)}, u32[]{:S(2)}, u32[]{:S(2)}) collective-permute-start(f32[512,128]{1,0:T(8,128)S(1)} %get-tuple-element.4), channel_id=1, source_target_pairs={{0,8},{4,12},{8,0},{12,4},{16,24},{20,28},{24,16},{28,20},{1,9},{5... | collective-permute-start | bytes 786440 | tf_op jit(solution)/shard_map/ppermute | solution.py:14
  55.8 11.0 %collective-permute-start.6 = (f32[512,128]{1,0:T(8,128)S(1)}, f32[512,128]{1,0:T(8,128)S(1)}, u32[]{:S(2)}, u32[]{:S(2)}) collective-permute-start(f32[512,128]{1,0:T(8,128)S(1)} %get-tuple-element.4), channel_id=1, source_target_pairs={{0,4},{4,0},{8,12},{12,8},{16,20},{20,16},{24,28},{28,24},{1,5},{5... | collective-permute-start | bytes 786440 | tf_op jit(solution)/shard_map/ppermute | solution.py:14
  72.7 1.7 %collective-permute-start.7 = (f32[576,128]{0,1:T(8,128)S(1)}, f32[576,128]{0,1:T(8,128)S(1)}, u32[]{:S(2)}, u32[]{:S(2)}) collective-permute-start(f32[576,128]{0,1:T(8,128)S(1)} %fusion.3), channel_id=1, source_target_pairs={{0,1},{1,0},{2,3},{3,2},{4,5},{5,4},{6,7},{7,6},{8,9},{9,8},{10,11... | collective-permute-start | bytes 884744 | tf_op jit(solution)/shard_map/ppermute | solution.py:14
  74.8 7.0 %collective-permute-start.8 = (f32[288,128]{0,1:T(8,128)S(1)}, f32[288,128]{0,1:T(8,128)S(1)}, u32[]{:S(2)}, u32[]{:S(2)}) collective-permute-start(f32[288,128]{0,1:T(8,128)S(1)} %constant_dynamic-slice_fusion.2), channel_id=1, source_target_pairs={{0,2},{1,3},{2,0},{3,1},{4,6},{5,7},{6,4},{7,5},{8,10},{9,11},{10,... | collective-permute-start | bytes 442376 | tf_op jit(solution)/shard_map/ppermute | solution.py:14
  82.0 5.0 %collective-permute-start.9 = (f32[144,128]{0,1:T(8,128)S(1)}, f32[144,128]{0,1:T(8,128)S(1)}, u32[]{:S(2)}, u32[]{:S(2)}) collective-permute-start(f32[144,128]{0,1:T(8,128)S(1)} %constant_dynamic-slice_fusion.1), channel_id=1, source_target_pairs={{0,4},{4,0},{8,12},{12,8},{16,20},{20,16},{24,28},{28,24},{1,5},{5... | collective-permute-start | bytes 221192 | tf_op jit(solution)/shard_map/ppermute | solution.py:14
  87.2 5.0 %collective-permute-start.10 = (f32[144,128]{0,1:T(8,128)S(1)}, f32[144,128]{0,1:T(8,128)S(1)}, u32[]{:S(2)}, u32[]{:S(2)}) collective-permute-start(f32[144,128]{0,1:T(8,128)S(1)} %dynamic-slice_add_fusion.1), channel_id=1, source_target_pairs={{0,8},{4,12},{8,0},{12,4},{16,24},{20,28},{24,16},{28,20},{1,9},{5... | collective-permute-start | bytes 221192 | tf_op jit(solution)/shard_map/ppermute | solution.py:14
  92.2 7.7 %collective-permute-start.11 = (f32[144,128]{0,1:T(8,128)S(1)}, f32[144,128]{0,1:T(8,128)S(1)}, u32[]{:S(2)}, u32[]{:S(2)}) collective-permute-start(f32[144,128]{0,1:T(8,128)S(1)} %add.109), channel_id=1, source_target_pairs={{0,16},{4,20},{8,24},{12,28},{16,0},{20,4},{24,8},{28,12},{1,17},{... | collective-permute-start | bytes 221192 | tf_op jit(solution)/shard_map/ppermute | solution.py:14
  99.9 5.0 %collective-permute-start.12 = (f32[144,128]{0,1:T(8,128)S(1)}, f32[144,128]{0,1:T(8,128)S(1)}, u32[]{:S(2)}, u32[]{:S(2)}) collective-permute-start(f32[144,128]{0,1:T(8,128)S(1)} %add.110), channel_id=1, source_target_pairs={{0,4},{4,0},{8,12},{12,8},{16,20},{20,16},{24,28},{28,24},{1,5},{5... | collective-permute-start | bytes 221192 | tf_op jit(solution)/shard_map/ppermute | solution.py:14
  105.1 5.7 %collective-permute-start.13 = (f32[288,128]{0,1:T(8,128)S(1)}, f32[288,128]{0,1:T(8,128)S(1)}, u32[]{:S(2)}, u32[]{:S(2)}) collective-permute-start(f32[288,128]{0,1:T(8,128)S(1)} %pad_maximum_fusion.3), channel_id=1, source_target_pairs={{0,2},{1,3},{2,0},{3,1},{4,6},{5,7},{6,4},{7,5},{8,10},{9,11},{10,... | collective-permute-start | bytes 442376 | tf_op jit(solution)/shard_map/ppermute | solution.py:14
  111.1 1.7 %collective-permute-start.14 = (f32[576,128]{0,1:T(8,128)S(1)}, f32[576,128]{0,1:T(8,128)S(1)}, u32[]{:S(2)}, u32[]{:S(2)}) collective-permute-start(f32[576,128]{0,1:T(8,128)S(1)} %pad_maximum_fusion.2), channel_id=1, source_target_pairs={{0,1},{1,0},{2,3},{3,2},{4,5},{5,4},{6,7},{7,6},{8,9},{9,8},{10,11... | collective-permute-start | bytes 884744 | tf_op jit(solution)/shard_map/ppermute | solution.py:14

commit v2 on v0

v2 whole, which is shorter than its diff:
```python
import functools
import math

import jax
import jax.numpy as jnp
from jax import lax
from jax.experimental import pallas as pl
from jax.experimental.pallas import tpu as pltpu
from jax.sharding import PartitionSpec as P

VMEM_LIMIT = 60 * 1024 * 1024
EXACT = lax.Precision.HIGHEST


def split(value):
    high = value.astype(jnp.bfloat16)
    return high, (value - high.astype(jnp.float32)).astype(jnp.bfloat16)


def dot(left, right, left_dim, right_dim, precision=None):
    return lax.dot_general(
        left,
        right,
        (((left_dim,), (right_dim,)), ((), ())),
        precision=precision,
        preferred_element_type=jnp.float32,
    )


def params(**more):
    return pltpu.CompilerParams(vmem_limit_bytes=VMEM_LIMIT, **more)


def swap(value, masks):
    axes = tuple(a for a in ("dp", "rows") if a in masks)
    sizes = [lax.axis_size(a) for a in axes]
    pairs = []
    for index in range(math.prod(sizes)):
        rest, there = index, 0
        coords = []
        for size in sizes[::-1]:
            coords.append(rest % size)
            rest //= size
        for axis, size, coord in zip(axes, sizes, coords[::-1]):
            there = there * size + (coord ^ masks[axis])
        pairs.append((index, there))
    return lax.ppermute(value, axes, pairs)


def bits_of(count):
    return [1 << b for b in range(count.bit_length() - 1)]


def bit_set(axis, mask):
    return jnp.where((lax.axis_index(axis) & mask) != 0, 1, 0).astype(jnp.int32)


def masks_of(chosen):
    masks = {}
    for axis, mask in chosen:
        masks[axis] = masks.get(axis, 0) | mask
    return masks


def scatter_sum(value, directions):
    count = 1 << len(directions)
    block = value.shape[0] // count
    mine = sum(bit_set(a, m) << b for b, (a, m) in enumerate(directions))
    parts = []
    for s in range(count - 1, 0, -1):
        give = lax.dynamic_slice_in_dim(value, (mine ^ s) * block, block, 0)
        parts.append(swap(give, masks_of([d for b, d in enumerate(directions) if s >> b & 1])))
    total = lax.dynamic_slice_in_dim(value, mine * block, block, 0)
    for part in parts:
        total = total + part
    return total


def gather(value, directions):
    count = 1 << len(directions)
    block = value.shape[0]
    mine = sum(bit_set(a, m) << b for b, (a, m) in enumerate(directions))
    parts = [value] + [
        swap(value, masks_of([d for b, d in enumerate(directions) if s >> b & 1])) for s in range(1, count)
    ]
    out = jnp.zeros((count * block,) + value.shape[1:], value.dtype)
    for s, part in enumerate(parts):
        out = lax.dynamic_update_slice_in_dim(out, part, (mine ^ s) * block, 0)
    return out


def blend_kernel(count, chained, who, acts, grads, momentum, basis, *refs):
    refs = refs[1:] if chained else refs
    blended, sketches = refs[0], refs[1:]
    rank = basis.shape[1]
    basis_high, basis_low = split(basis[...])
    both = jnp.concatenate([basis_high, basis_low], 1)
    rows = blended.shape[0]
    part = rows // 2
    outs = []
    for first in range(0, rows, part):
        here = pl.ds(first, part)
        value = momentum[here, :] + dot(acts[:, here], grads[...], 0, 0)
        blended[here, :] = value
        high, low = split(value)
        wide = dot(high, both, 1, 0)
        outs.append(wide[:, :rank] + wide[:, rank:] + dot(low, basis_high, 1, 0))
    result = jnp.concatenate(outs, 0)
    if count == 1:
        sketches[0][...] = result
    else:
        step = pl.program_id(0)
        for index, sketch in enumerate(sketches):

            @pl.when(step == index)
            def _(sketch=sketch):
                sketch[...] = result


def blend(low, acts, grads, momentum, basis, group, first, count, chain=None):
    tokens, rows = acts.shape
    kv, rank = basis.shape
    block = rows // group

    def where(i, who):
        return who[0] ^ (first - i)

    in_specs = [
        pl.BlockSpec((tokens, block), lambda i, who: (0, where(i, who))),
        pl.BlockSpec((tokens, kv), lambda i, who: (0, 0), pipeline_mode=pl.Buffered(1)),
        pl.BlockSpec((block, kv), lambda i, who: (where(i, who), 0)),
        pl.BlockSpec((kv, rank), lambda i, who: (0, 0), pipeline_mode=pl.Buffered(1)),
    ]
    operands = [low, acts, grads, momentum, basis]
    aliases = {}
    if chain is not None:
        in_specs.append(pl.BlockSpec(memory_space=pl.ANY))
        aliases = {len(operands): 0}
        operands.append(chain)
    out = pl.pallas_call(
        functools.partial(blend_kernel, count, chain is not None),
        grid_spec=pltpu.PrefetchScalarGridSpec(
            num_scalar_prefetch=1,
            grid=(count,),
            in_specs=in_specs,
            out_specs=[pl.BlockSpec((block, kv), lambda i, who: (where(i, who), 0))]
            + [pl.BlockSpec((block, rank), lambda i, who: (0, 0))] * count,
        ),
        out_shape=[jax.ShapeDtypeStruct((rows, kv), jnp.float32)]
        + [jax.ShapeDtypeStruct((block, rank), jnp.float32)] * count,
        input_output_aliases=aliases,
        compiler_params=params(),
        cost_estimate=pl.CostEstimate(
            flops=2 * count * block * tokens * kv, bytes_accessed=4 * count * block * kv * 3, transcendentals=0
        ),
        name="blend",
    )(*operands)
    return out[0], out[1:]


def right_product(sketch, blended):
    high, low = split(sketch.T)
    blended_high, blended_low = split(blended)
    rank = high.shape[0]
    wide = dot(jnp.concatenate([high, low], 0), blended_high, 1, 0)
    return wide[:rank] + wide[rank:] + dot(high, blended_low, 1, 0)


def right_first_kernel(share, scale, who, sketch, blended, right):
    value = sketch[...]
    right[:, : blended.shape[1]] = scale * right_product(value, blended[...])
    right[:, blended.shape[1] :] = share * dot(value, value, 0, 0, EXACT)


def right_next_kernel(scale, who, sketch, blended, before, right):
    kv = blended.shape[1]
    right[:, :kv] = before[:, :kv] + scale * right_product(sketch[...], blended[...])
    right[:, kv:] = before[:, kv:]


def right_term(low, sketch, blended, offset, scale, share, before=None):
    block, rank = sketch.shape
    kv = blended.shape[1]
    in_specs = [
        pl.BlockSpec((block, rank), lambda i, who: (0, 0)),
        pl.BlockSpec((block, kv), lambda i, who: (who[0] ^ offset, 0)),
    ]
    operands = [low, sketch, blended]
    whole = pl.BlockSpec((rank, kv + rank), lambda i, who: (0, 0))
    if before is None:
        kernel = functools.partial(right_first_kernel, share, scale)
    else:
        kernel = functools.partial(right_next_kernel, scale)
        in_specs.append(whole)
        operands.append(before)
    return pl.pallas_call(
        kernel,
        grid_spec=pltpu.PrefetchScalarGridSpec(
            num_scalar_prefetch=1, grid=(1,), in_specs=in_specs, out_specs=whole
        ),
        out_shape=jax.ShapeDtypeStruct((rank, kv + rank), jnp.float32),
        compiler_params=params(),
        cost_estimate=pl.CostEstimate(
            flops=6 * block * rank * kv, bytes_accessed=4 * block * kv, transcendentals=0
        ),
        name="right_term",
    )(*operands)


def factor_kernel(gram, inverse, work):
    rank = gram.shape[0]
    rows_id = lax.broadcasted_iota(jnp.int32, (rank, rank), 0)
    cols_id = lax.broadcasted_iota(jnp.int32, (rank, rank), 1)
    work[:, :rank] = gram[...]
    work[:, rank:] = jnp.where(rows_id == cols_id, 1.0, 0.0)
    panel = 16
    for start in range(0, rank, panel):
        here = slice(start, start + panel)
        rows = work[here, :]
        index = lax.broadcasted_iota(jnp.int32, (panel, 1), 0)
        for j in range(0, panel, 2):
            col_a = rows[:, start + j : start + j + 1]
            col_b = rows[:, start + j + 1 : start + j + 2]
            row_a = rows[j : j + 1, :]
            row_b = rows[j + 1 : j + 2, :]
            p_aa = col_a[j : j + 1, :]
            p_ab = col_b[j : j + 1, :]
            p_bb = col_b[j + 1 : j + 2, :]
            inv_a = 1.0 / p_aa
            ratio = p_ab * inv_a
            inv_b = 1.0 / (p_bb - ratio * p_ab)
            row_b = row_b - ratio * row_a
            col_b = col_b - ratio * col_a
            scale_a = jnp.where(index > j, col_a * inv_a, 0.0)
            scale_b = jnp.where(index > j + 1, col_b * inv_b, 0.0)
            rows = rows - scale_a * row_a - scale_b * row_b
        diagonal = jnp.sum(
            jnp.where(
                lax.broadcasted_iota(jnp.int32, (panel, panel), 0)
                == lax.broadcasted_iota(jnp.int32, (panel, panel), 1),
                rows[:, start : start + panel],
                0.0,
            ),
            axis=1,
            keepdims=True,
        )
        rows = rows / jnp.sqrt(diagonal)
        work[here, :] = rows
        if start + panel < rank:
            below = slice(start + panel, rank)
            left = rows[:, :rank]
            update = dot(left, rows, 0, 0, EXACT)
            work[below, :] = work[below, :] - update[start + panel :, :]
    inverse[...] = work[:, rank:]


def factor(gram):
    rank = gram.shape[0]
    return pl.pallas_call(
        factor_kernel,
        out_shape=jax.ShapeDtypeStruct((rank, rank), jnp.float32),
        scratch_shapes=[pltpu.VMEM((rank, 2 * rank), jnp.float32)],
        compiler_params=params(),
        name="factor",
    )(gram)


def finish_kernel(group, scale, who, right, inverse, blended, *refs):
    sketches = refs[:group]
    new_momentum, new_basis, update, total, middle_high, middle_low = refs[group:]
    step = pl.program_id(0)
    block = sketches[0].shape[0]

    @pl.when(step == 0)
    def _():
        for s in range(group):
            total[pl.ds(pl.multiple_of((who[0] ^ s) * block, block), block), :] = sketches[s][...]
        kv = right.shape[1]
        rank = right.shape[0]
        factor_inverse = inverse[...]
        coeff = dot(factor_inverse, right[...], 1, 0, EXACT)
        middle = dot(factor_inverse, coeff, 0, 0, EXACT)
        high, low = split(0.2 * middle)
        middle_high[...] = high
        middle_low[...] = low
        norm = jnp.sqrt(jnp.sum(coeff * coeff, axis=1, keepdims=True) + 1e-06)
        normed = coeff / norm
        count = new_basis.shape[0]
        for j in range(kv // count):

            @pl.when(who[2] == j)
            def _(j=j):
                new_basis[...] = normed[:, j * count : (j + 1) * count].T

        own = update.shape[0]
        own_rows = total[pl.ds(pl.multiple_of(who[1] * own, own), own), :]
        ortho = dot(own_rows, factor_inverse, 1, 1, EXACT)
        update[...] = (scale * dot(ortho, normed, 1, 0, EXACT)).astype(update.dtype)

    here = pl.ds(pl.multiple_of(step * block, block), block)
    high, low = split(total[here, :])
    feedback = dot(jnp.concatenate([high, low], 1), jnp.concatenate([middle_high[...], middle_high[...]], 0), 1, 0)
    feedback = feedback + dot(high, middle_low[...], 1, 0)
    new_momentum[...] = blended[...] - feedback


def finish(who, right, inverse, blended, sketches, n_dp, n_rows, scale):
    rows, kv = blended.shape
    rank = inverse.shape[0]
    group = len(sketches)
    block = rows // group
    const = lambda i, who: (0, 0)
    return pl.pallas_call(
        functools.partial(finish_kernel, group, scale),
        grid_spec=pltpu.PrefetchScalarGridSpec(
            num_scalar_prefetch=1,
            grid=(group,),
            in_specs=[
                pl.BlockSpec((rank, kv), const),
                pl.BlockSpec((rank, rank), const),
                pl.BlockSpec((block, kv), lambda i, who: (i, 0)),
            ]
            + [pl.BlockSpec((block, rank), const)] * group,
            out_specs=[
                pl.BlockSpec((block, kv), lambda i, who: (i, 0)),
                pl.BlockSpec((kv // n_rows, rank), const),
                pl.BlockSpec((rows // n_dp, kv), const),
            ],
            scratch_shapes=[
                pltpu.VMEM((rows, rank), jnp.float32),
                pltpu.VMEM((rank, kv), jnp.bfloat16),
                pltpu.VMEM((rank, kv), jnp.bfloat16),
            ],
        ),
        out_shape=[
            jax.ShapeDtypeStruct((rows, kv), jnp.float32),
            jax.ShapeDtypeStruct((kv // n_rows, rank), jnp.float32),
            jax.ShapeDtypeStruct((rows // n_dp, kv), jnp.bfloat16),
        ],
        compiler_params=params(),
        name="finish",
    )(who, right, inverse, blended, *sketches)


def body(activations, key_grads, momentum, basis):
    n_dp = lax.axis_size("dp")
    n_rows = lax.axis_size("rows")
    dp = lax.axis_index("dp")
    group = min(4, n_dp)
    low = dp & (group - 1)
    who = jnp.stack([low, dp, lax.axis_index("rows")]).astype(jnp.int32)
    kv, rank = basis.shape
    local_rows = activations.shape[1]

    blended, others = blend(who, activations, key_grads, momentum[0], basis, group, group - 1, group - 1)
    arrived = [swap(sketch, {"dp": group - 1 - i}) for i, sketch in enumerate(others)]
    blended, (own,) = blend(who, activations, key_grads, momentum[0], basis, group, 0, 1, blended)
    for part in arrived:
        own = own + part
    for mask in bits_of(n_dp):
        if mask >= group:
            own = own + swap(own, {"dp": mask})
    own = own / n_dp

    sketches = [own] + [swap(own, {"dp": s}) for s in range(1, group)]
    right = right_term(who, own, blended, 0, 1.0 / n_dp, group / n_dp)
    for s in range(group - 1, 0, -1):
        right = right_term(who, sketches[s], blended, s, 1.0 / n_dp, group / n_dp, right)

    core = [("rows", 1)]
    plane = [("rows", m) for m in bits_of(n_rows)[1:]] + [("dp", 1)]
    right = scatter_sum(right, core)
    right = scatter_sum(right, plane)
    for mask in bits_of(n_dp)[1:]:
        right = right + swap(right, {"dp": mask})
    right = gather(right, plane)
    right = gather(right, core)

    inverse = factor(right[:, kv:])
    scale = math.sqrt(local_rows * n_rows * kv / rank)
    new_momentum, new_basis, update = finish(
        who, right[:, :kv], inverse, blended, sketches, n_dp, n_rows, scale
    )
    return (new_momentum[None], new_basis, update)


def solution(mesh):
    in_specs = (P("dp", "rows"), P("dp", None), P("dp", "rows", None), P())
    out_specs = (P("dp", "rows", None), P("rows", None), P(("rows", "dp"), None))
    return jax.shard_map(body, mesh=mesh, in_specs=in_specs, out_specs=out_specs, check_vma=False)
```

time: 323 us -> 133 us (0.41)
  waiting for transfers between devices: 220 us -> 36.5 us
  Pallas kernels: 0 us -> 66.6 us
  matrix products: 57.3 us -> 0 us
  other arithmetic: 26 us -> 2.71 us
  starting transfers between devices: 0.34 us -> 20.8 us
  between operations: 13.8 us -> 0.79 us
    psum x4 -> x0, waiting for transfers between devices: 220 us -> none  [the longest x1 80.6 us: body(): total = lax.psum(sketch, 'dp') / n_dp]
    pallas_call x0 -> x8, Pallas kernels: none -> 66.6 us  [the longest x2 23.2 us: blend(): pl.pallas_call(functools.partial(blend_kernel, count, chain is not None),...]
    dot_general x6 -> x0, matrix products: 55.1 us -> none  [the longest x1 16.4 us: body(): lax.dot_general(blended, ortho, (((0,), (0,)), ((), ())), precision=high,...]
    ppermute x0 -> x17, waiting for transfers between devices: none -> 36.5 us  [swap(): return lax.ppermute(value, axes, pairs)]
    another operation x5 -> x1, other arithmetic: 22.9 us -> 0.64 us  [body(): who = jnp.stack([low, dp, lax.axis_index('rows')]).astype(jnp.int32)]
    ppermute x0 -> x17, starting transfers between devices: none -> 20.8 us  [swap(): return lax.ppermute(value, axes, pairs)]
  transfers between devices with their start and end apart: 4 -> 17, of which waited for: 4 -> 13; matrix products, arithmetic and copies ran while one was open for 0% -> 0% of each run, Pallas kernels for 0% -> 15%
where the time goes in v2:
time: 133 us; the launch traced here: 132 us
  Pallas kernels  66.6 us (50%)
  waiting for transfers between devices  36.5 us (27%)
  starting transfers between devices  20.8 us (16%)
  local copies, waits for them, and re-layouts  4.82 us (4%)
  other arithmetic  2.71 us (2%)
    ppermute x17, waiting for transfers between devices, swap(): return lax.ppermute(value, axes, pairs)  36.5 us
    pallas_call x2, Pallas kernels, blend(): pl.pallas_call(functools.partial(blend_kernel, count, chain is not None),...  23.2 us
    ppermute x17, starting transfers between devices, swap(): return lax.ppermute(value, axes, pairs)  20.8 us
    pallas_call x4, Pallas kernels, right_term(): pl.pallas_call(kernel, grid_spec=pltpu.PrefetchScalarGridSpec(num_scalar_...  15.9 us
    pallas_call x1, Pallas kernels, factor(): pl.pallas_call(factor_kernel, out_shape=jax.ShapeDtypeStruct((rank, rank)...  15.3 us
    pallas_call x1, Pallas kernels, finish(): pl.pallas_call(functools.partial(finish_kernel, group, scale), grid_spec=...  12.2 us
  transfers between devices with their start and end apart: 17, of which 13 were waited for; matrix products, arithmetic and copies ran while one was open for 0% of the time, Pallas kernels for 15%

profile of v2, /device:TPU:0, one launch (start us, length us, event | category | flops | bytes accessed | tf_op | source)
XLA Modules:
  0.0 132.2 jit_solution(3976724902818259031)
XLA Ops:
  0.6 0.6 pad_add_fusion.who
  1.3 14.8 %blend.2 = (f32[2048,1024]{1,0:T(8,128)}, f32[512,128]{1,0:T(8,128)}, f32[512,128]{1,0:T(8,128)}, f32[512,128]{1,0:T(8,128)}) custom-call(s32[3]{0:T(128)} %pad_add_fusion.who, bf16[2048,2048]{1,0:T(8,128)(2,1)} %acts.3, bf16[2048,1024]{1,0:T(8,128)(2,1)} %grads.3, f32[2048,1024]{1,0:T(8,128)} %bitcast.5, f32[1024,128]{1,0:T(8,128)} %basis.3), custom_call_target="tpu_custom_call" | custom-call | flops 6442450944 | bytes 18874368 | tf_op jit(solution)/shard_map/blend/pallas_call | solution.py:140
  16.1 4.1 %collective-permute-start = (f32[512,128]{1,0:T(8,128)}, f32[512,128]{1,0:T(8,128)S(1)}, u32[]{:S(2)}, u32[]{:S(2)}) collective-permute-start(f32[512,128]{1,0:T(8,128)} %get-tuple-element.14), channel_id=1, source_target_pairs={{0,12},{4,8},{8,4},{12,0},{16,28},{20,24},{24,20},{28,16},{1,13},{... | collective-permute-start | bytes 786440 | tf_op jit(solution)/shard_map/ppermute | solution.py:47
  20.1 0.5 collective-permute-start.1
  20.7 0.1 collective-permute-start.2
  20.8 8.4 %blend.3 = (f32[2048,1024]{1,0:T(8,128)}, f32[512,128]{1,0:T(8,128)}) custom-call(s32[3]{0:T(128)} %pad_add_fusion.who, bf16[2048,2048]{1,0:T(8,128)(2,1)} %acts.3, bf16[2048,1024]{1,0:T(8,128)(2,1)} %grads.3, f32[2048,1024]{1,0:T(8,128)} %bitcast.6, f32[1024,128]{1,0:T(8,128)} %basis.3, ...), custom_call_target="tpu_custom_call", output_to_operand_aliasing={{0}: (5, {})} | custom-call | flops 2147483648 | bytes 6291456 | tf_op jit(solution)/shard_map/blend/pallas_call | solution.py:140
  29.1 3.4 %collective-permute-done.1 = f32[512,128]{1,0:T(8,128)S(1)} collective-permute-done((f32[512,128]{1,0:T(8,128)}, f32[512,128]{1,0:T(8,128)S(1)}, u32[]{:S(2)}, u32[]{:S(2)}) %collective-permute-start.1) | collective-permute-done | bytes 262176 | tf_op jit(solution)/shard_map/ppermute | solution.py:47
  32.5 0.0 collective-permute-done.2
  32.5 1.0 add_add_fusion
  33.5 2.7 %collective-permute-start.3 = (f32[512,128]{1,0:T(8,128)S(1)}, f32[512,128]{1,0:T(8,128)S(1)}, u32[]{:S(2)}, u32[]{:S(2)}) collective-permute-start(f32[512,128]{1,0:T(8,128)S(1)} %add_add_fusion), channel_id=1, source_target_pairs={{0,16},{4,20},{8,24},{12,28},{16,0},{20,4},{24,8},{28,12},{1,17},{... | collective-permute-start | bytes 786440 | tf_op jit(solution)/shard_map/ppermute | solution.py:47
  36.2 11.9 %collective-permute-done.3 = f32[512,128]{1,0:T(8,128)S(1)} collective-permute-done((f32[512,128]{1,0:T(8,128)S(1)}, f32[512,128]{1,0:T(8,128)S(1)}, u32[]{:S(2)}, u32[]{:S(2)}) %collective-permute-start.3) | collective-permute-done | bytes 262176 | tf_op jit(solution)/shard_map/ppermute | solution.py:47
  48.1 1.9 %collective-permute-start.6 = (f32[512,128]{1,0:T(8,128)S(1)}, f32[512,128]{1,0:T(8,128)S(1)}, u32[]{:S(2)}, u32[]{:S(2)}) collective-permute-start(f32[512,128]{1,0:T(8,128)S(1)} %add_multiply_fusion.sketch.refs_0_), channel_id=1, source_target_pairs={{0,12},{4,8},{8,4},{12,0},{16,28},{20,24},{24,20},{28,16},{1,13},{... | collective-permute-start | bytes 786440 | tf_op jit(solution)/shard_map/ppermute | solution.py:47
  50.0 1.4 %collective-permute-start.5 = (f32[512,128]{1,0:T(8,128)S(1)}, f32[512,128]{1,0:T(8,128)S(1)}, u32[]{:S(2)}, u32[]{:S(2)}) collective-permute-start(f32[512,128]{1,0:T(8,128)S(1)} %add_multiply_fusion.sketch.refs_0_), channel_id=1, source_target_pairs={{0,8},{4,12},{8,0},{12,4},{16,24},{20,28},{24,16},{28,20},{1,9},{5... | collective-permute-start | bytes 786440 | tf_op jit(solution)/shard_map/ppermute | solution.py:47
  51.3 0.3 collective-permute-start.4
  51.7 4.0 %right_term.4.before = f32[128,1152]{1,0:T(8,128)} custom-call(s32[3]{0:T(128)} %pad_add_fusion.who, f32[512,128]{1,0:T(8,128)} %copy-done, f32[2048,1024]{1,0:T(8,128)} %get-tuple-element.17.blended), custom_call_target="tpu_custom_call" | custom-call | flops 402653184 | bytes 2097152 | tf_op jit(solution)/shard_map/right_term/pallas_call | solution.py:196
  55.7 2.7 %collective-permute-done.6.sketch.refs_3_ = f32[512,128]{1,0:T(8,128)S(1)} collective-permute-done((f32[512,128]{1,0:T(8,128)S(1)}, f32[512,128]{1,0:T(8,128)S(1)}, u32[]{:S(2)}, u32[]{:S(2)}) %collective-permute-start.6) | collective-permute-done | bytes 262176 | tf_op jit(solution)/shard_map/ppermute | solution.py:47
  58.4 0.7 copy-done.1
  59.1 4.0 %right_term.5.before = f32[128,1152]{1,0:T(8,128)} custom-call(s32[3]{0:T(128)} %pad_add_fusion.who, f32[512,128]{1,0:T(8,128)} %copy-done.1, f32[2048,1024]{1,0:T(8,128)} %get-tuple-element.17.blended, f32[128,1152]{1,0:T(8,128)} %right_term.4.before), custom_call_target="tpu_custom_call" | custom-call | flops 402653184 | bytes 2097152 | tf_op jit(solution)/shard_map/right_term/pallas_call | solution.py:196
  63.1 0.7 copy-done.2
  63.8 3.9 %right_term.6.before = f32[128,1152]{1,0:T(8,128)} custom-call(s32[3]{0:T(128)} %pad_add_fusion.who, f32[512,128]{1,0:T(8,128)} %copy-done.2, f32[2048,1024]{1,0:T(8,128)} %get-tuple-element.17.blended, f32[128,1152]{1,0:T(8,128)} %right_term.5.before), custom_call_target="tpu_custom_call" | custom-call | flops 402653184 | bytes 2097152 | tf_op jit(solution)/shard_map/right_term/pallas_call | solution.py:196
  67.7 0.7 copy-done.3
  68.4 4.0 %right_term.7 = f32[128,1152]{1,0:T(8,128)} custom-call(s32[3]{0:T(128)} %pad_add_fusion.who, f32[512,128]{1,0:T(8,128)} %copy-done.3, f32[2048,1024]{1,0:T(8,128)} %get-tuple-element.17.blended, f32[128,1152]{1,0:T(8,128)} %right_term.6.before), custom_call_target="tpu_custom_call" | custom-call | flops 402653184 | bytes 2097152 | tf_op jit(solution)/shard_map/right_term/pallas_call | solution.py:196
  72.3 1.0 constant_dynamic-slice_fusion.3
  73.3 0.1 collective-permute-start.7
  73.4 1.5 %collective-permute-done.7 = f32[64,1152]{1,0:T(8,128)S(1)} collective-permute-done((f32[64,1152]{1,0:T(8,128)S(1)}, f32[64,1152]{1,0:T(8,128)S(1)}, u32[]{:S(2)}, u32[]{:S(2)}) %collective-permute-start.7) | collective-permute-done | bytes 294944 | tf_op jit(solution)/shard_map/ppermute | solution.py:47
  75.0 1.0 dynamic-slice_add_fusion
  76.0 2.7 %collective-permute-start.8 = (f32[16,1152]{1,0:T(8,128)S(1)}, f32[16,1152]{1,0:T(8,128)S(1)}, u32[]{:S(2)}, u32[]{:S(2)}) collective-permute-start(f32[16,1152]{1,0:T(8,128)S(1)} %get-tuple-element.23), channel_id=1, source_target_pairs={{0,6},{1,7},{2,4},{3,5},{4,2},{5,3},{6,0},{7,1},{8,14},{9,15},{10,... | collective-permute-start | bytes 221192 | tf_op jit(solution)/shard_map/ppermute | solution.py:47
  78.7 0.5 collective-permute-start.10
  79.2 0.3 collective-permute-start.9
  79.5 1.8 %collective-permute-done.8 = f32[16,1152]{1,0:T(8,128)S(1)} collective-permute-done((f32[16,1152]{1,0:T(8,128)S(1)}, f32[16,1152]{1,0:T(8,128)S(1)}, u32[]{:S(2)}, u32[]{:S(2)}) %collective-permute-start.8) | collective-permute-done | bytes 73760 | tf_op jit(solution)/shard_map/ppermute | solution.py:47
  81.3 1.7 %collective-permute-done.10 = f32[16,1152]{1,0:T(8,128)S(1)} collective-permute-done((f32[16,1152]{1,0:T(8,128)S(1)}, f32[16,1152]{1,0:T(8,128)S(1)}, u32[]{:S(2)}, u32[]{:S(2)}) %collective-permute-start.10) | collective-permute-done | bytes 73760 | tf_op jit(solution)/shard_map/ppermute | solution.py:47
  83.0 0.5 collective-permute-done.9
  83.6 0.7 collective-permute-start.11
  84.2 3.8 %collective-permute-done.11 = f32[16,1152]{1,0:T(8,128)S(1)} collective-permute-done((f32[16,1152]{1,0:T(8,128)S(1)}, f32[16,1152]{1,0:T(8,128)S(1)}, u32[]{:S(2)}, u32[]{:S(2)}) %collective-permute-start.11) | collective-permute-done | bytes 73760 | tf_op jit(solution)/shard_map/ppermute | solution.py:47
  88.0 2.0 %collective-permute-start.12 = (f32[16,1152]{1,0:T(8,128)S(1)}, f32[16,1152]{1,0:T(8,128)S(1)}, u32[]{:S(2)}, u32[]{:S(2)}) collective-permute-start(f32[16,1152]{1,0:T(8,128)S(1)} %add.73), channel_id=1, source_target_pairs={{0,16},{4,20},{8,24},{12,28},{16,0},{20,4},{24,8},{28,12},{1,17},{... | collective-permute-start | bytes 221192 | tf_op jit(solution)/shard_map/ppermute | solution.py:47
  90.0 4.1 %collective-permute-done.12 = f32[16,1152]{1,0:T(8,128)S(1)} collective-permute-done((f32[16,1152]{1,0:T(8,128)S(1)}, f32[16,1152]{1,0:T(8,128)S(1)}, u32[]{:S(2)}, u32[]{:S(2)}) %collective-permute-start.12) | collective-permute-done | bytes 73760 | tf_op jit(solution)/shard_map/ppermute | solution.py:47
  94.2 1.6 %collective-permute-start.13 = (f32[16,1152]{1,0:T(8,128)S(1)}, f32[16,1152]{1,0:T(8,128)S(1)}, u32[]{:S(2)}, u32[]{:S(2)}) collective-permute-start(f32[16,1152]{1,0:T(8,128)S(1)} %get-tuple-element.22), channel_id=1, source_target_pairs={{0,2},{1,3},{2,0},{3,1},{4,6},{5,7},{6,4},{7,5},{8,10},{9,11},{10,... | collective-permute-start | bytes 221192 | tf_op jit(solution)/shard_map/ppermute | solution.py:47
  95.7 0.4 collective-permute-start.14
  96.1 1.6 %collective-permute-start.15 = (f32[16,1152]{1,0:T(8,128)S(1)}, f32[16,1152]{1,0:T(8,128)S(1)}, u32[]{:S(2)}, u32[]{:S(2)}) collective-permute-start(f32[16,1152]{1,0:T(8,128)S(1)} %get-tuple-element.22), channel_id=1, source_target_pairs={{0,6},{1,7},{2,4},{3,5},{4,2},{5,3},{6,0},{7,1},{8,14},{9,15},{10,... | collective-permute-start | bytes 221192 | tf_op jit(solution)/shard_map/ppermute | solution.py:47
  97.7 0.9 collective-permute-done.13
  98.6 1.5 %collective-permute-done.14 = f32[16,1152]{1,0:T(8,128)S(1)} collective-permute-done((f32[16,1152]{1,0:T(8,128)S(1)}, f32[16,1152]{1,0:T(8,128)S(1)}, u32[]{:S(2)}, u32[]{:S(2)}) %collective-permute-start.14) | collective-permute-done | bytes 73760 | tf_op jit(solution)/shard_map/ppermute | solution.py:47
  100.1 1.3 collective-permute-done.15
  101.4 0.1 collective-permute-start.16
  101.6 1.5 %collective-permute-done.16 = f32[64,1152]{1,0:T(8,128)S(1)} collective-permute-done((f32[64,1152]{1,0:T(8,128)S(1)}, f32[64,1152]{1,0:T(8,128)S(1)}, u32[]{:S(2)}, u32[]{:S(2)}) %collective-permute-start.16) | collective-permute-done | bytes 294944 | tf_op jit(solution)/shard_map/ppermute | solution.py:47
  103.1 0.6 slice.9.gram
  103.7 0.9 slice.8.right
  104.6 15.3 %factor.1.inverse = f32[128,128]{1,0:T(8,128)} custom-call(f32[128,128]{1,0:T(8,128)} %slice.9.gram), custom_call_target="tpu_custom_call" | custom-call | tf_op jit(solution)/shard_map/factor/pallas_call | solution.py:259
  120.0 12.2 %finish.1 = (f32[2048,1024]{1,0:T(8,128)}, f32[256,128]{1,0:T(8,128)}, bf16[256,1024]{1,0:T(8,128)(2,1)}) custom-call(s32[3]{0:T(128)} %pad_add_fusion.who, f32[128,1024]{1,0:T(8,128)} %slice.8.right, f32[128,128]{1,0:T(8,128)} %factor.1.inverse, f32[2048,1024]{1,0:T(8,128)} %get-tuple-element.17.blended, f32[512,128]{1,0:T(8,128)} %copy-done, ...), custom_call_target="tpu_custom_call" | custom-call | tf_op jit(solution)/shard_map/finish/pallas_call | solution.py:313
  (20 shorter events, 0.3 us)
Async XLA Ops:
  16.1 13.1 %collective-permute-start = (f32[512,128]{1,0:T(8,128)}, f32[512,128]{1,0:T(8,128)S(1)}, u32[]{:S(2)}, u32[]{:S(2)}) collective-permute-start(f32[512,128]{1,0:T(8,128)} %get-tuple-element.14), channel_id=1, source_target_pairs={{0,12},{4,8},{8,4},{12,0},{16,28},{20,24},{24,20},{28,16},{1,13},{... | collective-permute-start | bytes 786440 | tf_op jit(solution)/shard_map/ppermute | solution.py:47
  20.1 12.4 %collective-permute-start.1 = (f32[512,128]{1,0:T(8,128)}, f32[512,128]{1,0:T(8,128)S(1)}, u32[]{:S(2)}, u32[]{:S(2)}) collective-permute-start(f32[512,128]{1,0:T(8,128)} %get-tuple-element.15), channel_id=1, source_target_pairs={{0,8},{4,12},{8,0},{12,4},{16,24},{20,28},{24,16},{28,20},{1,9},{5... | collective-permute-start | bytes 786440 | tf_op jit(solution)/shard_map/ppermute | solution.py:47
  20.7 11.9 %collective-permute-start.2 = (f32[512,128]{1,0:T(8,128)}, f32[512,128]{1,0:T(8,128)S(1)}, u32[]{:S(2)}, u32[]{:S(2)}) collective-permute-start(f32[512,128]{1,0:T(8,128)} %get-tuple-element.16), channel_id=1, source_target_pairs={{0,4},{4,0},{8,12},{12,8},{16,20},{20,16},{24,28},{28,24},{1,5},{5... | collective-permute-start | bytes 786440 | tf_op jit(solution)/shard_map/ppermute | solution.py:47
  33.5 14.5 %collective-permute-start.3 = (f32[512,128]{1,0:T(8,128)S(1)}, f32[512,128]{1,0:T(8,128)S(1)}, u32[]{:S(2)}, u32[]{:S(2)}) collective-permute-start(f32[512,128]{1,0:T(8,128)S(1)} %add_add_fusion), channel_id=1, source_target_pairs={{0,16},{4,20},{8,24},{12,28},{16,0},{20,4},{24,8},{28,12},{1,17},{... | collective-permute-start | bytes 786440 | tf_op jit(solution)/shard_map/ppermute | solution.py:47
  48.1 3.6 %copy-start = (f32[512,128]{1,0:T(8,128)}, f32[512,128]{1,0:T(8,128)S(1)}, u32[]{:S(2)}) copy-start(f32[512,128]{1,0:T(8,128)S(1)} %add_multiply_fusion.sketch.refs_0_) | copy-start | bytes 786436
  48.1 10.3 %collective-permute-start.6 = (f32[512,128]{1,0:T(8,128)S(1)}, f32[512,128]{1,0:T(8,128)S(1)}, u32[]{:S(2)}, u32[]{:S(2)}) collective-permute-start(f32[512,128]{1,0:T(8,128)S(1)} %add_multiply_fusion.sketch.refs_0_), channel_id=1, source_target_pairs={{0,12},{4,8},{8,4},{12,0},{16,28},{20,24},{24,20},{28,16},{1,13},{... | collective-permute-start | bytes 786440 | tf_op jit(solution)/shard_map/ppermute | solution.py:47
  50.0 13.1 %collective-permute-start.5 = (f32[512,128]{1,0:T(8,128)S(1)}, f32[512,128]{1,0:T(8,128)S(1)}, u32[]{:S(2)}, u32[]{:S(2)}) collective-permute-start(f32[512,128]{1,0:T(8,128)S(1)} %add_multiply_fusion.sketch.refs_0_), channel_id=1, source_target_pairs={{0,8},{4,12},{8,0},{12,4},{16,24},{20,28},{24,16},{28,20},{1,9},{5... | collective-permute-start | bytes 786440 | tf_op jit(solution)/shard_map/ppermute | solution.py:47
  51.3 16.3 %collective-permute-start.4 = (f32[512,128]{1,0:T(8,128)S(1)}, f32[512,128]{1,0:T(8,128)S(1)}, u32[]{:S(2)}, u32[]{:S(2)}) collective-permute-start(f32[512,128]{1,0:T(8,128)S(1)} %add_multiply_fusion.sketch.refs_0_), channel_id=1, source_target_pairs={{0,4},{4,0},{8,12},{12,8},{16,20},{20,16},{24,28},{28,24},{1,5},{5... | collective-permute-start | bytes 786440 | tf_op jit(solution)/shard_map/ppermute | solution.py:47
  58.4 0.7 copy-start.1
  63.1 0.7 copy-start.2
  67.6 0.7 copy-start.3
  73.3 1.6 %collective-permute-start.7 = (f32[64,1152]{1,0:T(8,128)S(1)}, f32[64,1152]{1,0:T(8,128)S(1)}, u32[]{:S(2)}, u32[]{:S(2)}) collective-permute-start(f32[64,1152]{1,0:T(8,128)S(1)} %constant_dynamic-slice_fusion.3), channel_id=1, source_target_pairs={{0,1},{1,0},{2,3},{3,2},{4,5},{5,4},{6,7},{7,6},{8,9},{9,8},{10,11... | collective-permute-start | bytes 884744 | tf_op jit(solution)/shard_map/ppermute | solution.py:47
  76.0 5.3 %collective-permute-start.8 = (f32[16,1152]{1,0:T(8,128)S(1)}, f32[16,1152]{1,0:T(8,128)S(1)}, u32[]{:S(2)}, u32[]{:S(2)}) collective-permute-start(f32[16,1152]{1,0:T(8,128)S(1)} %get-tuple-element.23), channel_id=1, source_target_pairs={{0,6},{1,7},{2,4},{3,5},{4,2},{5,3},{6,0},{7,1},{8,14},{9,15},{10,... | collective-permute-start | bytes 221192 | tf_op jit(solution)/shard_map/ppermute | solution.py:47
  78.7 4.4 %collective-permute-start.10 = (f32[16,1152]{1,0:T(8,128)S(1)}, f32[16,1152]{1,0:T(8,128)S(1)}, u32[]{:S(2)}, u32[]{:S(2)}) collective-permute-start(f32[16,1152]{1,0:T(8,128)S(1)} %get-tuple-element.24), channel_id=1, source_target_pairs={{0,2},{1,3},{2,0},{3,1},{4,6},{5,7},{6,4},{7,5},{8,10},{9,11},{10,... | collective-permute-start | bytes 221192 | tf_op jit(solution)/shard_map/ppermute | solution.py:47
  79.2 4.4 %collective-permute-start.9 = (f32[16,1152]{1,0:T(8,128)S(1)}, f32[16,1152]{1,0:T(8,128)S(1)}, u32[]{:S(2)}, u32[]{:S(2)}) collective-permute-start(f32[16,1152]{1,0:T(8,128)S(1)} %get-tuple-element.25), channel_id=1, source_target_pairs={{0,4},{4,0},{8,12},{12,8},{16,20},{20,16},{24,28},{28,24},{1,5},{5... | collective-permute-start | bytes 221192 | tf_op jit(solution)/shard_map/ppermute | solution.py:47
  83.6 4.4 %collective-permute-start.11 = (f32[16,1152]{1,0:T(8,128)S(1)}, f32[16,1152]{1,0:T(8,128)S(1)}, u32[]{:S(2)}, u32[]{:S(2)}) collective-permute-start(f32[16,1152]{1,0:T(8,128)S(1)} %add_add_fusion.1), channel_id=1, source_target_pairs={{0,8},{4,12},{8,0},{12,4},{16,24},{20,28},{24,16},{28,20},{1,9},{5... | collective-permute-start | bytes 221192 | tf_op jit(solution)/shard_map/ppermute | solution.py:47
  88.0 6.1 %collective-permute-start.12 = (f32[16,1152]{1,0:T(8,128)S(1)}, f32[16,1152]{1,0:T(8,128)S(1)}, u32[]{:S(2)}, u32[]{:S(2)}) collective-permute-start(f32[16,1152]{1,0:T(8,128)S(1)} %add.73), channel_id=1, source_target_pairs={{0,16},{4,20},{8,24},{12,28},{16,0},{20,4},{24,8},{28,12},{1,17},{... | collective-permute-start | bytes 221192 | tf_op jit(solution)/shard_map/ppermute | solution.py:47
  94.2 4.4 %collective-permute-start.13 = (f32[16,1152]{1,0:T(8,128)S(1)}, f32[16,1152]{1,0:T(8,128)S(1)}, u32[]{:S(2)}, u32[]{:S(2)}) collective-permute-start(f32[16,1152]{1,0:T(8,128)S(1)} %get-tuple-element.22), channel_id=1, source_target_pairs={{0,2},{1,3},{2,0},{3,1},{4,6},{5,7},{6,4},{7,5},{8,10},{9,11},{10,... | collective-permute-start | bytes 221192 | tf_op jit(solution)/shard_map/ppermute | solution.py:47
  95.7 4.4 %collective-permute-start.14 = (f32[16,1152]{1,0:T(8,128)S(1)}, f32[16,1152]{1,0:T(8,128)S(1)}, u32[]{:S(2)}, u32[]{:S(2)}) collective-permute-start(f32[16,1152]{1,0:T(8,128)S(1)} %get-tuple-element.22), channel_id=1, source_target_pairs={{0,4},{4,0},{8,12},{12,8},{16,20},{20,16},{24,28},{28,24},{1,5},{5... | collective-permute-start | bytes 221192 | tf_op jit(solution)/shard_map/ppermute | solution.py:47
  96.1 5.3 %collective-permute-start.15 = (f32[16,1152]{1,0:T(8,128)S(1)}, f32[16,1152]{1,0:T(8,128)S(1)}, u32[]{:S(2)}, u32[]{:S(2)}) collective-permute-start(f32[16,1152]{1,0:T(8,128)S(1)} %get-tuple-element.22), channel_id=1, source_target_pairs={{0,6},{1,7},{2,4},{3,5},{4,2},{5,3},{6,0},{7,1},{8,14},{9,15},{10,... | collective-permute-start | bytes 221192 | tf_op jit(solution)/shard_map/ppermute | solution.py:47
  101.4 1.6 %collective-permute-start.16 = (f32[64,1152]{1,0:T(8,128)S(1)}, f32[64,1152]{1,0:T(8,128)S(1)}, u32[]{:S(2)}, u32[]{:S(2)}) collective-permute-start(f32[64,1152]{1,0:T(8,128)S(1)} %constant_dynamic-update-slice_fusion.2), channel_id=1, source_target_pairs={{0,1},{1,0},{2,3},{3,2},{4,5},{5,4},{6,7},{7,6},{8,9},{9,8},{10,11... | collective-permute-start | bytes 884744 | tf_op jit(solution)/shard_map/ppermute | solution.py:47

commit v3 on v0

v3 whole, which is shorter than its diff:
```python
import functools
import math

import jax
import jax.numpy as jnp
from jax import lax
from jax.experimental import pallas as pl
from jax.experimental.pallas import tpu as pltpu
from jax.sharding import PartitionSpec as P

VMEM_LIMIT = 48 * 1024 * 1024
EXACT = lax.Precision.HIGHEST


def split(value):
    high = value.astype(jnp.bfloat16)
    return high, (value - high.astype(jnp.float32)).astype(jnp.bfloat16)


def dot(left, right, left_dim, right_dim, precision=None):
    return lax.dot_general(
        left,
        right,
        (((left_dim,), (right_dim,)), ((), ())),
        precision=precision,
        preferred_element_type=jnp.float32,
    )


def params(**more):
    return pltpu.CompilerParams(vmem_limit_bytes=VMEM_LIMIT, **more)


def swap(value, masks):
    axes = tuple(a for a in ("dp", "rows") if a in masks)
    sizes = [lax.axis_size(a) for a in axes]
    pairs = []
    for index in range(math.prod(sizes)):
        rest, there = index, 0
        coords = []
        for size in sizes[::-1]:
            coords.append(rest % size)
            rest //= size
        for axis, size, coord in zip(axes, sizes, coords[::-1]):
            there = there * size + (coord ^ masks[axis])
        pairs.append((index, there))
    return lax.ppermute(value, axes, pairs)


def bits_of(count):
    return [1 << b for b in range(count.bit_length() - 1)]


def bit_set(axis, mask):
    return jnp.where((lax.axis_index(axis) & mask) != 0, 1, 0).astype(jnp.int32)


def masks_of(chosen):
    masks = {}
    for axis, mask in chosen:
        masks[axis] = masks.get(axis, 0) | mask
    return masks


def scatter_sum(value, directions):
    count = 1 << len(directions)
    block = value.shape[0] // count
    mine = sum(bit_set(a, m) << b for b, (a, m) in enumerate(directions))
    parts = []
    for s in range(count - 1, 0, -1):
        give = lax.dynamic_slice_in_dim(value, (mine ^ s) * block, block, 0)
        parts.append(swap(give, masks_of([d for b, d in enumerate(directions) if s >> b & 1])))
    total = lax.dynamic_slice_in_dim(value, mine * block, block, 0)
    for part in parts:
        total = total + part
    return total


def gather(value, directions):
    count = 1 << len(directions)
    block = value.shape[0]
    mine = sum(bit_set(a, m) << b for b, (a, m) in enumerate(directions))
    parts = [value] + [
        swap(value, masks_of([d for b, d in enumerate(directions) if s >> b & 1])) for s in range(1, count)
    ]
    out = jnp.zeros((count * block,) + value.shape[1:], value.dtype)
    for s, part in enumerate(parts):
        out = lax.dynamic_update_slice_in_dim(out, part, (mine ^ s) * block, 0)
    return out


VMEM = pl.BlockSpec(memory_space=pltpu.VMEM)
ANY = pl.BlockSpec(memory_space=pl.ANY)
SMEM = pl.BlockSpec(memory_space=pltpu.SMEM)
PARTS = 2


def blend_kernel(first, count, who, acts, grads, momentum, basis, *refs):
    load = count > 1
    blended = refs[0]
    held = refs[1] if load else grads
    sketches = refs[1 + load : 1 + load + PARTS * count]
    acts_held, acts_sem, grads_sem, momentum_sem = refs[1 + load + PARTS * count :]
    tokens, block = acts_held.shape[1:]
    rank = basis.shape[1]
    chunk = tokens // 2
    part = block // PARTS
    starts = [pl.multiple_of((who[0] ^ (first - i)) * block, block) for i in range(count)]

    def acts_copy(i, c):
        here = pl.ds(c * chunk, chunk)
        return pltpu.make_async_copy(
            acts.at[here, pl.ds(starts[i], block)], acts_held.at[i, here], acts_sem.at[i, c]
        )

    def grads_copy(c):
        here = pl.ds(c * chunk, chunk)
        return pltpu.make_async_copy(grads.at[here], held.at[here], grads_sem.at[c])

    def momentum_copy(i):
        return pltpu.make_async_copy(
            momentum.at[pl.ds(starts[i], block)], blended.at[pl.ds(i * block, block)], momentum_sem.at[i]
        )

    for c in range(2):
        acts_copy(0, c).start()
        if load:
            grads_copy(c).start()
    basis_high, basis_low = split(basis[...])
    both = jnp.concatenate([basis_high, basis_low], 1)

    def sketch(index, value):
        high, low = split(value)
        wide = dot(high, both, 1, 0)
        sketches[index][...] = wide[:, :rank] + wide[:, rank:] + dot(low, basis_high, 1, 0)

    pending = None
    for i in range(count):
        columns = [slice(p * part, (p + 1) * part) for p in range(PARTS)]
        if i == 0:
            sums = []
            for c in range(2):
                acts_copy(0, c).wait()
                if load:
                    grads_copy(c).wait()
                if c == 0:
                    momentum_copy(0).start()
                elif count > 1:
                    for d in range(2):
                        acts_copy(1, d).start()
                    momentum_copy(1).start()
                here = slice(c * chunk, (c + 1) * chunk)
                terms = [dot(acts_held[0, here, cols], held[here, :], 0, 0) for cols in columns]
                sums = terms if c == 0 else [a + b for a, b in zip(sums, terms)]
        else:
            for c in range(2):
                acts_copy(i, c).wait()
            if i + 1 < count:
                for d in range(2):
                    acts_copy(i + 1, d).start()
                momentum_copy(i + 1).start()
        momentum_copy(i).wait()
        for p, cols in enumerate(columns):
            rows = slice(i * block + p * part, i * block + (p + 1) * part)
            gradient = sums[p] if i == 0 else dot(acts_held[i, :, cols], held[...], 0, 0)
            value = blended[rows, :] + gradient
            blended[rows, :] = value
            if pending is not None:
                sketch(*pending)
            pending = (i * PARTS + p, value)
    sketch(*pending)


def blend(who, acts, grads, momentum, basis, group, first, count):
    tokens, rows = acts.shape
    kv, rank = basis.shape
    block = rows // group
    load = count > 1
    outs = [pltpu.VMEM((count * block, kv), jnp.float32)]
    if load:
        outs.append(pltpu.VMEM((tokens, kv), jnp.bfloat16))
    outs += [jax.ShapeDtypeStruct((block // PARTS, rank), jnp.float32)] * (PARTS * count)
    out = pl.pallas_call(
        functools.partial(blend_kernel, first, count),
        in_specs=[SMEM, ANY, ANY if load else VMEM, ANY, VMEM],
        out_specs=[VMEM] * len(outs),
        out_shape=outs,
        scratch_shapes=[
            pltpu.VMEM((count, tokens, block), jnp.bfloat16),
            pltpu.SemaphoreType.DMA((count, 2)),
            pltpu.SemaphoreType.DMA((2,)),
            pltpu.SemaphoreType.DMA((count,)),
        ],
        compiler_params=params(),
        cost_estimate=pl.CostEstimate(
            flops=2 * count * block * tokens * kv, bytes_accessed=4 * count * block * kv * 3, transcendentals=0
        ),
        name="blend",
    )(who, acts, grads, momentum, basis)
    return out[0], out[1 : 1 + load], out[1 + load :]


def right_product(sketch, blended):
    turned = sketch.T
    rank = turned.shape[0]
    high, low = split(turned)
    stacked = jnp.concatenate([high, low], 0)
    blended_high, blended_low = split(blended)
    wide = dot(stacked, blended_high, 1, 0)
    gram = dot(stacked, stacked, 1, 1)
    gram = gram[:rank, :rank] + gram[rank:, rank:] + (gram[:rank, rank:] + gram[rank:, :rank])
    return wide[:rank] + wide[rank:] + dot(high, blended_low, 1, 0), gram


def right_kernel(pieces, last, scale, *refs):
    who, blended = refs[:2]
    refs = refs[2:]
    sketches, refs = refs[: len(pieces)], refs[len(pieces) :]
    right, gram = None, None
    for (start, rows), sketch in zip(pieces, sketches):
        right_term, gram_term = right_product(sketch[...], blended[start : start + rows, :])
        right = right_term if right is None else right + right_term
        gram = gram_term if gram is None else gram + gram_term
    right = scale * right
    if not last:
        refs[0][...] = right
        refs[1][...] = gram
        return
    befores, refs = refs[:-4], refs[-4:]
    keep, give, gram_out, total = refs
    for before in befores[::2]:
        right = right + before[...]
    for before in befores[1::2]:
        gram = gram + before[...]
    gram_out[...] = gram
    total[...] = right
    half = keep.shape[0]
    core = who[2] & 1
    keep[...] = total[pl.ds(pl.multiple_of(core * half, half), half), :]
    give[...] = total[pl.ds(pl.multiple_of((1 - core) * half, half), half), :]


def right_terms(who, blended, pieces, sketches, scale, befores=None):
    rank = sketches[0].shape[1]
    kv = blended.shape[1]
    last = befores is not None
    gram = jax.ShapeDtypeStruct((rank, rank), jnp.float32)
    if last:
        outs = [jax.ShapeDtypeStruct((rank // 2, kv), jnp.float32)] * 2 + [gram]
    else:
        outs = [pltpu.VMEM((rank, kv), jnp.float32), pltpu.VMEM((rank, rank), jnp.float32)]
    operands = [who, blended, *sketches, *(befores or [])]
    return pl.pallas_call(
        functools.partial(right_kernel, pieces, last, scale),
        in_specs=[SMEM] + [VMEM] * (len(operands) - 1),
        out_specs=[VMEM] * len(outs),
        out_shape=outs,
        scratch_shapes=[pltpu.VMEM((rank, kv), jnp.float32)] if last else [],
        compiler_params=params(),
        cost_estimate=pl.CostEstimate(
            flops=6 * sum(r for _, r in pieces) * rank * kv,
            bytes_accessed=4 * rank * kv,
            transcendentals=0,
        ),
        name="right_terms",
    )(*operands)


PANEL = 16


def factor_kernel(panels, fresh, *refs):
    rank = refs[0].shape[0]
    if fresh:
        gram_a, gram_b, out = refs
        rows_id = lax.broadcasted_iota(jnp.int32, (rank, rank), 0)
        cols_id = lax.broadcasted_iota(jnp.int32, (rank, rank), 1)
        out[:, :rank] = gram_a[...] + gram_b[...]
        out[:, rank:] = jnp.where(rows_id == cols_id, 1.0, 0.0)
    else:
        out = refs[1]
        out[...] = refs[0][...]
    index = lax.broadcasted_iota(jnp.int32, (PANEL, rank), 0)
    for start in panels:
        here = slice(start, start + PANEL)
        left = out[here, :rank]
        right = out[here, rank:]
        columns = [
            jnp.broadcast_to(left[:, start + c : start + c + 1], (PANEL, rank)) for c in range(PANEL)
        ]
        pivots = jnp.ones((PANEL, rank), jnp.float32)
        for j in range(PANEL):
            pivot = columns[j][j : j + 1, :]
            pivots = jnp.where(index == j, pivot, pivots)
            factor = jnp.where(index > j, columns[j] * (1.0 / pivot), 0.0)
            for c in range(j + 1, PANEL):
                columns[c] = columns[c] - factor * columns[c][j : j + 1, :]
            left = left - factor * left[j : j + 1, :]
            right = right - factor * right[j : j + 1, :]
        weight = 1.0 / jnp.sqrt(pivots)
        left = left * weight
        right = right * weight
        out[here, :rank] = left
        out[here, rank:] = right
        if start + PANEL < rank:
            rows = jnp.concatenate([left, right], 1)
            high, rest = split(rows)
            middle = rest
            low = (rows - high.astype(jnp.float32) - middle.astype(jnp.float32)).astype(jnp.bfloat16)
            one = jnp.concatenate([high, high, middle, middle, high, low], 0)[:, :rank]
            two = jnp.concatenate([high, middle, high, middle, low, high], 0)
            update = dot(one, two, 0, 0)
            below = slice(start + PANEL, rank)
            out[below, :] = out[below, :] - update[start + PANEL :, :]


def factor(panels, *inputs):
    rank = inputs[0].shape[0]
    return pl.pallas_call(
        functools.partial(factor_kernel, panels, len(inputs) == 2),
        in_specs=[VMEM] * len(inputs),
        out_specs=VMEM,
        out_shape=pltpu.VMEM((rank, 2 * rank), jnp.float32),
        compiler_params=params(),
        cost_estimate=pl.CostEstimate(flops=2 * 10**9, bytes_accessed=10**6, transcendentals=0),
        name="factor",
    )(*inputs)


def ortho_kernel(group, who, state, *refs):
    sketches, refs = refs[: PARTS * group], refs[PARTS * group :]
    ortho, own_ortho, total = refs
    rank = state.shape[0]
    part = sketches[0].shape[0]
    inverse = state[:, rank:]
    for s in range(group):
        for p in range(PARTS):
            value = sketches[s * PARTS + p][...]
            high, low = split(value)
            first, second = split(inverse)
            wide = dot(high, jnp.concatenate([first, second], 0), 1, 1)
            value = wide[:, :rank] + wide[:, rank:] + dot(low, first, 1, 1)
            rows = slice((s * PARTS + p) * part, (s * PARTS + p + 1) * part)
            ortho[rows, :] = jnp.concatenate(split(value), 1)
            start = ((who[0] ^ s) * PARTS + p) * part
            total[pl.ds(pl.multiple_of(start, part), part), :] = value
    own = own_ortho.shape[0]
    own_ortho[...] = total[pl.ds(pl.multiple_of(who[1] * own, own), own), :]


def orthonormal(who, state, sketches, group, n_dp):
    rank = state.shape[0]
    rows = sketches[0].shape[0] * len(sketches)
    return pl.pallas_call(
        functools.partial(ortho_kernel, group),
        in_specs=[SMEM] + [VMEM] * (1 + len(sketches)),
        out_specs=[VMEM] * 2,
        out_shape=[
            pltpu.VMEM((rows, 2 * rank), jnp.bfloat16),
            pltpu.VMEM((rows // n_dp, rank), jnp.float32),
        ],
        scratch_shapes=[pltpu.VMEM((rows, rank), jnp.float32)],
        compiler_params=params(),
        cost_estimate=pl.CostEstimate(flops=10**9, bytes_accessed=10**6, transcendentals=0),
        name="ortho",
    )(who, state, *sketches)


def finish_kernel(group, scale, who, right, state, ortho, own_ortho, own_blended, other_blended, *refs):
    new_momentum, new_basis, update, coeff, coeff_high, coeff_low = refs
    step = pl.program_id(0)
    block = own_blended.shape[0]
    rank, kv = right.shape

    @pl.when(step == 0)
    def _():
        value = dot(state[:, rank:], right[...], 1, 0, EXACT)
        coeff[...] = value
        high, low = split(0.2 * value)
        coeff_high[:rank, :] = high
        coeff_high[rank:, :] = high
        coeff_low[...] = low

    def feedback(s):
        rows = ortho[s * block : (s + 1) * block, :]
        return dot(rows, coeff_high[...], 1, 0) + dot(rows[:, :rank], coeff_low[...], 1, 0)

    for s in range(group):

        @pl.when(step == s)
        def _(s=s):
            if s == 0:
                before = own_blended[...]
            else:
                at = (group - 1 - s) * block
                before = other_blended[at : at + block, :]
            new_momentum[...] = before - feedback(s)

    @pl.when(step == group - 1)
    def _():
        value = coeff[...]
        norm = jnp.sqrt(jnp.sum(value * value, axis=1, keepdims=True) + 1e-06)
        normed = value / norm
        count = new_basis.shape[0]
        for j in range(kv // count):

            @pl.when(who[2] == j)
            def _(j=j):
                new_basis[...] = normed[:, j * count : (j + 1) * count].T

        rows_high, rows_low = split(own_ortho[...])
        high, low = split(normed)
        product = dot(jnp.concatenate([rows_high, rows_low], 1), jnp.concatenate([high, high], 0), 1, 0)
        update[...] = (scale * (product + dot(rows_high, low, 1, 0))).astype(update.dtype)


def finish(who, right, state, ortho, own_ortho, own_blended, other_blended, group, n_rows, scale):
    rank, kv = right.shape
    block = own_blended.shape[0]
    rows = block * group
    const = lambda i, who: (0, 0)
    return pl.pallas_call(
        functools.partial(finish_kernel, group, scale),
        grid_spec=pltpu.PrefetchScalarGridSpec(
            num_scalar_prefetch=1,
            grid=(group,),
            in_specs=[VMEM] * 6,
            out_specs=[
                pl.BlockSpec((block, kv), lambda i, who: (who[0] ^ i, 0)),
                pl.BlockSpec((kv // n_rows, rank), const),
                pl.BlockSpec(own_ortho.shape[:1] + (kv,), const),
            ],
            scratch_shapes=[
                pltpu.VMEM((rank, kv), jnp.float32),
                pltpu.VMEM((2 * rank, kv), jnp.bfloat16),
                pltpu.VMEM((rank, kv), jnp.bfloat16),
            ],
        ),
        out_shape=[
            jax.ShapeDtypeStruct((rows, kv), jnp.float32),
            jax.ShapeDtypeStruct((kv // n_rows, rank), jnp.float32),
            jax.ShapeDtypeStruct(own_ortho.shape[:1] + (kv,), jnp.bfloat16),
        ],
        compiler_params=params(),
        name="finish",
    )(who, right, state, ortho, own_ortho, own_blended, other_blended)


def body(activations, key_grads, momentum, basis):
    n_dp = lax.axis_size("dp")
    n_rows = lax.axis_size("rows")
    dp = lax.axis_index("dp")
    group = min(4, n_dp)
    low = dp & (group - 1)
    who = jnp.stack([low, dp, lax.axis_index("rows")]).astype(jnp.int32)
    kv, rank = basis.shape
    local_rows = activations.shape[1]
    block = local_rows // group
    part = block // PARTS
    far = [mask for mask in bits_of(n_dp) if mask >= group]

    other_blended, held, others = blend(who, activations, key_grads, momentum[0], basis, group, group - 1, group - 1)
    arrived = []
    for p in range(PARTS):
        arrived.append([swap(others[i * PARTS + p], {"dp": group - 1 - i}) for i in range(group - 1)])
    own_blended, _, own = blend(who, activations, held[0], momentum[0], basis, group, 0, 1)
    own = list(own)
    sketches = [[None] * PARTS for _ in range(group)]
    for p in range(PARTS):
        for piece in arrived[p]:
            own[p] = own[p] + piece
        for mask in far:
            own[p] = own[p] + swap(own[p], {"dp": mask})
        own[p] = own[p] * (1.0 / n_dp)
        sketches[0][p] = own[p]
        for s in range(group - 1, 0, -1):
            sketches[s][p] = swap(own[p], {"dp": s})

    scale = 1.0 / n_dp
    befores = list(right_terms(who, own_blended, [(p * part, part) for p in range(PARTS)], own, scale))
    for p in range(PARTS):
        pieces = [((group - 1 - s) * block + p * part, part) for s in range(1, group)]
        given = [sketches[s][p] for s in range(1, group)]
        if p + 1 < PARTS:
            befores += right_terms(who, other_blended, pieces, given, scale)
        else:
            keep, give, gram = right_terms(who, other_blended, pieces, given, scale, befores)

    right = keep + swap(give, {"rows": 1})
    gram = gram + swap(gram, {"rows": 1})
    plane = [("rows", m) for m in bits_of(n_rows)[1:]] + [("dp", 1)]
    row_masks = bits_of(n_rows)[1:]
    for mask in row_masks[:-1]:
        gram = gram + swap(gram, {"rows": mask})
    gram_other = swap(gram, {"rows": row_masks[-1]})
    right = scatter_sum(right, plane)
    panels = list(range(0, rank, PANEL))
    middle = len(panels) // 2
    right, gram, gram_other = lax.optimization_barrier((right, gram, gram_other))
    state = None
    for step, mask in enumerate(bits_of(n_dp)[1:]):
        other = swap(right, {"dp": mask})
        if step == 0:
            state = factor(panels[:middle], gram, gram_other)
        elif step == 1:
            state = factor(panels[middle:], state)
        right, state = lax.optimization_barrier((right + other, state))
    flat = [sketches[s][p] for s in range(group) for p in range(PARTS)]
    right = gather(right, plane)
    ortho, own_ortho = orthonormal(who, state, flat, group, n_dp)
    right = gather(right, [("rows", 1)])

    new_momentum, new_basis, update = finish(
        who, right, state, ortho, own_ortho, own_blended, other_blended, group, n_rows,
        math.sqrt(local_rows * n_rows * kv / rank),
    )
    return (new_momentum[None], new_basis, update)


def solution(mesh):
    in_specs = (P("dp", "rows"), P("dp", None), P("dp", "rows", None), P())
    out_specs = (P("dp", "rows", None), P("rows", None), P(("rows", "dp"), None))
    return jax.shard_map(body, mesh=mesh, in_specs=in_specs, out_specs=out_specs, check_vma=False)
```

time: 323 us -> 109 us (0.34)
  waiting for transfers between devices: 220 us -> 20.3 us
  matrix products: 57.3 us -> 0 us
  Pallas kernels: 0 us -> 44.7 us
  starting transfers between devices: 0.34 us -> 33.2 us
  other arithmetic: 26 us -> 2.63 us
  between operations: 13.8 us -> 0.9 us
    psum x4 -> x0, waiting for transfers between devices: 220 us -> none  [the longest x1 80.6 us: body(): total = lax.psum(sketch, 'dp') / n_dp]
    dot_general x6 -> x0, matrix products: 55.1 us -> none  [the longest x1 16.4 us: body(): lax.dot_general(blended, ortho, (((0,), (0,)), ((), ())), precision=high,...]
    pallas_call x0 -> x9, Pallas kernels: none -> 44.7 us  [the longest x2 21.1 us: blend(): pl.pallas_call(functools.partial(blend_kernel, first, count), in_specs=[S...]
    ppermute x0 -> x26, starting transfers between devices: none -> 33.2 us  [swap(): return lax.ppermute(value, axes, pairs)]
    another operation x5 -> x1, other arithmetic: 22.9 us -> 0.66 us  [body(): who = jnp.stack([low, dp, lax.axis_index('rows')]).astype(jnp.int32)]
    ppermute x0 -> x26, waiting for transfers between devices: none -> 20.3 us  [swap(): return lax.ppermute(value, axes, pairs)]
  transfers between devices with their start and end apart: 4 -> 26, of which waited for: 4 -> 12; matrix products, arithmetic and copies ran while one was open for 0% -> 3% of each run, Pallas kernels for 0% -> 16%
where the time goes in v3:
time: 109 us
  Pallas kernels  44.7 us (41%)
  starting transfers between devices  33.2 us (30%)
  waiting for transfers between devices  20.3 us (19%)
  local copies, waits for them, and re-layouts  7.11 us (7%)
  other arithmetic  2.63 us (2%)
    ppermute x26, starting transfers between devices, swap(): return lax.ppermute(value, axes, pairs)  33.2 us
    pallas_call x2, Pallas kernels, blend(): pl.pallas_call(functools.partial(blend_kernel, first, count), in_specs=[S...  21.1 us
    ppermute x26, waiting for transfers between devices, swap(): return lax.ppermute(value, axes, pairs)  20.3 us
    pallas_call x3, Pallas kernels, right_terms(): pl.pallas_call(functools.partial(right_kernel, pieces, last, scale), in_s...  9.74 us
    pallas_call x1, Pallas kernels, finish(): pl.pallas_call(functools.partial(finish_kernel, group, scale), grid_spec=...  9.23 us
    unnamed x12, local copies, waits for them, and re-layouts  5.35 us
    pallas_call x2, Pallas kernels, factor(): pl.pallas_call(functools.partial(factor_kernel, panels, len(inputs) == 2)...  3.53 us
  transfers between devices with their start and end apart: 26, of which 12 were waited for; matrix products, arithmetic and copies ran while one was open for 3% of the time, Pallas kernels for 16%

profile of v3, /device:TPU:0, one launch (start us, length us, event | category | flops | bytes accessed | tf_op | source)
XLA Modules:
  0.0 108.9 jit_solution(15359172757573280884)
XLA Ops:
  0.6 0.7 pad_add_fusion.who.refs_0_
  1.3 14.1 %blend.2 = (f32[1536,1024]{1,0:T(8,128)S(1)}, bf16[2048,1024]{1,0:T(8,128)(2,1)S(1)}, f32[256,128]{1,0:T(8,128)}, f32[256,128]{1,0:T(8,128)}, f32[256,128]{1,0:T...) custom-call(s32[3]{0:T(128)} %pad_add_fusion.who.refs_0_, bf16[2048,2048]{1,0:T(8,128)(2,1)} %acts.3, ...), custom_call_target="tpu_custom_call" | custom-call | flops 6442450944 | bytes 18874368 | tf_op jit(solution)/shard_map/blend/pallas_call | solution.py:183
  15.4 2.6 %copy-done = f32[1536,1024]{1,0:T(8,128)} copy-done((f32[1536,1024]{1,0:T(8,128)}, f32[1536,1024]{1,0:T(8,128)S(1)}, u32[]{:S(2)}) %copy-start) | copy-done | bytes 6291480
  18.0 2.0 %copy-done.1 = bf16[2048,1024]{1,0:T(8,128)(2,1)} copy-done((bf16[2048,1024]{1,0:T(8,128)(2,1)}, bf16[2048,1024]{1,0:T(8,128)(2,1)S(1)}, u32[]{:S(2)}) %copy-start.1) | copy-done | bytes 4194328
  20.0 4.0 %collective-permute-start = (f32[256,128]{1,0:T(8,128)}, f32[256,128]{1,0:T(8,128)S(1)}, u32[]{:S(2)}, u32[]{:S(2)}) collective-permute-start(f32[256,128]{1,0:T(8,128)} %get-tuple-element.36), channel_id=1, source_target_pairs={{0,12},{4,8},{8,4},{12,0},{16,28},{20,24},{24,20},{28,16},{1,13},{... | collective-permute-start | bytes 393224 | tf_op jit(solution)/shard_map/ppermute | solution.py:47
  24.0 0.5 collective-permute-start.1
  24.4 1.5 %collective-permute-start.7 = (f32[256,128]{1,0:T(8,128)}, f32[256,128]{1,0:T(8,128)S(1)}, u32[]{:S(2)}, u32[]{:S(2)}) collective-permute-start(f32[256,128]{1,0:T(8,128)} %get-tuple-element.41), channel_id=1, source_target_pairs={{0,12},{4,8},{8,4},{12,0},{16,28},{20,24},{24,20},{28,16},{1,13},{... | collective-permute-start | bytes 393224 | tf_op jit(solution)/shard_map/ppermute | solution.py:47
  26.0 1.9 %collective-permute-start.9 = (f32[256,128]{1,0:T(8,128)}, f32[256,128]{1,0:T(8,128)S(1)}, u32[]{:S(2)}, u32[]{:S(2)}) collective-permute-start(f32[256,128]{1,0:T(8,128)} %get-tuple-element.43), channel_id=1, source_target_pairs={{0,4},{4,0},{8,12},{12,8},{16,20},{20,16},{24,28},{28,24},{1,5},{5... | collective-permute-start | bytes 393224 | tf_op jit(solution)/shard_map/ppermute | solution.py:47
  27.9 7.0 %blend.3 = (f32[512,1024]{1,0:T(8,128)S(1)}, f32[256,128]{1,0:T(8,128)S(1)}, f32[256,128]{1,0:T(8,128)S(1)}) custom-call(s32[3]{0:T(128)S(1)} %copy-done.3, bf16[2048,2048]{1,0:T(8,128)(2,1)} %acts.3, bf16[2048,1024]{1,0:T(8,128)(2,1)} %copy-done.1, f32[2048,1024]{1,0:T(8,128)} %bitcast.6, f32[1024,128]{1,0:T(8,128)S(1)} %copy-done.2), custom_call_target="tpu_custom_call" | custom-call | flops 2147483648 | bytes 6291456 | tf_op jit(solution)/shard_map/blend/pallas_call | solution.py:183
  35.0 1.1 %collective-permute-start.2 = (f32[256,128]{1,0:T(8,128)S(1)}, f32[256,128]{1,0:T(8,128)S(1)}, u32[]{:S(2)}, u32[]{:S(2)}) collective-permute-start(f32[256,128]{1,0:T(8,128)S(1)} %copy-done.5), channel_id=1, source_target_pairs={{0,4},{4,0},{8,12},{12,8},{16,20},{20,16},{24,28},{28,24},{1,5},{5... | collective-permute-start | bytes 393224 | tf_op jit(solution)/shard_map/ppermute | solution.py:47
  36.3 2.6 %collective-permute-start.10 = (f32[256,128]{1,0:T(8,128)S(1)}, f32[256,128]{1,0:T(8,128)S(1)}, u32[]{:S(2)}, u32[]{:S(2)}) collective-permute-start(f32[256,128]{1,0:T(8,128)S(1)} %add_add_fusion), channel_id=1, source_target_pairs={{0,16},{4,20},{8,24},{12,28},{16,0},{20,4},{24,8},{28,12},{1,17},{... | collective-permute-start | bytes 393224 | tf_op jit(solution)/shard_map/ppermute | solution.py:47
  39.0 1.0 collective-permute-done.2
  40.0 2.6 %collective-permute-start.3 = (f32[256,128]{1,0:T(8,128)S(1)}, f32[256,128]{1,0:T(8,128)S(1)}, u32[]{:S(2)}, u32[]{:S(2)}) collective-permute-start(f32[256,128]{1,0:T(8,128)S(1)} %add_add_fusion.1), channel_id=1, source_target_pairs={{0,16},{4,20},{8,24},{12,28},{16,0},{20,4},{24,8},{28,12},{1,17},{... | collective-permute-start | bytes 393224 | tf_op jit(solution)/shard_map/ppermute | solution.py:47
  42.7 5.8 %collective-permute-done.10 = f32[256,128]{1,0:T(8,128)S(1)} collective-permute-done((f32[256,128]{1,0:T(8,128)S(1)}, f32[256,128]{1,0:T(8,128)S(1)}, u32[]{:S(2)}, u32[]{:S(2)}) %collective-permute-start.10) | collective-permute-done | bytes 131104 | tf_op jit(solution)/shard_map/ppermute | solution.py:47
  48.5 0.3 collective-permute-start.13
  48.8 1.8 %collective-permute-start.12 = (f32[256,128]{1,0:T(8,128)S(1)}, f32[256,128]{1,0:T(8,128)S(1)}, u32[]{:S(2)}, u32[]{:S(2)}) collective-permute-start(f32[256,128]{1,0:T(8,128)S(1)} %add_multiply_fusion.refs_2_.refs_0_), channel_id=1, source_target_pairs={{0,8},{4,12},{8,0},{12,4},{16,24},{20,28},{24,16},{28,20},{1,9},{5... | collective-permute-start | bytes 393224 | tf_op jit(solution)/shard_map/ppermute | solution.py:47
  50.6 1.4 %collective-permute-start.11 = (f32[256,128]{1,0:T(8,128)S(1)}, f32[256,128]{1,0:T(8,128)S(1)}, u32[]{:S(2)}, u32[]{:S(2)}) collective-permute-start(f32[256,128]{1,0:T(8,128)S(1)} %add_multiply_fusion.refs_2_.refs_0_), channel_id=1, source_target_pairs={{0,4},{4,0},{8,12},{12,8},{16,20},{20,16},{24,28},{28,24},{1,5},{5... | collective-permute-start | bytes 393224 | tf_op jit(solution)/shard_map/ppermute | solution.py:47
  52.4 1.9 %collective-permute-start.5 = (f32[256,128]{1,0:T(8,128)S(1)}, f32[256,128]{1,0:T(8,128)S(1)}, u32[]{:S(2)}, u32[]{:S(2)}) collective-permute-start(f32[256,128]{1,0:T(8,128)S(1)} %add_multiply_fusion.1.refs_3_.refs_1_), channel_id=1, source_target_pairs={{0,8},{4,12},{8,0},{12,4},{16,24},{20,28},{24,16},{28,20},{1,9},{5... | collective-permute-start | bytes 393224 | tf_op jit(solution)/shard_map/ppermute | solution.py:47
  54.2 1.5 %collective-permute-done.13.refs_4_.refs_6_ = f32[256,128]{1,0:T(8,128)S(1)} collective-permute-done((f32[256,128]{1,0:T(8,128)S(1)}, f32[256,128]{1,0:T(8,128)S(1)}, u32[]{:S(2)}, u32[]{:S(2)}) %collective-permute-start.13) | collective-permute-done | bytes 131104 | tf_op jit(solution)/shard_map/ppermute | solution.py:47
  55.7 0.9 collective-permute-start.4
  56.6 1.5 %right_terms.3 = (f32[128,1024]{1,0:T(8,128)S(1)}, f32[128,128]{1,0:T(8,128)S(1)}) custom-call(s32[3]{0:T(128)S(1)} %copy-done.3, f32[512,1024]{1,0:T(8,128)S(1)} %get-tuple-element.39.refs_1_.own_blended, f32[256,128]{1,0:T(8,128)S(1)} %add_multiply_fusion.refs_2_.refs_0_, f32[256,128]{1,0:T(8,128)S(1)} %add_multiply_fusion.1.refs_3_.refs_1_), custom_call_target="tpu_custom_call" | custom-call | flops 402653184 | bytes 524288 | tf_op jit(solution)/shard_map/right_terms/pallas_call | solution.py:253
  58.2 3.7 %right_terms.4 = (f32[128,1024]{1,0:T(8,128)S(1)}, f32[128,128]{1,0:T(8,128)S(1)}) custom-call(s32[3]{0:T(128)S(1)} %copy-done.3, f32[1536,1024]{1,0:T(8,128)} %copy-done, f32[256,128]{1,0:T(8,128)S(1)} %collective-permute-done.11.refs_2_, f32[256,128]{1,0:T(8,128)S(1)} %collective-permute-done.12.refs_3_.refs_4_, ...), custom_call_target="tpu_custom_call" | custom-call | flops 603979776 | bytes 524288 | tf_op jit(solution)/shard_map/right_terms/pallas_call | solution.py:253
  62.0 4.5 %right_terms.5 = (f32[64,1024]{1,0:T(8,128)S(1)}, f32[64,1024]{1,0:T(8,128)}, f32[128,128]{1,0:T(8,128)S(1)}) custom-call(s32[3]{0:T(128)S(1)} %copy-done.3, f32[1536,1024]{1,0:T(8,128)} %copy-done, f32[256,128]{1,0:T(8,128)S(1)} %collective-permute-done.4.refs_2_.refs_3_, f32[256,128]{1,0:T(8,128)S(1)} %collective-permute-done.5.refs_3_.refs_5_, ...), custom_call_target="tpu_custom_call" | custom-call | flops 603979776 | bytes 524288 | tf_op jit(solution)/shard_map/right_terms/pallas_call | solution.py:253
  66.5 0.5 collective-permute-start.18
  67.1 1.5 %collective-permute-done.14 = f32[64,1024]{1,0:T(8,128)} collective-permute-done((f32[64,1024]{1,0:T(8,128)}, f32[64,1024]{1,0:T(8,128)}, u32[]{:S(2)}, u32[]{:S(2)}) %collective-permute-start.14) | collective-permute-done | bytes 262176 | tf_op jit(solution)/shard_map/ppermute | solution.py:47
  68.5 1.0 add.79
  69.5 0.7 copy-done.4
  70.2 0.7 constant_dynamic-slice_fusion.2
  70.9 3.4 %collective-permute-start.15 = (f32[16,1024]{1,0:T(8,128)}, f32[16,1024]{1,0:T(8,128)S(1)}, u32[]{:S(2)}, u32[]{:S(2)}) collective-permute-start(f32[16,1024]{1,0:T(8,128)} %get-tuple-element.63), channel_id=1, source_target_pairs={{0,6},{1,7},{2,4},{3,5},{4,2},{5,3},{6,0},{7,1},{8,14},{9,15},{10,... | collective-permute-start | bytes 196616 | tf_op jit(solution)/shard_map/ppermute | solution.py:47
  74.3 0.5 collective-permute-start.17
  74.9 1.5 %collective-permute-start.19 = (f32[128,128]{1,0:T(8,128)S(1)}, f32[128,128]{1,0:T(8,128)S(1)}, u32[]{:S(2)}, u32[]{:S(2)}) collective-permute-start(f32[128,128]{1,0:T(8,128)S(1)} %add.88.refs_0_), channel_id=1, source_target_pairs={{0,2},{1,3},{2,0},{3,1},{4,6},{5,7},{6,4},{7,5},{8,10},{9,11},{10,... | collective-permute-start | bytes 196616 | tf_op jit(solution)/shard_map/ppermute | solution.py:47
  76.4 0.6 collective-permute-done.15
  77.0 2.1 %collective-permute-done.17 = f32[16,1024]{1,0:T(8,128)S(1)} collective-permute-done((f32[16,1024]{1,0:T(8,128)}, f32[16,1024]{1,0:T(8,128)S(1)}, u32[]{:S(2)}, u32[]{:S(2)}) %collective-permute-start.17) | collective-permute-done | bytes 65568 | tf_op jit(solution)/shard_map/ppermute | solution.py:47
  79.1 0.9 add_add_fusion.2
  80.0 0.4 collective-permute-start.20
  80.3 1.9 %factor.2.refs_0_ = f32[128,256]{1,0:T(8,128)S(1)} custom-call(f32[128,128]{1,0:T(8,128)S(1)} %add.88.refs_0_, f32[128,128]{1,0:T(8,128)S(1)} %collective-permute-done.19.refs_1_), custom_call_target="tpu_custom_call" | custom-call | flops 2000000000 | bytes 1000000 | tf_op jit(solution)/shard_map/factor/pallas_call | solution.py:319
  82.2 2.1 %collective-permute-done.20 = f32[16,1024]{1,0:T(8,128)S(1)} collective-permute-done((f32[16,1024]{1,0:T(8,128)S(1)}, f32[16,1024]{1,0:T(8,128)S(1)}, u32[]{:S(2)}, u32[]{:S(2)}) %collective-permute-start.20) | collective-permute-done | bytes 65568 | tf_op jit(solution)/shard_map/ppermute | solution.py:47
  84.3 2.3 %collective-permute-start.21 = (f32[16,1024]{1,0:T(8,128)S(1)}, f32[16,1024]{1,0:T(8,128)S(1)}, u32[]{:S(2)}, u32[]{:S(2)}) collective-permute-start(f32[16,1024]{1,0:T(8,128)S(1)} %add.89), channel_id=1, source_target_pairs={{0,16},{4,20},{8,24},{12,28},{16,0},{20,4},{24,8},{28,12},{1,17},{... | collective-permute-start | bytes 196616 | tf_op jit(solution)/shard_map/ppermute | solution.py:47
  86.6 1.7 %factor.3.state = f32[128,256]{1,0:T(8,128)S(1)} custom-call(f32[128,256]{1,0:T(8,128)S(1)} %factor.2.refs_0_), custom_call_target="tpu_custom_call" | custom-call | flops 2000000000 | bytes 1000000 | tf_op jit(solution)/shard_map/factor/pallas_call | solution.py:319
  88.3 1.3 %collective-permute-done.21 = f32[16,1024]{1,0:T(8,128)S(1)} collective-permute-done((f32[16,1024]{1,0:T(8,128)S(1)}, f32[16,1024]{1,0:T(8,128)S(1)}, u32[]{:S(2)}, u32[]{:S(2)}) %collective-permute-start.21) | collective-permute-done | bytes 65568 | tf_op jit(solution)/shard_map/ppermute | solution.py:47
  89.6 2.2 %collective-permute-start.24 = (f32[16,1024]{1,0:T(8,128)S(1)}, f32[16,1024]{1,0:T(8,128)S(1)}, u32[]{:S(2)}, u32[]{:S(2)}) collective-permute-start(f32[16,1024]{1,0:T(8,128)S(1)} %add.90), channel_id=1, source_target_pairs={{0,6},{1,7},{2,4},{3,5},{4,2},{5,3},{6,0},{7,1},{8,14},{9,15},{10,... | collective-permute-start | bytes 196616 | tf_op jit(solution)/shard_map/ppermute | solution.py:47
  91.7 0.9 collective-permute-start.23
  92.6 0.5 collective-permute-start.22
  93.1 3.7 %collective-permute-done.22 = f32[16,1024]{1,0:T(8,128)S(1)} collective-permute-done((f32[16,1024]{1,0:T(8,128)S(1)}, f32[16,1024]{1,0:T(8,128)S(1)}, u32[]{:S(2)}, u32[]{:S(2)}) %collective-permute-start.22) | collective-permute-done | bytes 65568 | tf_op jit(solution)/shard_map/ppermute | solution.py:47
  97.0 1.1 %ortho.1 = (bf16[2048,256]{1,0:T(8,128)(2,1)S(1)}, f32[256,128]{1,0:T(8,128)S(1)}) custom-call(s32[3]{0:T(128)S(1)} %copy-done.3, f32[128,256]{1,0:T(8,128)S(1)} %factor.3.state, f32[256,128]{1,0:T(8,128)S(1)} %add_multiply_fusion.refs_2_.refs_0_, f32[256,128]{1,0:T(8,128)S(1)} %add_multiply_fusion.1.refs_3_.refs_1_, ...), custom_call_target="tpu_custom_call" | custom-call | flops 1000000000 | bytes 1000000 | tf_op jit(solution)/shard_map/ortho/pallas_call | solution.py:354
  98.2 0.4 collective-permute-done.25
  98.7 1.0 constant_dynamic-update-slice_fusion.right
  99.6 9.2 %finish.1 = (f32[2048,1024]{1,0:T(8,128)}, f32[256,128]{1,0:T(8,128)}, bf16[256,1024]{1,0:T(8,128)(2,1)}) custom-call(s32[3]{0:T(128)S(1)} %copy-done.3, f32[128,1024]{1,0:T(8,128)S(1)} %constant_dynamic-update-slice_fusion.right, f32[128,256]{1,0:T(8,128)S(1)} %factor.3.state, bf16[2048,256]{1,0:T(8,128)(2,1)S(1)} %get-tuple-element.58.ortho, ...), custom_call_target="tpu_custom_call" | custom-call | tf_op jit(solution)/shard_map/finish/pallas_call | solution.py:422
  (44 shorter events, 1.2 us)
Async XLA Ops:
  1.3 26.6 %copy-start.2 = (f32[1024,128]{1,0:T(8,128)S(1)}, f32[1024,128]{1,0:T(8,128)}, u32[]{:S(2)}) copy-start(f32[1024,128]{1,0:T(8,128)} %basis.3) | copy-start | bytes 1572868
  1.3 26.6 %copy-start.3 = (s32[3]{0:T(128)S(1)}, s32[3]{0:T(128)}, u32[]{:S(2)}) copy-start(s32[3]{0:T(128)} %pad_add_fusion.who.refs_0_) | copy-start | bytes 40
  15.4 2.6 %copy-start = (f32[1536,1024]{1,0:T(8,128)}, f32[1536,1024]{1,0:T(8,128)S(1)}, u32[]{:S(2)}) copy-start(f32[1536,1024]{1,0:T(8,128)S(1)} %get-tuple-element.33.refs_1_.other_blended) | copy-start | bytes 18874372
  18.0 2.0 %copy-start.1 = (bf16[2048,1024]{1,0:T(8,128)(2,1)}, bf16[2048,1024]{1,0:T(8,128)(2,1)S(1)}, u32[]{:S(2)}) copy-start(bf16[2048,1024]{1,0:T(8,128)(2,1)S(1)} %get-tuple-element.34.grads) | copy-start | bytes 12582916
  20.0 18.9 %collective-permute-start = (f32[256,128]{1,0:T(8,128)}, f32[256,128]{1,0:T(8,128)S(1)}, u32[]{:S(2)}, u32[]{:S(2)}) collective-permute-start(f32[256,128]{1,0:T(8,128)} %get-tuple-element.36), channel_id=1, source_target_pairs={{0,12},{4,8},{8,4},{12,0},{16,28},{20,24},{24,20},{28,16},{1,13},{... | collective-permute-start | bytes 393224 | tf_op jit(solution)/shard_map/ppermute | solution.py:47
  24.0 15.0 %collective-permute-start.1 = (f32[256,128]{1,0:T(8,128)}, f32[256,128]{1,0:T(8,128)S(1)}, u32[]{:S(2)}, u32[]{:S(2)}) collective-permute-start(f32[256,128]{1,0:T(8,128)} %get-tuple-element.37), channel_id=1, source_target_pairs={{0,8},{4,12},{8,0},{12,4},{16,24},{20,28},{24,16},{28,20},{1,9},{5... | collective-permute-start | bytes 393224 | tf_op jit(solution)/shard_map/ppermute | solution.py:47
  24.4 10.5 %collective-permute-start.7 = (f32[256,128]{1,0:T(8,128)}, f32[256,128]{1,0:T(8,128)S(1)}, u32[]{:S(2)}, u32[]{:S(2)}) collective-permute-start(f32[256,128]{1,0:T(8,128)} %get-tuple-element.41), channel_id=1, source_target_pairs={{0,12},{4,8},{8,4},{12,0},{16,28},{20,24},{24,20},{28,16},{1,13},{... | collective-permute-start | bytes 393224 | tf_op jit(solution)/shard_map/ppermute | solution.py:47
  26.0 10.3 %collective-permute-start.8 = (f32[256,128]{1,0:T(8,128)}, f32[256,128]{1,0:T(8,128)S(1)}, u32[]{:S(2)}, u32[]{:S(2)}) collective-permute-start(f32[256,128]{1,0:T(8,128)} %get-tuple-element.42), channel_id=1, source_target_pairs={{0,8},{4,12},{8,0},{12,4},{16,24},{20,28},{24,16},{28,20},{1,9},{5... | collective-permute-start | bytes 393224 | tf_op jit(solution)/shard_map/ppermute | solution.py:47
  26.0 10.3 %collective-permute-start.9 = (f32[256,128]{1,0:T(8,128)}, f32[256,128]{1,0:T(8,128)S(1)}, u32[]{:S(2)}, u32[]{:S(2)}) collective-permute-start(f32[256,128]{1,0:T(8,128)} %get-tuple-element.43), channel_id=1, source_target_pairs={{0,4},{4,0},{8,12},{12,8},{16,20},{20,16},{24,28},{28,24},{1,5},{5... | collective-permute-start | bytes 393224 | tf_op jit(solution)/shard_map/ppermute | solution.py:47
  27.9 7.0 %copy-start.5 = (f32[256,128]{1,0:T(8,128)S(1)}, f32[256,128]{1,0:T(8,128)}, u32[]{:S(2)}) copy-start(f32[256,128]{1,0:T(8,128)} %get-tuple-element.38) | copy-start | bytes 393220
  35.0 5.0 %collective-permute-start.2 = (f32[256,128]{1,0:T(8,128)S(1)}, f32[256,128]{1,0:T(8,128)S(1)}, u32[]{:S(2)}, u32[]{:S(2)}) collective-permute-start(f32[256,128]{1,0:T(8,128)S(1)} %copy-done.5), channel_id=1, source_target_pairs={{0,4},{4,0},{8,12},{12,8},{16,20},{20,16},{24,28},{28,24},{1,5},{5... | collective-permute-start | bytes 393224 | tf_op jit(solution)/shard_map/ppermute | solution.py:47
  36.3 12.1 %collective-permute-start.10 = (f32[256,128]{1,0:T(8,128)S(1)}, f32[256,128]{1,0:T(8,128)S(1)}, u32[]{:S(2)}, u32[]{:S(2)}) collective-permute-start(f32[256,128]{1,0:T(8,128)S(1)} %add_add_fusion), channel_id=1, source_target_pairs={{0,16},{4,20},{8,24},{12,28},{16,0},{20,4},{24,8},{28,12},{1,17},{... | collective-permute-start | bytes 393224 | tf_op jit(solution)/shard_map/ppermute | solution.py:47
  40.0 12.0 %collective-permute-start.3 = (f32[256,128]{1,0:T(8,128)S(1)}, f32[256,128]{1,0:T(8,128)S(1)}, u32[]{:S(2)}, u32[]{:S(2)}) collective-permute-start(f32[256,128]{1,0:T(8,128)S(1)} %add_add_fusion.1), channel_id=1, source_target_pairs={{0,16},{4,20},{8,24},{12,28},{16,0},{20,4},{24,8},{28,12},{1,17},{... | collective-permute-start | bytes 393224 | tf_op jit(solution)/shard_map/ppermute | solution.py:47
  48.5 7.2 %collective-permute-start.13 = (f32[256,128]{1,0:T(8,128)S(1)}, f32[256,128]{1,0:T(8,128)S(1)}, u32[]{:S(2)}, u32[]{:S(2)}) collective-permute-start(f32[256,128]{1,0:T(8,128)S(1)} %add_multiply_fusion.refs_2_.refs_0_), channel_id=1, source_target_pairs={{0,12},{4,8},{8,4},{12,0},{16,28},{20,24},{24,20},{28,16},{1,13},{... | collective-permute-start | bytes 393224 | tf_op jit(solution)/shard_map/ppermute | solution.py:47
  48.8 9.3 %collective-permute-start.12 = (f32[256,128]{1,0:T(8,128)S(1)}, f32[256,128]{1,0:T(8,128)S(1)}, u32[]{:S(2)}, u32[]{:S(2)}) collective-permute-start(f32[256,128]{1,0:T(8,128)S(1)} %add_multiply_fusion.refs_2_.refs_0_), channel_id=1, source_target_pairs={{0,8},{4,12},{8,0},{12,4},{16,24},{20,28},{24,16},{28,20},{1,9},{5... | collective-permute-start | bytes 393224 | tf_op jit(solution)/shard_map/ppermute | solution.py:47
  50.6 7.6 %collective-permute-start.11 = (f32[256,128]{1,0:T(8,128)S(1)}, f32[256,128]{1,0:T(8,128)S(1)}, u32[]{:S(2)}, u32[]{:S(2)}) collective-permute-start(f32[256,128]{1,0:T(8,128)S(1)} %add_multiply_fusion.refs_2_.refs_0_), channel_id=1, source_target_pairs={{0,4},{4,0},{8,12},{12,8},{16,20},{20,16},{24,28},{28,24},{1,5},{5... | collective-permute-start | bytes 393224 | tf_op jit(solution)/shard_map/ppermute | solution.py:47
  52.0 9.9 %collective-permute-start.6 = (f32[256,128]{1,0:T(8,128)S(1)}, f32[256,128]{1,0:T(8,128)S(1)}, u32[]{:S(2)}, u32[]{:S(2)}) collective-permute-start(f32[256,128]{1,0:T(8,128)S(1)} %add_multiply_fusion.1.refs_3_.refs_1_), channel_id=1, source_target_pairs={{0,12},{4,8},{8,4},{12,0},{16,28},{20,24},{24,20},{28,16},{1,13},{... | collective-permute-start | bytes 393224 | tf_op jit(solution)/shard_map/ppermute | solution.py:47
  52.4 9.6 %collective-permute-start.5 = (f32[256,128]{1,0:T(8,128)S(1)}, f32[256,128]{1,0:T(8,128)S(1)}, u32[]{:S(2)}, u32[]{:S(2)}) collective-permute-start(f32[256,128]{1,0:T(8,128)S(1)} %add_multiply_fusion.1.refs_3_.refs_1_), channel_id=1, source_target_pairs={{0,8},{4,12},{8,0},{12,4},{16,24},{20,28},{24,16},{28,20},{1,9},{5... | collective-permute-start | bytes 393224 | tf_op jit(solution)/shard_map/ppermute | solution.py:47
  55.7 6.3 %collective-permute-start.4 = (f32[256,128]{1,0:T(8,128)S(1)}, f32[256,128]{1,0:T(8,128)S(1)}, u32[]{:S(2)}, u32[]{:S(2)}) collective-permute-start(f32[256,128]{1,0:T(8,128)S(1)} %add_multiply_fusion.1.refs_3_.refs_1_), channel_id=1, source_target_pairs={{0,4},{4,0},{8,12},{12,8},{16,20},{20,16},{24,28},{28,24},{1,5},{5... | collective-permute-start | bytes 393224 | tf_op jit(solution)/shard_map/ppermute | solution.py:47
  66.5 2.0 %collective-permute-start.14 = (f32[64,1024]{1,0:T(8,128)}, f32[64,1024]{1,0:T(8,128)}, u32[]{:S(2)}, u32[]{:S(2)}) collective-permute-start(f32[64,1024]{1,0:T(8,128)} %get-tuple-element.49), channel_id=1, source_target_pairs={{0,1},{1,0},{2,3},{3,2},{4,5},{5,4},{6,7},{7,6},{8,9},{9,8},{10,11... | collective-permute-start | bytes 786440 | tf_op jit(solution)/shard_map/ppermute | solution.py:47
  66.5 8.3 %collective-permute-start.18 = (f32[128,128]{1,0:T(8,128)S(1)}, f32[128,128]{1,0:T(8,128)S(1)}, u32[]{:S(2)}, u32[]{:S(2)}) collective-permute-start(f32[128,128]{1,0:T(8,128)S(1)} %get-tuple-element.50), channel_id=1, source_target_pairs={{0,1},{1,0},{2,3},{3,2},{4,5},{5,4},{6,7},{7,6},{8,9},{9,8},{10,11... | collective-permute-start | bytes 196616 | tf_op jit(solution)/shard_map/ppermute | solution.py:47
  69.5 0.7 copy-start.4
  70.9 6.1 %collective-permute-start.15 = (f32[16,1024]{1,0:T(8,128)}, f32[16,1024]{1,0:T(8,128)S(1)}, u32[]{:S(2)}, u32[]{:S(2)}) collective-permute-start(f32[16,1024]{1,0:T(8,128)} %get-tuple-element.63), channel_id=1, source_target_pairs={{0,6},{1,7},{2,4},{3,5},{4,2},{5,3},{6,0},{7,1},{8,14},{9,15},{10,... | collective-permute-start | bytes 196616 | tf_op jit(solution)/shard_map/ppermute | solution.py:47
  74.3 4.8 %collective-permute-start.17 = (f32[16,1024]{1,0:T(8,128)}, f32[16,1024]{1,0:T(8,128)S(1)}, u32[]{:S(2)}, u32[]{:S(2)}) collective-permute-start(f32[16,1024]{1,0:T(8,128)} %get-tuple-element.64), channel_id=1, source_target_pairs={{0,2},{1,3},{2,0},{3,1},{4,6},{5,7},{6,4},{7,5},{8,10},{9,11},{10,... | collective-permute-start | bytes 196616 | tf_op jit(solution)/shard_map/ppermute | solution.py:47
  74.8 4.3 %collective-permute-start.16 = (f32[16,1024]{1,0:T(8,128)S(1)}, f32[16,1024]{1,0:T(8,128)S(1)}, u32[]{:S(2)}, u32[]{:S(2)}) collective-permute-start(f32[16,1024]{1,0:T(8,128)S(1)} %get-tuple-element.65), channel_id=1, source_target_pairs={{0,4},{4,0},{8,12},{12,8},{16,20},{20,16},{24,28},{28,24},{1,5},{5... | collective-permute-start | bytes 196616 | tf_op jit(solution)/shard_map/ppermute | solution.py:47
  74.9 5.1 %collective-permute-start.19 = (f32[128,128]{1,0:T(8,128)S(1)}, f32[128,128]{1,0:T(8,128)S(1)}, u32[]{:S(2)}, u32[]{:S(2)}) collective-permute-start(f32[128,128]{1,0:T(8,128)S(1)} %add.88.refs_0_), channel_id=1, source_target_pairs={{0,2},{1,3},{2,0},{3,1},{4,6},{5,7},{6,4},{7,5},{8,10},{9,11},{10,... | collective-permute-start | bytes 196616 | tf_op jit(solution)/shard_map/ppermute | solution.py:47
  80.0 4.3 %collective-permute-start.20 = (f32[16,1024]{1,0:T(8,128)S(1)}, f32[16,1024]{1,0:T(8,128)S(1)}, u32[]{:S(2)}, u32[]{:S(2)}) collective-permute-start(f32[16,1024]{1,0:T(8,128)S(1)} %add_add_fusion.2), channel_id=1, source_target_pairs={{0,8},{4,12},{8,0},{12,4},{16,24},{20,28},{24,16},{28,20},{1,9},{5... | collective-permute-start | bytes 196616 | tf_op jit(solution)/shard_map/ppermute | solution.py:47
  84.3 5.2 %collective-permute-start.21 = (f32[16,1024]{1,0:T(8,128)S(1)}, f32[16,1024]{1,0:T(8,128)S(1)}, u32[]{:S(2)}, u32[]{:S(2)}) collective-permute-start(f32[16,1024]{1,0:T(8,128)S(1)} %add.89), channel_id=1, source_target_pairs={{0,16},{4,20},{8,24},{12,28},{16,0},{20,4},{24,8},{28,12},{1,17},{... | collective-permute-start | bytes 196616 | tf_op jit(solution)/shard_map/ppermute | solution.py:47
  89.6 7.3 %collective-permute-start.24 = (f32[16,1024]{1,0:T(8,128)S(1)}, f32[16,1024]{1,0:T(8,128)S(1)}, u32[]{:S(2)}, u32[]{:S(2)}) collective-permute-start(f32[16,1024]{1,0:T(8,128)S(1)} %add.90), channel_id=1, source_target_pairs={{0,6},{1,7},{2,4},{3,5},{4,2},{5,3},{6,0},{7,1},{8,14},{9,15},{10,... | collective-permute-start | bytes 196616 | tf_op jit(solution)/shard_map/ppermute | solution.py:47
  91.7 5.1 %collective-permute-start.23 = (f32[16,1024]{1,0:T(8,128)S(1)}, f32[16,1024]{1,0:T(8,128)S(1)}, u32[]{:S(2)}, u32[]{:S(2)}) collective-permute-start(f32[16,1024]{1,0:T(8,128)S(1)} %add.90), channel_id=1, source_target_pairs={{0,4},{4,0},{8,12},{12,8},{16,20},{20,16},{24,28},{28,24},{1,5},{5... | collective-permute-start | bytes 196616 | tf_op jit(solution)/shard_map/ppermute | solution.py:47
  92.6 4.3 %collective-permute-start.22 = (f32[16,1024]{1,0:T(8,128)S(1)}, f32[16,1024]{1,0:T(8,128)S(1)}, u32[]{:S(2)}, u32[]{:S(2)}) collective-permute-start(f32[16,1024]{1,0:T(8,128)S(1)} %add.90), channel_id=1, source_target_pairs={{0,2},{1,3},{2,0},{3,1},{4,6},{5,7},{6,4},{7,5},{8,10},{9,11},{10,... | collective-permute-start | bytes 196616 | tf_op jit(solution)/shard_map/ppermute | solution.py:47
  96.9 1.7 %collective-permute-start.25 = (f32[64,1024]{1,0:T(8,128)S(1)}, f32[64,1024]{1,0:T(8,128)}, u32[]{:S(2)}, u32[]{:S(2)}) collective-permute-start(f32[64,1024]{1,0:T(8,128)S(1)} %constant_dynamic-update-slice_fusion.2), channel_id=1, source_target_pairs={{0,1},{1,0},{2,3},{3,2},{4,5},{5,4},{6,7},{7,6},{8,9},{9,8},{10,11... | collective-permute-start | bytes 786440 | tf_op jit(solution)/shard_map/ppermute | solution.py:47

commit v4 on v3

v4 whole, which is shorter than its diff:
```python
import functools
import math

import jax
import jax.numpy as jnp
from jax import lax
from jax.experimental import pallas as pl
from jax.experimental.pallas import tpu as pltpu
from jax.sharding import PartitionSpec as P

MIB = 1024 * 1024
FIRST_MIB = 44
BLEND_MIB = 40
EXACT = lax.Precision.HIGHEST


def split(value):
    high = value.astype(jnp.bfloat16)
    return high, (value - high.astype(jnp.float32)).astype(jnp.bfloat16)


def dot(left, right, left_dim, right_dim, precision=None):
    return lax.dot_general(
        left,
        right,
        (((left_dim,), (right_dim,)), ((), ())),
        precision=precision,
        preferred_element_type=jnp.float32,
    )


def params(mib):
    return pltpu.CompilerParams(vmem_limit_bytes=mib * MIB)


def swap(value, masks):
    axes = tuple(a for a in ("dp", "rows") if a in masks)
    sizes = [lax.axis_size(a) for a in axes]
    pairs = []
    for index in range(math.prod(sizes)):
        rest, there = index, 0
        coords = []
        for size in sizes[::-1]:
            coords.append(rest % size)
            rest //= size
        for axis, size, coord in zip(axes, sizes, coords[::-1]):
            there = there * size + (coord ^ masks[axis])
        pairs.append((index, there))
    return lax.ppermute(value, axes, pairs)


def bits_of(count):
    return [1 << b for b in range(count.bit_length() - 1)]


def bit_set(axis, mask):
    return jnp.where((lax.axis_index(axis) & mask) != 0, 1, 0).astype(jnp.int32)


def masks_of(chosen):
    masks = {}
    for axis, mask in chosen:
        masks[axis] = masks.get(axis, 0) | mask
    return masks


def gather(value, directions, beside):
    count = 1 << len(directions)
    block = value.shape[0]
    mine = sum(bit_set(a, m) << b for b, (a, m) in enumerate(directions))
    parts = [value] + [
        swap(value, masks_of([d for b, d in enumerate(directions) if s >> b & 1])) for s in range(1, count)
    ]
    *parts, beside = lax.optimization_barrier((*parts, beside))
    out = jnp.zeros((count * block,) + value.shape[1:], value.dtype)
    for s, part in enumerate(parts):
        out = lax.dynamic_update_slice_in_dim(out, part, (mine ^ s) * block, 0)
    return out, beside


VMEM = pl.BlockSpec(memory_space=pltpu.VMEM)
ANY = pl.BlockSpec(memory_space=pl.ANY)
SMEM = pl.BlockSpec(memory_space=pltpu.SMEM)
PARTS = 2


def sketch_of(value, both, rank):
    high, low = split(value)
    wide = dot(high, both, 1, 0)
    return wide[:, :rank] + wide[:, rank:] + dot(low, both[:, :rank], 1, 0)


CHUNKS = 4


def first_blend_kernel(group, offsets, later, acts, grads, momentum, basis, *refs):
    count, extra = len(offsets), len(later)
    blended, held, acts_later = refs[:3]
    momentum_later = refs[3 : 3 + extra]
    sketches = refs[3 + extra : 3 + extra + PARTS * count]
    refs = refs[3 + extra + PARTS * count :]
    acts_held, values, both, acts_sem, grads_sem, momentum_sem, later_sem, out_sem = refs
    low = lax.axis_index("dp") & (group - 1)
    tokens, block = acts_held.shape[1:]
    rank = basis.shape[1]
    chunk = tokens // CHUNKS
    part = block // PARTS

    def start_of(offset):
        return pl.multiple_of((low ^ offset) * block, block)

    def acts_copy(i, c):
        here = pl.ds(c * chunk, chunk)
        return pltpu.make_async_copy(
            acts.at[here, pl.ds(start_of(offsets[i]), block)], acts_held.at[i, here], acts_sem.at[i, c]
        )

    def grads_copy(c):
        here = pl.ds(c * chunk, chunk)
        return pltpu.make_async_copy(grads.at[here], held.at[here], grads_sem.at[c])

    def momentum_copy(i):
        return pltpu.make_async_copy(
            momentum.at[pl.ds(start_of(offsets[i]), block)],
            values.at[pl.ds(i * block, block)],
            momentum_sem.at[i],
        )

    def out_copy(index):
        here = pl.ds(index * part, part)
        return pltpu.make_async_copy(values.at[here], blended.at[here], out_sem.at[index])

    def later_copies(i):
        here = pl.ds(start_of(later[i]), block)
        return [
            pltpu.make_async_copy(acts.at[:, here], acts_later.at[i], later_sem.at[i, 0]),
            pltpu.make_async_copy(momentum.at[here], momentum_later[i], later_sem.at[i, 1]),
        ]

    for c in range(CHUNKS):
        acts_copy(0, c).start()
        grads_copy(c).start()
    basis_high, basis_low = split(basis[...])
    both[:, :rank] = basis_high
    both[:, rank:] = basis_low
    columns = [slice(p * part, (p + 1) * part) for p in range(PARTS)]
    pending = None
    for i in range(count):
        if i == 0:
            sums = None
            for c in range(CHUNKS):
                acts_copy(0, c).wait()
                grads_copy(c).wait()
                if c == CHUNKS // 2:
                    momentum_copy(0).start()
                here = slice(c * chunk, (c + 1) * chunk)
                terms = [dot(acts_held[0, here, cols], held[here, :], 0, 0) for cols in columns]
                sums = terms if c == 0 else [a + b for a, b in zip(sums, terms)]
        else:
            for c in range(CHUNKS):
                acts_copy(i, c).wait()
        if i + 1 < count:
            for c in range(CHUNKS):
                acts_copy(i + 1, c).start()
            momentum_copy(i + 1).start()
        else:
            for n in range(extra):
                for copy in later_copies(n):
                    copy.start()
        momentum_copy(i).wait()
        for p, cols in enumerate(columns):
            rows = slice(i * block + p * part, i * block + (p + 1) * part)
            gradient = sums[p] if i == 0 else dot(acts_held[i, :, cols], held[...], 0, 0)
            value = values[rows, :] + gradient
            values[rows, :] = value
            if pending is not None:
                out_copy(pending[0]).start()
                sketches[pending[0]][...] = sketch_of(pending[1], both[...], rank)
            pending = (i * PARTS + p, value)
    out_copy(pending[0]).start()
    sketches[pending[0]][...] = sketch_of(pending[1], both[...], rank)
    for index in range(count * PARTS):
        out_copy(index).wait()
    for n in range(extra):
        for copy in later_copies(n):
            copy.wait()


def first_blend(acts, grads, momentum, basis, group, offsets, later):
    tokens, rows = acts.shape
    kv, rank = basis.shape
    block = rows // group
    count, extra = len(offsets), len(later)
    outs = [
        jax.ShapeDtypeStruct((rows, kv), jnp.float32),
        pltpu.VMEM((tokens, kv), jnp.bfloat16),
        pltpu.VMEM((extra, tokens, block), jnp.bfloat16),
    ]
    outs += [pltpu.VMEM((block, kv), jnp.float32)] * extra
    outs += [pltpu.VMEM((block // PARTS, rank), jnp.float32)] * (PARTS * count)
    out = pl.pallas_call(
        functools.partial(first_blend_kernel, group, offsets, later),
        in_specs=[ANY, ANY, ANY, VMEM],
        out_specs=[ANY] + [VMEM] * (len(outs) - 1),
        out_shape=outs,
        scratch_shapes=[
            pltpu.VMEM((count, tokens, block), jnp.bfloat16),
            pltpu.VMEM((count * block, kv), jnp.float32),
            pltpu.VMEM((kv, 2 * rank), jnp.bfloat16),
            pltpu.SemaphoreType.DMA((count, CHUNKS)),
            pltpu.SemaphoreType.DMA((CHUNKS,)),
            pltpu.SemaphoreType.DMA((count,)),
            pltpu.SemaphoreType.DMA((extra, 2)),
            pltpu.SemaphoreType.DMA((count * PARTS,)),
        ],
        compiler_params=params(FIRST_MIB),
        name="first_blend",
    )(acts, grads, momentum, basis)
    return out[0], out[1], out[2], out[3 : 3 + extra], out[3 + extra :]


def blend_kernel(index, first, acts, grads, basis, momentum, _, blended, *refs):
    sketches, (values, out_sem) = refs[:PARTS], refs[PARTS:]
    block = acts.shape[2]
    rank = basis.shape[1]
    part = block // PARTS
    both = jnp.concatenate(split(basis[...]), 1)

    def out_copy(p):
        return pltpu.make_async_copy(
            values.at[pl.ds(p * part, part)], blended.at[pl.ds(first + p * part, part)], out_sem.at[p]
        )

    pending = None
    for p in range(PARTS):
        rows = slice(p * part, (p + 1) * part)
        value = momentum[rows, :] + dot(acts[index, :, rows], grads[...], 0, 0)
        values[rows, :] = value
        if pending is not None:
            out_copy(p - 1).start()
            sketches[p - 1][...] = sketch_of(pending, both, rank)
        pending = value
    out_copy(PARTS - 1).start()
    sketches[PARTS - 1][...] = sketch_of(pending, both, rank)
    for p in range(PARTS):
        out_copy(p).wait()


def blend(acts, grads, basis, momentum, blended, index, first):
    block = acts.shape[2]
    kv, rank = basis.shape
    outs = [jax.ShapeDtypeStruct(blended.shape, jnp.float32)]
    outs += [pltpu.VMEM((block // PARTS, rank), jnp.float32)] * PARTS
    out = pl.pallas_call(
        functools.partial(blend_kernel, index, first),
        in_specs=[VMEM] * 4 + [ANY],
        out_specs=[ANY] + [VMEM] * PARTS,
        out_shape=outs,
        scratch_shapes=[pltpu.VMEM((block, kv), jnp.float32), pltpu.SemaphoreType.DMA((PARTS,))],
        input_output_aliases={4: 0},
        compiler_params=params(BLEND_MIB),
        name="blend",
    )(acts, grads, basis, momentum, blended)
    return out[0], out[1:]


def right_product(sketch, blended):
    turned = sketch.T
    rank = turned.shape[0]
    high, low = split(turned)
    stacked = jnp.concatenate([high, low], 0)
    blended_high, blended_low = split(blended)
    wide = dot(stacked, blended_high, 1, 0)
    gram = dot(stacked, stacked, 1, 1)
    gram = gram[:rank, :rank] + gram[rank:, rank:] + (gram[:rank, rank:] + gram[rank:, :rank])
    return wide[:rank] + wide[rank:] + dot(high, blended_low, 1, 0), gram


def right_kernel(pieces, first, last, scale, *refs):
    who, blended = refs[:2]
    refs = refs[2:]
    sketches, refs = refs[: len(pieces)], refs[len(pieces) :]
    if first:
        held, sem = refs[-2:]
        start, rows = pieces[0][0], sum(r for _, r in pieces)
        copies = []
        for at, size in ((start, rows), (0, start), (start + rows, blended.shape[0] - start - rows)):
            if size:
                here = pl.ds(at, size)
                copies.append(pltpu.make_async_copy(blended.at[here], held.at[here], sem.at[len(copies)]))
                copies[-1].start()
        copies[0].wait()
        blended = held
    right, gram = None, None
    for (start, rows), sketch in zip(pieces, sketches):
        right_term, gram_term = right_product(sketch[...], blended[start : start + rows, :])
        right = right_term if right is None else right + right_term
        gram = gram_term if gram is None else gram + gram_term
    right = scale * right
    if not last:
        refs[0][...] = right
        refs[1][...] = gram
        if first:
            for copy in copies[1:]:
                copy.wait()
        return
    befores, refs = refs[:-4], refs[-4:]
    keep, give, gram_out, total = refs
    for before in befores[::2]:
        right = right + before[...]
    for before in befores[1::2]:
        gram = gram + before[...]
    gram_out[...] = gram
    total[...] = right
    half = keep.shape[0]
    core = who[2] & 1
    keep[...] = total[pl.ds(pl.multiple_of(core * half, half), half), :]
    give[...] = total[pl.ds(pl.multiple_of((1 - core) * half, half), half), :]


def right_terms(who, blended, pieces, sketches, scale, befores=None, first=False):
    rank = sketches[0].shape[1]
    kv = blended.shape[1]
    last = befores is not None
    gram = pltpu.VMEM((rank, rank), jnp.float32)
    if last:
        outs = [pltpu.VMEM((rank // 2, kv), jnp.float32)] * 2 + [gram]
    else:
        outs = [pltpu.VMEM((rank, kv), jnp.float32), pltpu.VMEM((rank, rank), jnp.float32)]
    scratch = [pltpu.VMEM((rank, kv), jnp.float32)] if last else []
    if first:
        outs.append(pltpu.VMEM(blended.shape, jnp.float32))
        scratch = [pltpu.SemaphoreType.DMA((3,))]
    operands = [who, blended, *sketches, *(befores or [])]
    return pl.pallas_call(
        functools.partial(right_kernel, pieces, first, last, scale),
        in_specs=[SMEM, ANY if first else VMEM] + [VMEM] * (len(operands) - 2),
        out_specs=[VMEM] * len(outs),
        out_shape=outs,
        scratch_shapes=scratch,
        compiler_params=params(FIRST_MIB if first else 16),
        name="right_terms",
    )(*operands)


def cut_kernel(count, who, keep, arrived, *blocks):
    block = blocks[0].shape[0]
    for s, out in enumerate(blocks):
        here = pl.ds(pl.multiple_of((who[3] ^ s) * block, block), block)
        out[...] = keep[here, :] + arrived[here, :]


def cut(who, keep, arrived, count):
    rows, kv = keep.shape
    return pl.pallas_call(
        functools.partial(cut_kernel, count),
        in_specs=[SMEM, VMEM, VMEM],
        out_specs=[VMEM] * count,
        out_shape=[pltpu.VMEM((rows // count, kv), jnp.float32)] * count,
        compiler_params=params(16),
        name="cut",
    )(who, keep, arrived)


PANEL = 16


def factor_kernel(panels, fresh, *refs):
    rank = refs[0].shape[0]
    if fresh:
        gram_a, gram_b, out = refs
        rows_id = lax.broadcasted_iota(jnp.int32, (rank, rank), 0)
        cols_id = lax.broadcasted_iota(jnp.int32, (rank, rank), 1)
        out[:, :rank] = gram_a[...] + gram_b[...]
        out[:, rank:] = jnp.where(rows_id == cols_id, 1.0, 0.0)
    else:
        out = refs[1]
        out[...] = refs[0][...]
    index = lax.broadcasted_iota(jnp.int32, (PANEL, rank), 0)
    for start in panels:
        here = slice(start, start + PANEL)
        left = out[here, :rank]
        right = out[here, rank:]
        columns = [
            jnp.broadcast_to(left[:, start + c : start + c + 1], (PANEL, rank)) for c in range(PANEL)
        ]
        pivots = jnp.ones((PANEL, rank), jnp.float32)
        for j in range(PANEL):
            pivot = columns[j][j : j + 1, :]
            pivots = jnp.where(index == j, pivot, pivots)
            factor = jnp.where(index > j, columns[j] * (1.0 / pivot), 0.0)
            for c in range(j + 1, PANEL):
                columns[c] = columns[c] - factor * columns[c][j : j + 1, :]
            left = left - factor * left[j : j + 1, :]
            right = right - factor * right[j : j + 1, :]
        weight = 1.0 / jnp.sqrt(pivots)
        left = left * weight
        right = right * weight
        out[here, :rank] = left
        out[here, rank:] = right
        if start + PANEL < rank:
            rows = jnp.concatenate([left, right], 1)
            high, rest = split(rows)
            middle = rest
            low = (rows - high.astype(jnp.float32) - middle.astype(jnp.float32)).astype(jnp.bfloat16)
            one = jnp.concatenate([high, high, middle, middle, high, low], 0)[:, :rank]
            two = jnp.concatenate([high, middle, high, middle, low, high], 0)
            update = dot(one, two, 0, 0)
            below = slice(start + PANEL, rank)
            out[below, :] = out[below, :] - update[start + PANEL :, :]


def factor(panels, *inputs):
    rank = inputs[0].shape[0]
    return pl.pallas_call(
        functools.partial(factor_kernel, panels, len(inputs) == 2),
        in_specs=[VMEM] * len(inputs),
        out_specs=VMEM,
        out_shape=pltpu.VMEM((rank, 2 * rank), jnp.float32),
        compiler_params=params(16),
        name="factor",
    )(*inputs)


def ortho_kernel(group, who, state, *refs):
    sketches, refs = refs[: PARTS * group], refs[PARTS * group :]
    blended, ortho, own_ortho, held, total, sem = refs
    copy = pltpu.make_async_copy(blended, held, sem)
    copy.start()
    rank = state.shape[0]
    part = sketches[0].shape[0]
    inverse = state[:, rank:]
    for s in range(group):
        for p in range(PARTS):
            value = sketches[s * PARTS + p][...]
            high, low = split(value)
            first, second = split(inverse)
            wide = dot(high, jnp.concatenate([first, second], 0), 1, 1)
            value = wide[:, :rank] + wide[:, rank:] + dot(low, first, 1, 1)
            rows = slice((s * PARTS + p) * part, (s * PARTS + p + 1) * part)
            ortho[rows, :] = jnp.concatenate(split(value), 1)
            start = ((who[0] ^ s) * PARTS + p) * part
            total[pl.ds(pl.multiple_of(start, part), part), :] = value
    own = own_ortho.shape[0]
    own_ortho[...] = total[pl.ds(pl.multiple_of(who[1] * own, own), own), :]
    copy.wait()


def orthonormal(who, state, sketches, blended, group, n_dp):
    rank = state.shape[0]
    rows = sketches[0].shape[0] * len(sketches)
    return pl.pallas_call(
        functools.partial(ortho_kernel, group),
        in_specs=[SMEM] + [VMEM] * (1 + len(sketches)) + [ANY],
        out_specs=[VMEM] * 3,
        out_shape=[
            pltpu.VMEM((rows, 2 * rank), jnp.bfloat16),
            pltpu.VMEM((rows // n_dp, rank), jnp.float32),
            pltpu.VMEM(blended.shape, jnp.float32),
        ],
        scratch_shapes=[pltpu.VMEM((rows, rank), jnp.float32), pltpu.SemaphoreType.DMA],
        compiler_params=params(FIRST_MIB),
        name="ortho",
    )(who, state, *sketches, blended)


def finish_kernel(group, places, scale, who, right_here, right_there, state, ortho, own_ortho, *refs):
    blended, new_momentum, new_basis, update, right, coeff, coeff_high, coeff_low = refs
    step = pl.program_id(0)
    block = new_momentum.shape[0]
    rank, kv = right.shape
    half = rank // 2
    core = who[2] & 1

    @pl.when(step == 0)
    def _():
        right[pl.ds(pl.multiple_of(core * half, half), half), :] = right_here[...]
        right[pl.ds(pl.multiple_of((1 - core) * half, half), half), :] = right_there[...]
        value = dot(state[:, rank:], right[...], 1, 0, EXACT)
        coeff[...] = value
        high, low = split(0.2 * value)
        coeff_high[:rank, :] = high
        coeff_high[rank:, :] = high
        coeff_low[...] = low

    def feedback(s):
        rows = ortho[s * block : (s + 1) * block, :]
        return dot(rows, coeff_high[...], 1, 0) + dot(rows[:, :rank], coeff_low[...], 1, 0)

    for s in range(group):

        @pl.when(step == s)
        def _(s=s):
            new_momentum[...] = blended[places[s] : places[s] + block, :] - feedback(s)

    @pl.when(step == group - 1)
    def _():
        value = coeff[...]
        norm = jnp.sqrt(jnp.sum(value * value, axis=1, keepdims=True) + 1e-06)
        normed = value / norm
        count = new_basis.shape[0]
        for j in range(kv // count):

            @pl.when(who[2] == j)
            def _(j=j):
                new_basis[...] = normed[:, j * count : (j + 1) * count].T

        rows_high, rows_low = split(own_ortho[...])
        high, low = split(normed)
        product = dot(jnp.concatenate([rows_high, rows_low], 1), jnp.concatenate([high, high], 0), 1, 0)
        update[...] = (scale * (product + dot(rows_high, low, 1, 0))).astype(update.dtype)


def finish(who, right_here, right_there, state, ortho, own_ortho, blended, places, n_rows, scale):
    rank, kv = 2 * right_here.shape[0], right_here.shape[1]
    group = len(places)
    rows = ortho.shape[0]
    block = rows // group
    const = lambda i, who: (0, 0)
    return pl.pallas_call(
        functools.partial(finish_kernel, group, places, scale),
        grid_spec=pltpu.PrefetchScalarGridSpec(
            num_scalar_prefetch=1,
            grid=(group,),
            in_specs=[VMEM] * 6,
            out_specs=[
                pl.BlockSpec((block, kv), lambda i, who: (who[0] ^ i, 0)),
                pl.BlockSpec((kv // n_rows, rank), const),
                pl.BlockSpec(own_ortho.shape[:1] + (kv,), const),
            ],
            scratch_shapes=[
                pltpu.VMEM((rank, kv), jnp.float32),
                pltpu.VMEM((rank, kv), jnp.float32),
                pltpu.VMEM((2 * rank, kv), jnp.bfloat16),
                pltpu.VMEM((rank, kv), jnp.bfloat16),
            ],
        ),
        out_shape=[
            jax.ShapeDtypeStruct((rows, kv), jnp.float32),
            jax.ShapeDtypeStruct((kv // n_rows, rank), jnp.float32),
            jax.ShapeDtypeStruct(own_ortho.shape[:1] + (kv,), jnp.bfloat16),
        ],
        compiler_params=params(16),
        name="finish",
    )(who, right_here, right_there, state, ortho, own_ortho, blended)


def body(activations, key_grads, momentum, basis):
    n_dp = lax.axis_size("dp")
    n_rows = lax.axis_size("rows")
    dp = lax.axis_index("dp")
    group = min(4, n_dp)
    low = dp & (group - 1)
    kv, rank = basis.shape
    local_rows = activations.shape[1]
    block = local_rows // group
    part = block // PARTS
    far = [mask for mask in bits_of(n_dp) if mask >= group]
    plane = [("rows", m) for m in bits_of(n_rows)[1:]] + [("dp", 1)]
    mine = sum(bit_set(a, m) << b for b, (a, m) in enumerate(plane))
    who = jnp.stack([low, dp, lax.axis_index("rows"), mine]).astype(jnp.int32)

    offsets, later = tuple(range(group - 1, 1, -1)), (1, 0)
    blended, held, acts_later, momentum_later, given = first_blend(
        activations, key_grads, momentum[0], basis, group, offsets, later
    )
    places = [0] * group
    arrived = [[] for _ in range(PARTS)]
    for i, offset in enumerate(offsets):
        places[offset] = i * block
        for p in range(PARTS):
            arrived[p].append(swap(given[i * PARTS + p], {"dp": offset}))
    for n, offset in enumerate(later):
        places[offset] = (len(offsets) + n) * block
        blended, given = blend(acts_later, held, basis, momentum_later[n], blended, n, places[offset])
        if offset == 0:
            own = list(given)
        else:
            for p in range(PARTS):
                arrived[p].append(swap(given[p], {"dp": offset}))
    sketches = [[None] * PARTS for _ in range(group)]
    for p in range(PARTS):
        for piece in arrived[p]:
            own[p] = own[p] + piece
        for mask in far:
            own[p] = own[p] + swap(own[p], {"dp": mask})
        own[p] = own[p] * (1.0 / n_dp)
        sketches[0][p] = own[p]
        for s in range(group - 1, 0, -1):
            sketches[s][p] = swap(own[p], {"dp": s})

    scale = 1.0 / n_dp
    pieces = [(places[0] + p * part, part) for p in range(PARTS)]
    *befores, held = right_terms(who, blended, pieces, own, scale, first=True)
    for p in range(PARTS):
        pieces = [(places[s] + p * part, part) for s in range(1, group)]
        given = [sketches[s][p] for s in range(1, group)]
        if p + 1 < PARTS:
            befores += right_terms(who, held, pieces, given, scale)
        else:
            keep, give, gram = right_terms(who, held, pieces, given, scale, befores)

    blocks = cut(who, keep, swap(give, {"rows": 1}), 1 << len(plane))
    gram = gram + swap(gram, {"rows": 1})
    row_masks = bits_of(n_rows)[1:]
    for mask in row_masks[:-1]:
        gram = gram + swap(gram, {"rows": mask})
    gram_other = swap(gram, {"rows": row_masks[-1]})
    right = blocks[0]
    for s in range(len(blocks) - 1, 0, -1):
        right = right + swap(blocks[s], masks_of([d for b, d in enumerate(plane) if s >> b & 1]))
    panels = list(range(0, rank, PANEL))
    middle = len(panels) // 2
    right, gram, gram_other = lax.optimization_barrier((right, gram, gram_other))
    state = None
    for step, mask in enumerate(bits_of(n_dp)[1:]):
        other = swap(right, {"dp": mask})
        if step == 0:
            state = factor(panels[:middle], gram, gram_other)
        elif step == 1:
            state = factor(panels[middle:], state)
        right, state = lax.optimization_barrier((right + other, state))
    flat = [sketches[s][p] for s in range(group) for p in range(PARTS)]
    ortho, own_ortho, held = orthonormal(who, state, flat, blended, group, n_dp)
    right, ortho = gather(right, plane, ortho)
    other = swap(right, {"rows": 1})

    new_momentum, new_basis, update = finish(
        who, right, other, state, ortho, own_ortho, held, places, n_rows,
        math.sqrt(local_rows * n_rows * kv / rank),
    )
    return (new_momentum[None], new_basis, update)


def solution(mesh):
    in_specs = (P("dp", "rows"), P("dp", None), P("dp", "rows", None), P())
    out_specs = (P("dp", "rows", None), P("rows", None), P(("rows", "dp"), None))
    return jax.shard_map(body, mesh=mesh, in_specs=in_specs, out_specs=out_specs, check_vma=False)
```

time: 109 us -> 93.1 us (0.85)
  waiting for transfers between devices: 20.3 us -> 11.9 us
  local copies, waits for them, and re-layouts: 7.11 us -> 0.09 us
  starting transfers between devices: 33.2 us -> 38 us
  Pallas kernels: 44.7 us -> 41.9 us
  other arithmetic: 2.63 us -> 0.21 us
    ppermute x26, waiting for transfers between devices: 20.3 us -> 11.9 us  [swap(): return lax.ppermute(value, axes, pairs)]
    pallas_call x6 -> x8, Pallas kernels: 40 us -> 33.6 us  [the longest x1 11.9 us: first_blend(): pl.pallas_call(functools.partial(first_blend_kernel, group, offsets, late...]
    unnamed x12 -> x8, local copies, waits for them, and re-layouts: 5.35 us -> 0.02 us
    ppermute x26, starting transfers between devices: 33.2 us -> 38 us  [swap(): return lax.ppermute(value, axes, pairs)]
    pallas_call x1, Pallas kernels: 1.13 us -> 4.71 us  [orthonormal(): pl.pallas_call(functools.partial(ortho_kernel, group), in_specs=[SMEM] +...]
    add x2 -> x1, other arithmetic: 1.86 us -> 0.02 us  [body(): right + swap(blocks[s], masks_of([d for b, d in enumerate(plane) if s >>...]
  transfers between devices with their start and end apart: 26 -> 26, of which waited for: 12 -> 12; matrix products, arithmetic and copies ran while one was open for 3% -> 0% of each run, Pallas kernels for 16% -> 19%
where the time goes in v4:
time: 93.1 us; the launch traced here: 92.9 us
  Pallas kernels  41.9 us (45%)
  starting transfers between devices  38 us (41%)
  waiting for transfers between devices  11.9 us (13%)
    ppermute x26, starting transfers between devices, swap(): return lax.ppermute(value, axes, pairs)  38 us
    ppermute x26, waiting for transfers between devices, swap(): return lax.ppermute(value, axes, pairs)  11.9 us
    pallas_call x1, Pallas kernels, first_blend(): pl.pallas_call(functools.partial(first_blend_kernel, group, offsets, late...  11.9 us
    pallas_call x2, Pallas kernels, blend(): pl.pallas_call(functools.partial(blend_kernel, index, first), in_specs=[V...  7.49 us
    pallas_call x3, Pallas kernels, right_terms(): pl.pallas_call(functools.partial(right_kernel, pieces, first, last, scale...  7.18 us
    pallas_call x1, Pallas kernels, finish(): pl.pallas_call(functools.partial(finish_kernel, group, places, scale), gr...  6.51 us
    pallas_call x1, Pallas kernels, orthonormal(): pl.pallas_call(functools.partial(ortho_kernel, group), in_specs=[SMEM] +...  4.71 us
    pallas_call x2, Pallas kernels, factor(): pl.pallas_call(functools.partial(factor_kernel, panels, len(inputs) == 2)...  3.53 us
  transfers between devices with their start and end apart: 26, of which 12 were waited for; matrix products, arithmetic and copies ran while one was open for 0% of the time, Pallas kernels for 19%

profile of v4, /device:TPU:0, one launch (start us, length us, event | category | flops | bytes accessed | tf_op | source)
XLA Modules:
  0.0 92.9 jit_solution(9395907109945880472)
XLA Ops:
  0.6 11.9 %first_blend.1 = (f32[2048,1024]{1,0:T(8,128)}, bf16[2048,1024]{1,0:T(8,128)(2,1)S(1)}, bf16[2,2048,512]{2,1,0:T(8,128)(2,1)S(1)}, f32[512,1024]{1,0:T(8,128)S(1...) custom-call(bf16[2048,2048]{1,0:T(8,128)(2,1)} %acts.1, ...), custom_call_target="tpu_custom_call" | custom-call | tf_op jit(solution)/shard_map/first_blend/pallas_call | solution.py:201
  12.5 3.7 %blend.2 = (f32[2048,1024]{1,0:T(8,128)}, f32[256,128]{1,0:T(8,128)S(1)}, f32[256,128]{1,0:T(8,128)S(1)}) custom-call(bf16[2,2048,512]{2,1,0:T(8,128)(2,1)S(1)} %get-tuple-element.48.acts, bf16[2048,1024]{1,0:T(8,128)(2,1)S(1)} %get-tuple-element.49.grads, f32[1024,128]{1,0:T(8,128)S(1)} %copy-done, ...), custom_call_target="tpu_custom_call", output_to_operand_aliasing={{0}: (4, {})} | custom-call | tf_op jit(solution)/shard_map/blend/pallas_call | solution.py:254
  16.3 3.0 %collective-permute-start.2 = (f32[256,128]{1,0:T(8,128)S(1)}, f32[256,128]{1,0:T(8,128)S(1)}, u32[]{:S(2)}, u32[]{:S(2)}) collective-permute-start(f32[256,128]{1,0:T(8,128)S(1)} %get-tuple-element.58), channel_id=1, source_target_pairs={{0,4},{4,0},{8,12},{12,8},{16,20},{20,16},{24,28},{28,24},{1,5},{5... | collective-permute-start | bytes 393224 | tf_op jit(solution)/shard_map/ppermute | solution.py:49
  19.3 1.6 %collective-permute-start = (f32[256,128]{1,0:T(8,128)S(1)}, f32[256,128]{1,0:T(8,128)S(1)}, u32[]{:S(2)}, u32[]{:S(2)}) collective-permute-start(f32[256,128]{1,0:T(8,128)S(1)} %get-tuple-element.56), channel_id=1, source_target_pairs={{0,12},{4,8},{8,4},{12,0},{16,28},{20,24},{24,20},{28,16},{1,13},{... | collective-permute-start | bytes 393224 | tf_op jit(solution)/shard_map/ppermute | solution.py:49
  20.9 1.9 %collective-permute-start.6 = (f32[256,128]{1,0:T(8,128)S(1)}, f32[256,128]{1,0:T(8,128)S(1)}, u32[]{:S(2)}, u32[]{:S(2)}) collective-permute-start(f32[256,128]{1,0:T(8,128)S(1)} %get-tuple-element.62), channel_id=1, source_target_pairs={{0,4},{4,0},{8,12},{12,8},{16,20},{20,16},{24,28},{28,24},{1,5},{5... | collective-permute-start | bytes 393224 | tf_op jit(solution)/shard_map/ppermute | solution.py:49
  22.8 1.6 %collective-permute-start.4 = (f32[256,128]{1,0:T(8,128)S(1)}, f32[256,128]{1,0:T(8,128)S(1)}, u32[]{:S(2)}, u32[]{:S(2)}) collective-permute-start(f32[256,128]{1,0:T(8,128)S(1)} %get-tuple-element.60), channel_id=1, source_target_pairs={{0,12},{4,8},{8,4},{12,0},{16,28},{20,24},{24,20},{28,16},{1,13},{... | collective-permute-start | bytes 393224 | tf_op jit(solution)/shard_map/ppermute | solution.py:49
  24.3 3.7 %blend.3 = (f32[2048,1024]{1,0:T(8,128)}, f32[256,128]{1,0:T(8,128)S(1)}, f32[256,128]{1,0:T(8,128)S(1)}) custom-call(bf16[2,2048,512]{2,1,0:T(8,128)(2,1)S(1)} %get-tuple-element.48.acts, bf16[2048,1024]{1,0:T(8,128)(2,1)S(1)} %get-tuple-element.49.grads, f32[1024,128]{1,0:T(8,128)S(1)} %copy-done, ...), custom_call_target="tpu_custom_call", output_to_operand_aliasing={{0}: (4, {})} | custom-call | tf_op jit(solution)/shard_map/blend/pallas_call | solution.py:254
  28.1 0.4 collective-permute-start.5
  28.5 2.8 %collective-permute-start.3 = (f32[256,128]{1,0:T(8,128)S(1)}, f32[256,128]{1,0:T(8,128)S(1)}, u32[]{:S(2)}, u32[]{:S(2)}) collective-permute-start(f32[256,128]{1,0:T(8,128)S(1)} %add_add_fusion.1), channel_id=1, source_target_pairs={{0,16},{4,20},{8,24},{12,28},{16,0},{20,4},{24,8},{28,12},{1,17},{... | collective-permute-start | bytes 393224 | tf_op jit(solution)/shard_map/ppermute | solution.py:49
  31.3 1.5 %collective-permute-done.4 = f32[256,128]{1,0:T(8,128)S(1)} collective-permute-done((f32[256,128]{1,0:T(8,128)S(1)}, f32[256,128]{1,0:T(8,128)S(1)}, u32[]{:S(2)}, u32[]{:S(2)}) %collective-permute-start.4) | collective-permute-done | bytes 131104 | tf_op jit(solution)/shard_map/ppermute | solution.py:49
  32.8 2.0 %collective-permute-done.5 = f32[256,128]{1,0:T(8,128)S(1)} collective-permute-done((f32[256,128]{1,0:T(8,128)S(1)}, f32[256,128]{1,0:T(8,128)S(1)}, u32[]{:S(2)}, u32[]{:S(2)}) %collective-permute-start.5) | collective-permute-done | bytes 131104 | tf_op jit(solution)/shard_map/ppermute | solution.py:49
  34.8 1.9 %collective-permute-start.7 = (f32[256,128]{1,0:T(8,128)S(1)}, f32[256,128]{1,0:T(8,128)S(1)}, u32[]{:S(2)}, u32[]{:S(2)}) collective-permute-start(f32[256,128]{1,0:T(8,128)S(1)} %add_add_fusion), channel_id=1, source_target_pairs={{0,16},{4,20},{8,24},{12,28},{16,0},{20,4},{24,8},{28,12},{1,17},{... | collective-permute-start | bytes 393224 | tf_op jit(solution)/shard_map/ppermute | solution.py:49
  36.8 4.1 %collective-permute-start.11 = (f32[256,128]{1,0:T(8,128)S(1)}, f32[256,128]{1,0:T(8,128)S(1)}, u32[]{:S(2)}, u32[]{:S(2)}) collective-permute-start(f32[256,128]{1,0:T(8,128)S(1)} %add_multiply_fusion.1.refs_2_.refs_0_), channel_id=1, source_target_pairs={{0,4},{4,0},{8,12},{12,8},{16,20},{20,16},{24,28},{28,24},{1,5},{5... | collective-permute-start | bytes 393224 | tf_op jit(solution)/shard_map/ppermute | solution.py:49
  40.9 0.1 collective-permute-start.12
  41.0 1.5 %collective-permute-start.13 = (f32[256,128]{1,0:T(8,128)S(1)}, f32[256,128]{1,0:T(8,128)S(1)}, u32[]{:S(2)}, u32[]{:S(2)}) collective-permute-start(f32[256,128]{1,0:T(8,128)S(1)} %add_multiply_fusion.1.refs_2_.refs_0_), channel_id=1, source_target_pairs={{0,12},{4,8},{8,4},{12,0},{16,28},{20,24},{24,20},{28,16},{1,13},{... | collective-permute-start | bytes 393224 | tf_op jit(solution)/shard_map/ppermute | solution.py:49
  42.4 0.7 collective-permute-done.7
  43.2 1.7 %collective-permute-start.10 = (f32[256,128]{1,0:T(8,128)S(1)}, f32[256,128]{1,0:T(8,128)S(1)}, u32[]{:S(2)}, u32[]{:S(2)}) collective-permute-start(f32[256,128]{1,0:T(8,128)S(1)} %add_multiply_fusion.refs_3_.refs_1_), channel_id=1, source_target_pairs={{0,12},{4,8},{8,4},{12,0},{16,28},{20,24},{24,20},{28,16},{1,13},{... | collective-permute-start | bytes 393224 | tf_op jit(solution)/shard_map/ppermute | solution.py:49
  44.8 0.2 collective-permute-start.8
  45.1 1.6 %collective-permute-start.9 = (f32[256,128]{1,0:T(8,128)S(1)}, f32[256,128]{1,0:T(8,128)S(1)}, u32[]{:S(2)}, u32[]{:S(2)}) collective-permute-start(f32[256,128]{1,0:T(8,128)S(1)} %add_multiply_fusion.refs_3_.refs_1_), channel_id=1, source_target_pairs={{0,8},{4,12},{8,0},{12,4},{16,24},{20,28},{24,16},{28,20},{1,9},{5... | collective-permute-start | bytes 393224 | tf_op jit(solution)/shard_map/ppermute | solution.py:49
  46.7 0.1 pad_add_fusion.refs_0_.who
  46.8 4.0 %right_terms.3 = (f32[128,1024]{1,0:T(8,128)S(1)}, f32[128,128]{1,0:T(8,128)S(1)}, f32[2048,1024]{1,0:T(8,128)S(1)}) custom-call(s32[4]{0:T(128)S(1)} %pad_add_fusion.refs_0_.who, f32[2048,1024]{1,0:T(8,128)} %get-tuple-element.54.refs_1_.refs_8_, f32[256,128]{1,0:T(8,128)S(1)} %add_multiply_fusion.1.refs_2_.refs_0_, ...), custom_call_target="tpu_custom_call" | custom-call | tf_op jit(solution)/shard_map/right_terms/pallas_call | solution.py:335
  50.8 1.6 %right_terms.4 = (f32[128,1024]{1,0:T(8,128)S(1)}, f32[128,128]{1,0:T(8,128)S(1)}) custom-call(s32[4]{0:T(128)S(1)} %pad_add_fusion.refs_0_.who, f32[2048,1024]{1,0:T(8,128)S(1)} %get-tuple-element.63.refs_1_, f32[256,128]{1,0:T(8,128)S(1)} %collective-permute-done.11.refs_2_, f32[256,128]{1,0:T(8,128)S(1)} %collective-permute-done.12.refs_3_.refs_4_, ...), custom_call_target="tpu_custom_call" | custom-call | tf_op jit(solution)/shard_map/right_terms/pallas_call | solution.py:335
  52.4 0.6 collective-permute-done.8.refs_2_.refs_3_
  53.0 1.6 %right_terms.5 = (f32[64,1024]{1,0:T(8,128)S(1)}, f32[64,1024]{1,0:T(8,128)S(1)}, f32[128,128]{1,0:T(8,128)S(1)}) custom-call(s32[4]{0:T(128)S(1)} %pad_add_fusion.refs_0_.who, f32[2048,1024]{1,0:T(8,128)S(1)} %get-tuple-element.63.refs_1_, f32[256,128]{1,0:T(8,128)S(1)} %collective-permute-done.8.refs_2_.refs_3_, ...), custom_call_target="tpu_custom_call" | custom-call | tf_op jit(solution)/shard_map/right_terms/pallas_call | solution.py:335
  54.7 0.5 collective-permute-start.18
  55.2 1.0 %collective-permute-done.14.arrived = f32[64,1024]{1,0:T(8,128)S(1)} collective-permute-done((f32[64,1024]{1,0:T(8,128)S(1)}, f32[64,1024]{1,0:T(8,128)S(1)}, u32[]{:S(2)}, u32[]{:S(2)}) %collective-permute-start.14) | collective-permute-done | bytes 262176 | tf_op jit(solution)/shard_map/ppermute | solution.py:49
  56.2 0.6 cut.1
  56.8 2.4 %collective-permute-start.15 = (f32[16,1024]{1,0:T(8,128)S(1)}, f32[16,1024]{1,0:T(8,128)S(1)}, u32[]{:S(2)}, u32[]{:S(2)}) collective-permute-start(f32[16,1024]{1,0:T(8,128)S(1)} %get-tuple-element.71), channel_id=1, source_target_pairs={{0,6},{1,7},{2,4},{3,5},{4,2},{5,3},{6,0},{7,1},{8,14},{9,15},{10,... | collective-permute-start | bytes 196616 | tf_op jit(solution)/shard_map/ppermute | solution.py:49
  59.3 0.6 collective-permute-start.16
  59.9 0.5 collective-permute-start.17
  60.4 1.6 %collective-permute-start.19 = (f32[128,128]{1,0:T(8,128)S(1)}, f32[128,128]{1,0:T(8,128)S(1)}, u32[]{:S(2)}, u32[]{:S(2)}) collective-permute-start(f32[128,128]{1,0:T(8,128)S(1)} %add.70.refs_0_), channel_id=1, source_target_pairs={{0,2},{1,3},{2,0},{3,1},{4,6},{5,7},{6,4},{7,5},{8,10},{9,11},{10,... | collective-permute-start | bytes 196616 | tf_op jit(solution)/shard_map/ppermute | solution.py:49
  62.0 0.5 collective-permute-done.15
  62.5 1.1 %collective-permute-done.16 = f32[16,1024]{1,0:T(8,128)S(1)} collective-permute-done((f32[16,1024]{1,0:T(8,128)S(1)}, f32[16,1024]{1,0:T(8,128)S(1)}, u32[]{:S(2)}, u32[]{:S(2)}) %collective-permute-start.16) | collective-permute-done | bytes 65568 | tf_op jit(solution)/shard_map/ppermute | solution.py:49
  63.5 0.8 collective-permute-done.17
  64.4 0.7 collective-permute-done.19.refs_1_
  65.1 1.5 %collective-permute-start.20 = (f32[16,1024]{1,0:T(8,128)S(1)}, f32[16,1024]{1,0:T(8,128)S(1)}, u32[]{:S(2)}, u32[]{:S(2)}) collective-permute-start(f32[16,1024]{1,0:T(8,128)S(1)} %add_add_fusion.2), channel_id=1, source_target_pairs={{0,8},{4,12},{8,0},{12,4},{16,24},{20,28},{24,16},{28,20},{1,9},{5... | collective-permute-start | bytes 196616 | tf_op jit(solution)/shard_map/ppermute | solution.py:49
  66.6 1.9 %factor.2.refs_0_ = f32[128,256]{1,0:T(8,128)S(1)} custom-call(f32[128,128]{1,0:T(8,128)S(1)} %add.70.refs_0_, f32[128,128]{1,0:T(8,128)S(1)} %collective-permute-done.19.refs_1_), custom_call_target="tpu_custom_call" | custom-call | tf_op jit(solution)/shard_map/factor/pallas_call | solution.py:415
  68.4 0.9 collective-permute-done.20
  69.3 4.7 %collective-permute-start.21 = (f32[16,1024]{1,0:T(8,128)S(1)}, f32[16,1024]{1,0:T(8,128)S(1)}, u32[]{:S(2)}, u32[]{:S(2)}) collective-permute-start(f32[16,1024]{1,0:T(8,128)S(1)} %add.71), channel_id=1, source_target_pairs={{0,16},{4,20},{8,24},{12,28},{16,0},{20,4},{24,8},{28,12},{1,17},{... | collective-permute-start | bytes 196616 | tf_op jit(solution)/shard_map/ppermute | solution.py:49
  74.1 1.7 %factor.3.state = f32[128,256]{1,0:T(8,128)S(1)} custom-call(f32[128,256]{1,0:T(8,128)S(1)} %factor.2.refs_0_), custom_call_target="tpu_custom_call" | custom-call | tf_op jit(solution)/shard_map/factor/pallas_call | solution.py:415
  75.7 0.6 collective-permute-done.21
  76.3 1.0 %collective-permute-start.22 = (f32[16,1024]{1,0:T(8,128)S(1)}, f32[16,1024]{1,0:T(8,128)S(1)}, u32[]{:S(2)}, u32[]{:S(2)}) collective-permute-start(f32[16,1024]{1,0:T(8,128)S(1)} %add.72), channel_id=1, source_target_pairs={{0,2},{1,3},{2,0},{3,1},{4,6},{5,7},{6,4},{7,5},{8,10},{9,11},{10,... | collective-permute-start | bytes 196616 | tf_op jit(solution)/shard_map/ppermute | solution.py:49
  77.4 1.9 %collective-permute-start.23 = (f32[16,1024]{1,0:T(8,128)S(1)}, f32[16,1024]{1,0:T(8,128)S(1)}, u32[]{:S(2)}, u32[]{:S(2)}) collective-permute-start(f32[16,1024]{1,0:T(8,128)S(1)} %add.72), channel_id=1, source_target_pairs={{0,4},{4,0},{8,12},{12,8},{16,20},{20,16},{24,28},{28,24},{1,5},{5... | collective-permute-start | bytes 196616 | tf_op jit(solution)/shard_map/ppermute | solution.py:49
  79.2 0.7 collective-permute-start.24
  79.9 4.7 %ortho.1 = (bf16[2048,256]{1,0:T(8,128)(2,1)S(1)}, f32[256,128]{1,0:T(8,128)S(1)}, f32[2048,1024]{1,0:T(8,128)S(1)}) custom-call(s32[4]{0:T(128)S(1)} %pad_add_fusion.refs_0_.who, f32[128,256]{1,0:T(8,128)S(1)} %factor.3.state, f32[256,128]{1,0:T(8,128)S(1)} %add_multiply_fusion.1.refs_2_.refs_0_, f32[256,128]{1,0:T(8,128)S(1)} %add_multiply_fusion.refs_3_.refs_1_, ...), custom_call_target="tpu_custom_call" | custom-call | tf_op jit(solution)/shard_map/ortho/pallas_call | solution.py:452
  84.8 0.1 collective-permute-start.25
  84.9 1.5 %collective-permute-done.25.right_there = f32[64,1024]{1,0:T(8,128)S(1)} collective-permute-done((f32[64,1024]{1,0:T(8,128)S(1)}, f32[64,1024]{1,0:T(8,128)S(1)}, u32[]{:S(2)}, u32[]{:S(2)}) %collective-permute-start.25) | collective-permute-done | bytes 262176 | tf_op jit(solution)/shard_map/ppermute | solution.py:49
  86.4 6.5 %finish.1 = (f32[2048,1024]{1,0:T(8,128)}, f32[256,128]{1,0:T(8,128)}, bf16[256,1024]{1,0:T(8,128)(2,1)}) custom-call(s32[4]{0:T(128)S(1)} %pad_add_fusion.refs_0_.who, f32[64,1024]{1,0:T(8,128)S(1)} %constant_dynamic-update-slice_fusion.right_here, f32[64,1024]{1,0:T(8,128)S(1)} %collective-permute-done.25.right_there, f32[128,256]{1,0:T(8,128)S(1)} %factor.3.state, ...), custom_call_target="tpu_custom_call" | custom-call | tf_op jit(solution)/shard_map/finish/pallas_call | solution.py:520
  (37 shorter events, 0.4 us)
Async XLA Ops:
  0.6 11.9 %copy-start = (f32[1024,128]{1,0:T(8,128)S(1)}, f32[1024,128]{1,0:T(8,128)}, u32[]{:S(2)}) copy-start(f32[1024,128]{1,0:T(8,128)} %basis.5) | copy-start | bytes 1572868
  16.3 11.8 %collective-permute-start.2 = (f32[256,128]{1,0:T(8,128)S(1)}, f32[256,128]{1,0:T(8,128)S(1)}, u32[]{:S(2)}, u32[]{:S(2)}) collective-permute-start(f32[256,128]{1,0:T(8,128)S(1)} %get-tuple-element.58), channel_id=1, source_target_pairs={{0,4},{4,0},{8,12},{12,8},{16,20},{20,16},{24,28},{28,24},{1,5},{5... | collective-permute-start | bytes 393224 | tf_op jit(solution)/shard_map/ppermute | solution.py:49
  19.3 9.2 %collective-permute-start = (f32[256,128]{1,0:T(8,128)S(1)}, f32[256,128]{1,0:T(8,128)S(1)}, u32[]{:S(2)}, u32[]{:S(2)}) collective-permute-start(f32[256,128]{1,0:T(8,128)S(1)} %get-tuple-element.56), channel_id=1, source_target_pairs={{0,12},{4,8},{8,4},{12,0},{16,28},{20,24},{24,20},{28,16},{1,13},{... | collective-permute-start | bytes 393224 | tf_op jit(solution)/shard_map/ppermute | solution.py:49
  20.8 7.6 %collective-permute-start.1 = (f32[256,128]{1,0:T(8,128)S(1)}, f32[256,128]{1,0:T(8,128)S(1)}, u32[]{:S(2)}, u32[]{:S(2)}) collective-permute-start(f32[256,128]{1,0:T(8,128)S(1)} %get-tuple-element.57), channel_id=1, source_target_pairs={{0,8},{4,12},{8,0},{12,4},{16,24},{20,28},{24,16},{28,20},{1,9},{5... | collective-permute-start | bytes 393224 | tf_op jit(solution)/shard_map/ppermute | solution.py:49
  20.9 10.4 %collective-permute-start.6 = (f32[256,128]{1,0:T(8,128)S(1)}, f32[256,128]{1,0:T(8,128)S(1)}, u32[]{:S(2)}, u32[]{:S(2)}) collective-permute-start(f32[256,128]{1,0:T(8,128)S(1)} %get-tuple-element.62), channel_id=1, source_target_pairs={{0,4},{4,0},{8,12},{12,8},{16,20},{20,16},{24,28},{28,24},{1,5},{5... | collective-permute-start | bytes 393224 | tf_op jit(solution)/shard_map/ppermute | solution.py:49
  22.8 10.1 %collective-permute-start.4 = (f32[256,128]{1,0:T(8,128)S(1)}, f32[256,128]{1,0:T(8,128)S(1)}, u32[]{:S(2)}, u32[]{:S(2)}) collective-permute-start(f32[256,128]{1,0:T(8,128)S(1)} %get-tuple-element.60), channel_id=1, source_target_pairs={{0,12},{4,8},{8,4},{12,0},{16,28},{20,24},{24,20},{28,16},{1,13},{... | collective-permute-start | bytes 393224 | tf_op jit(solution)/shard_map/ppermute | solution.py:49
  28.1 6.7 %collective-permute-start.5 = (f32[256,128]{1,0:T(8,128)S(1)}, f32[256,128]{1,0:T(8,128)S(1)}, u32[]{:S(2)}, u32[]{:S(2)}) collective-permute-start(f32[256,128]{1,0:T(8,128)S(1)} %get-tuple-element.61), channel_id=1, source_target_pairs={{0,8},{4,12},{8,0},{12,4},{16,24},{20,28},{24,16},{28,20},{1,9},{5... | collective-permute-start | bytes 393224 | tf_op jit(solution)/shard_map/ppermute | solution.py:49
  28.5 8.3 %collective-permute-start.3 = (f32[256,128]{1,0:T(8,128)S(1)}, f32[256,128]{1,0:T(8,128)S(1)}, u32[]{:S(2)}, u32[]{:S(2)}) collective-permute-start(f32[256,128]{1,0:T(8,128)S(1)} %add_add_fusion.1), channel_id=1, source_target_pairs={{0,16},{4,20},{8,24},{12,28},{16,0},{20,4},{24,8},{28,12},{1,17},{... | collective-permute-start | bytes 393224 | tf_op jit(solution)/shard_map/ppermute | solution.py:49
  34.8 8.3 %collective-permute-start.7 = (f32[256,128]{1,0:T(8,128)S(1)}, f32[256,128]{1,0:T(8,128)S(1)}, u32[]{:S(2)}, u32[]{:S(2)}) collective-permute-start(f32[256,128]{1,0:T(8,128)S(1)} %add_add_fusion), channel_id=1, source_target_pairs={{0,16},{4,20},{8,24},{12,28},{16,0},{20,4},{24,8},{28,12},{1,17},{... | collective-permute-start | bytes 393224 | tf_op jit(solution)/shard_map/ppermute | solution.py:49
  36.8 8.3 %collective-permute-start.11 = (f32[256,128]{1,0:T(8,128)S(1)}, f32[256,128]{1,0:T(8,128)S(1)}, u32[]{:S(2)}, u32[]{:S(2)}) collective-permute-start(f32[256,128]{1,0:T(8,128)S(1)} %add_multiply_fusion.1.refs_2_.refs_0_), channel_id=1, source_target_pairs={{0,4},{4,0},{8,12},{12,8},{16,20},{20,16},{24,28},{28,24},{1,5},{5... | collective-permute-start | bytes 393224 | tf_op jit(solution)/shard_map/ppermute | solution.py:49
  40.9 9.9 %collective-permute-start.12 = (f32[256,128]{1,0:T(8,128)S(1)}, f32[256,128]{1,0:T(8,128)S(1)}, u32[]{:S(2)}, u32[]{:S(2)}) collective-permute-start(f32[256,128]{1,0:T(8,128)S(1)} %add_multiply_fusion.1.refs_2_.refs_0_), channel_id=1, source_target_pairs={{0,8},{4,12},{8,0},{12,4},{16,24},{20,28},{24,16},{28,20},{1,9},{5... | collective-permute-start | bytes 393224 | tf_op jit(solution)/shard_map/ppermute | solution.py:49
  41.0 9.8 %collective-permute-start.13 = (f32[256,128]{1,0:T(8,128)S(1)}, f32[256,128]{1,0:T(8,128)S(1)}, u32[]{:S(2)}, u32[]{:S(2)}) collective-permute-start(f32[256,128]{1,0:T(8,128)S(1)} %add_multiply_fusion.1.refs_2_.refs_0_), channel_id=1, source_target_pairs={{0,12},{4,8},{8,4},{12,0},{16,28},{20,24},{24,20},{28,16},{1,13},{... | collective-permute-start | bytes 393224 | tf_op jit(solution)/shard_map/ppermute | solution.py:49
  43.2 9.2 %collective-permute-start.10 = (f32[256,128]{1,0:T(8,128)S(1)}, f32[256,128]{1,0:T(8,128)S(1)}, u32[]{:S(2)}, u32[]{:S(2)}) collective-permute-start(f32[256,128]{1,0:T(8,128)S(1)} %add_multiply_fusion.refs_3_.refs_1_), channel_id=1, source_target_pairs={{0,12},{4,8},{8,4},{12,0},{16,28},{20,24},{24,20},{28,16},{1,13},{... | collective-permute-start | bytes 393224 | tf_op jit(solution)/shard_map/ppermute | solution.py:49
  44.8 8.1 %collective-permute-start.8 = (f32[256,128]{1,0:T(8,128)S(1)}, f32[256,128]{1,0:T(8,128)S(1)}, u32[]{:S(2)}, u32[]{:S(2)}) collective-permute-start(f32[256,128]{1,0:T(8,128)S(1)} %add_multiply_fusion.refs_3_.refs_1_), channel_id=1, source_target_pairs={{0,4},{4,0},{8,12},{12,8},{16,20},{20,16},{24,28},{28,24},{1,5},{5... | collective-permute-start | bytes 393224 | tf_op jit(solution)/shard_map/ppermute | solution.py:49
  45.1 7.9 %collective-permute-start.9 = (f32[256,128]{1,0:T(8,128)S(1)}, f32[256,128]{1,0:T(8,128)S(1)}, u32[]{:S(2)}, u32[]{:S(2)}) collective-permute-start(f32[256,128]{1,0:T(8,128)S(1)} %add_multiply_fusion.refs_3_.refs_1_), channel_id=1, source_target_pairs={{0,8},{4,12},{8,0},{12,4},{16,24},{20,28},{24,16},{28,20},{1,9},{5... | collective-permute-start | bytes 393224 | tf_op jit(solution)/shard_map/ppermute | solution.py:49
  50.8 3.8 %copy-start.1 = (f32[256,128]{1,0:T(8,128)}, f32[256,128]{1,0:T(8,128)S(1)}, u32[]{:S(2)}) copy-start(f32[256,128]{1,0:T(8,128)S(1)} %collective-permute-done.13.refs_4_.refs_6_) | copy-start | bytes 393220
  52.4 27.5 %copy-start.2 = (f32[256,128]{1,0:T(8,128)}, f32[256,128]{1,0:T(8,128)S(1)}, u32[]{:S(2)}) copy-start(f32[256,128]{1,0:T(8,128)S(1)} %collective-permute-done.10.refs_4_.refs_7_) | copy-start | bytes 393220
  53.0 26.9 %copy-start.3 = (f32[256,128]{1,0:T(8,128)}, f32[256,128]{1,0:T(8,128)S(1)}, u32[]{:S(2)}) copy-start(f32[256,128]{1,0:T(8,128)S(1)} %collective-permute-done.9.refs_3_.refs_5_) | copy-start | bytes 393220
  54.6 1.6 %collective-permute-start.14 = (f32[64,1024]{1,0:T(8,128)S(1)}, f32[64,1024]{1,0:T(8,128)S(1)}, u32[]{:S(2)}, u32[]{:S(2)}) collective-permute-start(f32[64,1024]{1,0:T(8,128)S(1)} %get-tuple-element.69), channel_id=1, source_target_pairs={{0,1},{1,0},{2,3},{3,2},{4,5},{5,4},{6,7},{7,6},{8,9},{9,8},{10,11... | collective-permute-start | bytes 786440 | tf_op jit(solution)/shard_map/ppermute | solution.py:49
  54.7 5.7 %collective-permute-start.18 = (f32[128,128]{1,0:T(8,128)S(1)}, f32[128,128]{1,0:T(8,128)S(1)}, u32[]{:S(2)}, u32[]{:S(2)}) collective-permute-start(f32[128,128]{1,0:T(8,128)S(1)} %get-tuple-element.74), channel_id=1, source_target_pairs={{0,1},{1,0},{2,3},{3,2},{4,5},{5,4},{6,7},{7,6},{8,9},{9,8},{10,11... | collective-permute-start | bytes 196616 | tf_op jit(solution)/shard_map/ppermute | solution.py:49
  56.8 5.7 %collective-permute-start.15 = (f32[16,1024]{1,0:T(8,128)S(1)}, f32[16,1024]{1,0:T(8,128)S(1)}, u32[]{:S(2)}, u32[]{:S(2)}) collective-permute-start(f32[16,1024]{1,0:T(8,128)S(1)} %get-tuple-element.71), channel_id=1, source_target_pairs={{0,6},{1,7},{2,4},{3,5},{4,2},{5,3},{6,0},{7,1},{8,14},{9,15},{10,... | collective-permute-start | bytes 196616 | tf_op jit(solution)/shard_map/ppermute | solution.py:49
  59.3 4.3 %collective-permute-start.16 = (f32[16,1024]{1,0:T(8,128)S(1)}, f32[16,1024]{1,0:T(8,128)S(1)}, u32[]{:S(2)}, u32[]{:S(2)}) collective-permute-start(f32[16,1024]{1,0:T(8,128)S(1)} %get-tuple-element.72), channel_id=1, source_target_pairs={{0,4},{4,0},{8,12},{12,8},{16,20},{20,16},{24,28},{28,24},{1,5},{5... | collective-permute-start | bytes 196616 | tf_op jit(solution)/shard_map/ppermute | solution.py:49
  59.9 4.5 %collective-permute-start.17 = (f32[16,1024]{1,0:T(8,128)S(1)}, f32[16,1024]{1,0:T(8,128)S(1)}, u32[]{:S(2)}, u32[]{:S(2)}) collective-permute-start(f32[16,1024]{1,0:T(8,128)S(1)} %get-tuple-element.73), channel_id=1, source_target_pairs={{0,2},{1,3},{2,0},{3,1},{4,6},{5,7},{6,4},{7,5},{8,10},{9,11},{10,... | collective-permute-start | bytes 196616 | tf_op jit(solution)/shard_map/ppermute | solution.py:49
  60.4 4.7 %collective-permute-start.19 = (f32[128,128]{1,0:T(8,128)S(1)}, f32[128,128]{1,0:T(8,128)S(1)}, u32[]{:S(2)}, u32[]{:S(2)}) collective-permute-start(f32[128,128]{1,0:T(8,128)S(1)} %add.70.refs_0_), channel_id=1, source_target_pairs={{0,2},{1,3},{2,0},{3,1},{4,6},{5,7},{6,4},{7,5},{8,10},{9,11},{10,... | collective-permute-start | bytes 196616 | tf_op jit(solution)/shard_map/ppermute | solution.py:49
  65.1 4.3 %collective-permute-start.20 = (f32[16,1024]{1,0:T(8,128)S(1)}, f32[16,1024]{1,0:T(8,128)S(1)}, u32[]{:S(2)}, u32[]{:S(2)}) collective-permute-start(f32[16,1024]{1,0:T(8,128)S(1)} %add_add_fusion.2), channel_id=1, source_target_pairs={{0,8},{4,12},{8,0},{12,4},{16,24},{20,28},{24,16},{28,20},{1,9},{5... | collective-permute-start | bytes 196616 | tf_op jit(solution)/shard_map/ppermute | solution.py:49
  69.3 7.0 %collective-permute-start.21 = (f32[16,1024]{1,0:T(8,128)S(1)}, f32[16,1024]{1,0:T(8,128)S(1)}, u32[]{:S(2)}, u32[]{:S(2)}) collective-permute-start(f32[16,1024]{1,0:T(8,128)S(1)} %add.71), channel_id=1, source_target_pairs={{0,16},{4,20},{8,24},{12,28},{16,0},{20,4},{24,8},{28,12},{1,17},{... | collective-permute-start | bytes 196616 | tf_op jit(solution)/shard_map/ppermute | solution.py:49
  76.3 8.3 %collective-permute-start.22 = (f32[16,1024]{1,0:T(8,128)S(1)}, f32[16,1024]{1,0:T(8,128)S(1)}, u32[]{:S(2)}, u32[]{:S(2)}) collective-permute-start(f32[16,1024]{1,0:T(8,128)S(1)} %add.72), channel_id=1, source_target_pairs={{0,2},{1,3},{2,0},{3,1},{4,6},{5,7},{6,4},{7,5},{8,10},{9,11},{10,... | collective-permute-start | bytes 196616 | tf_op jit(solution)/shard_map/ppermute | solution.py:49
  77.4 7.3 %collective-permute-start.23 = (f32[16,1024]{1,0:T(8,128)S(1)}, f32[16,1024]{1,0:T(8,128)S(1)}, u32[]{:S(2)}, u32[]{:S(2)}) collective-permute-start(f32[16,1024]{1,0:T(8,128)S(1)} %add.72), channel_id=1, source_target_pairs={{0,4},{4,0},{8,12},{12,8},{16,20},{20,16},{24,28},{28,24},{1,5},{5... | collective-permute-start | bytes 196616 | tf_op jit(solution)/shard_map/ppermute | solution.py:49
  79.2 5.4 %collective-permute-start.24 = (f32[16,1024]{1,0:T(8,128)S(1)}, f32[16,1024]{1,0:T(8,128)S(1)}, u32[]{:S(2)}, u32[]{:S(2)}) collective-permute-start(f32[16,1024]{1,0:T(8,128)S(1)} %add.72), channel_id=1, source_target_pairs={{0,6},{1,7},{2,4},{3,5},{4,2},{5,3},{6,0},{7,1},{8,14},{9,15},{10,... | collective-permute-start | bytes 196616 | tf_op jit(solution)/shard_map/ppermute | solution.py:49
  84.8 1.6 %collective-permute-start.25 = (f32[64,1024]{1,0:T(8,128)S(1)}, f32[64,1024]{1,0:T(8,128)S(1)}, u32[]{:S(2)}, u32[]{:S(2)}) collective-permute-start(f32[64,1024]{1,0:T(8,128)S(1)} %constant_dynamic-update-slice_fusion.right_here), channel_id=1, source_target_pairs={{0,1},{1,0},{2,3},{3,2},{4,5},{5,4},{6,7},{7,6},{8,9},{9,8},{10,11... | collective-permute-start | bytes 786440 | tf_op jit(solution)/shard_map/ppermute | solution.py:49

commit v5 on v4

--- a/solution.py
+++ b/solution.py
@@ -82,6 +82,7 @@
 ANY = pl.BlockSpec(memory_space=pl.ANY)
 SMEM = pl.BlockSpec(memory_space=pltpu.SMEM)
 PARTS = 2
+CALLS = (((0, 0), (0, 1)), ((1, 0), (1, 1)))
 
 
 def sketch_of(value, both, rank):
@@ -144,7 +145,6 @@
     both[:, :rank] = basis_high
     both[:, rank:] = basis_low
     columns = [slice(p * part, (p + 1) * part) for p in range(PARTS)]
-    pending = None
     for i in range(count):
         if i == 0:
             sums = None
@@ -171,14 +171,10 @@
         for p, cols in enumerate(columns):
             rows = slice(i * block + p * part, i * block + (p + 1) * part)
             gradient = sums[p] if i == 0 else dot(acts_held[i, :, cols], held[...], 0, 0)
-            value = values[rows, :] + gradient
-            values[rows, :] = value
-            if pending is not None:
-                out_copy(pending[0]).start()
-                sketches[pending[0]][...] = sketch_of(pending[1], both[...], rank)
-            pending = (i * PARTS + p, value)
-    out_copy(pending[0]).start()
-    sketches[pending[0]][...] = sketch_of(pending[1], both[...], rank)
+            values[rows, :] = values[rows, :] + gradient
+            out_copy(i * PARTS + p).start()
+        for index in range(i * PARTS, (i + 1) * PARTS):
+            sketches[index][...] = sketch_of(values[index * part : (index + 1) * part, :], both[...], rank)
     for index in range(count * PARTS):
         out_copy(index).wait()
     for n in range(extra):
@@ -219,48 +215,46 @@
     return out[0], out[1], out[2], out[3 : 3 + extra], out[3 + extra :]
 
 
-def blend_kernel(index, first, acts, grads, basis, momentum, _, blended, *refs):
-    sketches, (values, out_sem) = refs[:PARTS], refs[PARTS:]
-    block = acts.shape[2]
+def blend_kernel(jobs, extra, acts, grads, basis, *refs):
+    momentum, refs = refs[:extra], refs[extra + 1 :]
+    blended, sketches, (values, out_sem) = refs[0], refs[1:-2], refs[-2:]
     rank = basis.shape[1]
-    part = block // PARTS
+    part = values.shape[0] // len(jobs)
     both = jnp.concatenate(split(basis[...]), 1)
-
-    def out_copy(p):
-        return pltpu.make_async_copy(
-            values.at[pl.ds(p * part, part)], blended.at[pl.ds(first + p * part, part)], out_sem.at[p]
+    copies = []
+    for n, (which, p, place) in enumerate(jobs):
+        here = slice(n * part, (n + 1) * part)
+        rows = slice(p * part, (p + 1) * part)
+        values[here, :] = momentum[which][rows, :] + dot(acts[which, :, rows], grads[...], 0, 0)
+        copies.append(
+            pltpu.make_async_copy(values.at[here], blended.at[pl.ds(place + p * part, part)], out_sem.at[n])
         )
-
-    pending = None
-    for p in range(PARTS):
-        rows = slice(p * part, (p + 1) * part)
-        value = momentum[rows, :] + dot(acts[index, :, rows], grads[...], 0, 0)
-        values[rows, :] = value
-        if pending is not None:
-            out_copy(p - 1).start()
-            sketches[p - 1][...] = sketch_of(pending, both, rank)
-        pending = value
-    out_copy(PARTS - 1).start()
-    sketches[PARTS - 1][...] = sketch_of(pending, both, rank)
-    for p in range(PARTS):
-        out_copy(p).wait()
-
-
-def blend(acts, grads, basis, momentum, blended, index, first):
+        copies[-1].start()
+    for n, sketch in enumerate(sketches):
+        sketch[...] = sketch_of(values[n * part : (n + 1) * part, :], both, rank)
+    for copy in copies:
+        copy.wait()
+
+
+def blend(acts, grads, basis, momentum, blended, jobs):
     block = acts.shape[2]
     kv, rank = basis.shape
+    part = block // PARTS
     outs = [jax.ShapeDtypeStruct(blended.shape, jnp.float32)]
-    outs += [pltpu.VMEM((block // PARTS, rank), jnp.float32)] * PARTS
+    outs += [pltpu.VMEM((part, rank), jnp.float32)] * len(jobs)
     out = pl.pallas_call(
-        functools.partial(blend_kernel, index, first),
-        in_specs=[VMEM] * 4 + [ANY],
-        out_specs=[ANY] + [VMEM] * PARTS,
+        functools.partial(blend_kernel, jobs, len(momentum)),
+        in_specs=[VMEM] * (3 + len(momentum)) + [ANY],
+        out_specs=[ANY] + [VMEM] * len(jobs),
         out_shape=outs,
-        scratch_shapes=[pltpu.VMEM((block, kv), jnp.float32), pltpu.SemaphoreType.DMA((PARTS,))],
-        input_output_aliases={4: 0},
+        scratch_shapes=[
+            pltpu.VMEM((len(jobs) * part, kv), jnp.float32),
+            pltpu.SemaphoreType.DMA((len(jobs),)),
+        ],
+        input_output_aliases={3 + len(momentum): 0},
         compiler_params=params(BLEND_MIB),
         name="blend",
-    )(acts, grads, basis, momentum, blended)
+    )(acts, grads, basis, *momentum, blended)
     return out[0], out[1:]
 
 
@@ -274,6 +268,16 @@
     gram = dot(stacked, stacked, 1, 1)
     gram = gram[:rank, :rank] + gram[rank:, rank:] + (gram[:rank, rank:] + gram[rank:, :rank])
     return wide[:rank] + wide[rank:] + dot(high, blended_low, 1, 0), gram
+
+
+def pack(gram, width):
+    rank = gram.shape[0]
+    rows = rank * rank // width
+    return jnp.concatenate([gram[k * rows : (k + 1) * rows, :] for k in range(rank // rows)], 1)
+
+
+def unpack(packed, rank):
+    return jnp.concatenate([packed[:, k * rank : (k + 1) * rank] for k in range(packed.shape[1] // rank)], 0)
 
 
 def right_kernel(pieces, first, last, scale, *refs):
@@ -304,18 +308,20 @@
             for copy in copies[1:]:
                 copy.wait()
         return
-    befores, refs = refs[:-4], refs[-4:]
-    keep, give, gram_out, total = refs
+    befores, refs = refs[:-3], refs[-3:]
+    keep, give, total = refs
     for before in befores[::2]:
         right = right + before[...]
     for before in befores[1::2]:
         gram = gram + before[...]
-    gram_out[...] = gram
     total[...] = right
-    half = keep.shape[0]
+    half = total.shape[0] // 2
     core = who[2] & 1
-    keep[...] = total[pl.ds(pl.multiple_of(core * half, half), half), :]
-    give[...] = total[pl.ds(pl.multiple_of((1 - core) * half, half), half), :]
+    keep[:half, :] = total[pl.ds(pl.multiple_of(core * half, half), half), :]
+    give[:half, :] = total[pl.ds(pl.multiple_of((1 - core) * half, half), half), :]
+    packed = pack(gram, right.shape[1])
+    keep[half:, :] = packed
+    give[half:, :] = packed
 
 
 def right_terms(who, blended, pieces, sketches, scale, befores=None, first=False):
@@ -324,7 +330,7 @@
     last = befores is not None
     gram = pltpu.VMEM((rank, rank), jnp.float32)
     if last:
-        outs = [pltpu.VMEM((rank // 2, kv), jnp.float32)] * 2 + [gram]
+        outs = [pltpu.VMEM((rank // 2 + rank * rank // kv, kv), jnp.float32)] * 2
     else:
         outs = [pltpu.VMEM((rank, kv), jnp.float32), pltpu.VMEM((rank, rank), jnp.float32)]
     scratch = [pltpu.VMEM((rank, kv), jnp.float32)] if last else []
@@ -343,20 +349,29 @@
     )(*operands)
 
 
-def cut_kernel(count, who, keep, arrived, *blocks):
+def cut_kernel(count, who, keep, arrived, *outs):
+    blocks, gram = outs[:-1], outs[-1]
     block = blocks[0].shape[0]
+    half = count * block
+    packed = keep[half:, :] + arrived[half:, :]
+    gram[...] = packed
     for s, out in enumerate(blocks):
         here = pl.ds(pl.multiple_of((who[3] ^ s) * block, block), block)
-        out[...] = keep[here, :] + arrived[here, :]
-
-
-def cut(who, keep, arrived, count):
-    rows, kv = keep.shape
+        out[:block, :] = keep[here, :] + arrived[here, :]
+        if 0 < s < count // 2:
+            out[block:, :] = packed
+
+
+def cut(who, keep, arrived, rank, count):
+    kv = keep.shape[1]
+    block = rank // 2 // count
+    extra = rank * rank // kv
+    shapes = [(block + (extra if 0 < s < count // 2 else 0), kv) for s in range(count)] + [(extra, kv)]
     return pl.pallas_call(
         functools.partial(cut_kernel, count),
         in_specs=[SMEM, VMEM, VMEM],
-        out_specs=[VMEM] * count,
-        out_shape=[pltpu.VMEM((rows // count, kv), jnp.float32)] * count,
+        out_specs=[VMEM] * len(shapes),
+        out_shape=[pltpu.VMEM(shape, jnp.float32) for shape in shapes],
         compiler_params=params(16),
         name="cut",
     )(who, keep, arrived)
@@ -365,16 +380,18 @@
 PANEL = 16
 
 
-def factor_kernel(panels, fresh, *refs):
-    rank = refs[0].shape[0]
-    if fresh:
-        gram_a, gram_b, out = refs
+def factor_kernel(panels, grams, block, *refs):
+    out = refs[-1]
+    rank = out.shape[0]
+    if grams:
+        packed = refs[0][...]
+        for ref in refs[1:grams]:
+            packed = packed + ref[block:, :]
         rows_id = lax.broadcasted_iota(jnp.int32, (rank, rank), 0)
         cols_id = lax.broadcasted_iota(jnp.int32, (rank, rank), 1)
-        out[:, :rank] = gram_a[...] + gram_b[...]
+        out[:, :rank] = unpack(packed, rank)
         out[:, rank:] = jnp.where(rows_id == cols_id, 1.0, 0.0)
     else:
-        out = refs[1]
         out[...] = refs[0][...]
     index = lax.broadcasted_iota(jnp.int32, (PANEL, rank), 0)
     for start in panels:
@@ -410,10 +427,9 @@
             out[below, :] = out[below, :] - update[start + PANEL :, :]
 
 
-def factor(panels, *inputs):
-    rank = inputs[0].shape[0]
+def factor(panels, rank, inputs, grams, block):
     return pl.pallas_call(
-        functools.partial(factor_kernel, panels, len(inputs) == 2),
+        functools.partial(factor_kernel, panels, grams, block),
         in_specs=[VMEM] * len(inputs),
         out_specs=VMEM,
         out_shape=pltpu.VMEM((rank, 2 * rank), jnp.float32),
@@ -422,11 +438,35 @@
     )(*inputs)
 
 
+LOADS = 4
+
+
+def load_kernel(source, token, held, sem):
+    rows = source.shape[0] // LOADS
+    copies = []
+    for n in range(LOADS):
+        here = pl.ds(n * rows, rows)
+        copies.append(pltpu.make_async_copy(source.at[here], held.at[here], sem.at[n]))
+        copies[-1].start()
+    for copy in copies:
+        copy.wait()
+
+
+def load(source, token):
+    return pl.pallas_call(
+        load_kernel,
+        in_specs=[ANY, ANY],
+        out_specs=VMEM,
+        out_shape=pltpu.VMEM(source.shape, source.dtype),
+        scratch_shapes=[pltpu.SemaphoreType.DMA((LOADS,))],
+        compiler_params=params(FIRST_MIB),
+        name="load",
+    )(source, token)
+
+
 def ortho_kernel(group, who, state, *refs):
     sketches, refs = refs[: PARTS * group], refs[PARTS * group :]
-    blended, ortho, own_ortho, held, total, sem = refs
-    copy = pltpu.make_async_copy(blended, held, sem)
-    copy.start()
+    ortho, own_ortho, total = refs
     rank = state.shape[0]
     part = sketches[0].shape[0]
     inverse = state[:, rank:]
@@ -443,104 +483,93 @@
             total[pl.ds(pl.multiple_of(start, part), part), :] = value
     own = own_ortho.shape[0]
     own_ortho[...] = total[pl.ds(pl.multiple_of(who[1] * own, own), own), :]
-    copy.wait()
-
-
-def orthonormal(who, state, sketches, blended, group, n_dp):
+
+
+def orthonormal(who, state, sketches, group, n_dp):
     rank = state.shape[0]
     rows = sketches[0].shape[0] * len(sketches)
     return pl.pallas_call(
         functools.partial(ortho_kernel, group),
-        in_specs=[SMEM] + [VMEM] * (1 + len(sketches)) + [ANY],
-        out_specs=[VMEM] * 3,
+        in_specs=[SMEM] + [VMEM] * (1 + len(sketches)),
+        out_specs=[VMEM] * 2,
         out_shape=[
             pltpu.VMEM((rows, 2 * rank), jnp.bfloat16),
             pltpu.VMEM((rows // n_dp, rank), jnp.float32),
-            pltpu.VMEM(blended.shape, jnp.float32),
         ],
-        scratch_shapes=[pltpu.VMEM((rows, rank), jnp.float32), pltpu.SemaphoreType.DMA],
-        compiler_params=params(FIRST_MIB),
+        scratch_shapes=[pltpu.VMEM((rows, rank), jnp.float32)],
+        compiler_params=params(16),
         name="ortho",
-    )(who, state, *sketches, blended)
+    )(who, state, *sketches)
+
+
+CUTS = 2
 
 
 def finish_kernel(group, places, scale, who, right_here, right_there, state, ortho, own_ortho, *refs):
-    blended, new_momentum, new_basis, update, right, coeff, coeff_high, coeff_low = refs
-    step = pl.program_id(0)
-    block = new_momentum.shape[0]
+    blended, new_momentum, new_basis, update, right, values, coeff_high, coeff_low, sem = refs
     rank, kv = right.shape
     half = rank // 2
     core = who[2] & 1
-
-    @pl.when(step == 0)
-    def _():
-        right[pl.ds(pl.multiple_of(core * half, half), half), :] = right_here[...]
-        right[pl.ds(pl.multiple_of((1 - core) * half, half), half), :] = right_there[...]
-        value = dot(state[:, rank:], right[...], 1, 0, EXACT)
-        coeff[...] = value
-        high, low = split(0.2 * value)
-        coeff_high[:rank, :] = high
-        coeff_high[rank:, :] = high
-        coeff_low[...] = low
-
-    def feedback(s):
-        rows = ortho[s * block : (s + 1) * block, :]
-        return dot(rows, coeff_high[...], 1, 0) + dot(rows[:, :rank], coeff_low[...], 1, 0)
-
+    right[pl.ds(pl.multiple_of(core * half, half), half), :] = right_here[...]
+    right[pl.ds(pl.multiple_of((1 - core) * half, half), half), :] = right_there[...]
+    coeff = dot(state[:, rank:], right[...], 1, 0, EXACT)
+    high, low = split(0.2 * coeff)
+    coeff_high[:rank, :] = high
+    coeff_high[rank:, :] = high
+    coeff_low[...] = low
+    block = values.shape[0] // group
+    rows = block // CUTS
+    copies = []
     for s in range(group):
-
-        @pl.when(step == s)
-        def _(s=s):
-            new_momentum[...] = blended[places[s] : places[s] + block, :] - feedback(s)
-
-    @pl.when(step == group - 1)
-    def _():
-        value = coeff[...]
-        norm = jnp.sqrt(jnp.sum(value * value, axis=1, keepdims=True) + 1e-06)
-        normed = value / norm
-        count = new_basis.shape[0]
-        for j in range(kv // count):
-
-            @pl.when(who[2] == j)
-            def _(j=j):
-                new_basis[...] = normed[:, j * count : (j + 1) * count].T
-
-        rows_high, rows_low = split(own_ortho[...])
-        high, low = split(normed)
-        product = dot(jnp.concatenate([rows_high, rows_low], 1), jnp.concatenate([high, high], 0), 1, 0)
-        update[...] = (scale * (product + dot(rows_high, low, 1, 0))).astype(update.dtype)
+        for c in range(CUTS):
+            here = slice(s * block + c * rows, s * block + (c + 1) * rows)
+            part = ortho[here, :]
+            feedback = dot(part, coeff_high[...], 1, 0) + dot(part[:, :rank], coeff_low[...], 1, 0)
+            at = places[s] + c * rows
+            values[here, :] = blended[at : at + rows, :] - feedback
+            there = pl.multiple_of((who[0] ^ s) * block + c * rows, rows)
+            copies.append(
+                pltpu.make_async_copy(values.at[here], new_momentum.at[pl.ds(there, rows)], sem.at[len(copies)])
+            )
+            copies[-1].start()
+    norm = jnp.sqrt(jnp.sum(coeff * coeff, axis=1, keepdims=True) + 1e-06)
+    normed = coeff / norm
+    count = new_basis.shape[0]
+    for j in range(kv // count):
+
+        @pl.when(who[2] == j)
+        def _(j=j):
+            new_basis[...] = normed[:, j * count : (j + 1) * count].T
+
+    rows_high, rows_low = split(own_ortho[...])
+    high, low = split(normed)
+    product = dot(jnp.concatenate([rows_high, rows_low], 1), jnp.concatenate([high, high], 0), 1, 0)
+    update[...] = (scale * (product + dot(rows_high, low, 1, 0))).astype(update.dtype)
+    for copy in copies:
+        copy.wait()
 
 
 def finish(who, right_here, right_there, state, ortho, own_ortho, blended, places, n_rows, scale):
     rank, kv = 2 * right_here.shape[0], right_here.shape[1]
     group = len(places)
     rows = ortho.shape[0]
-    block = rows // group
-    const = lambda i, who: (0, 0)
     return pl.pallas_call(
         functools.partial(finish_kernel, group, places, scale),
-        grid_spec=pltpu.PrefetchScalarGridSpec(
-            num_scalar_prefetch=1,
-            grid=(group,),
-            in_specs=[VMEM] * 6,
-            out_specs=[
-                pl.BlockSpec((block, kv), lambda i, who: (who[0] ^ i, 0)),
-                pl.BlockSpec((kv // n_rows, rank), const),
-                pl.BlockSpec(own_ortho.shape[:1] + (kv,), const),
-            ],
-            scratch_shapes=[
-                pltpu.VMEM((rank, kv), jnp.float32),
-                pltpu.VMEM((rank, kv), jnp.float32),
-                pltpu.VMEM((2 * rank, kv), jnp.bfloat16),
-                pltpu.VMEM((rank, kv), jnp.bfloat16),
-            ],
-        ),
+        in_specs=[SMEM] + [VMEM] * 6,
+        out_specs=[ANY, VMEM, VMEM],
         out_shape=[
             jax.ShapeDtypeStruct((rows, kv), jnp.float32),
             jax.ShapeDtypeStruct((kv // n_rows, rank), jnp.float32),
             jax.ShapeDtypeStruct(own_ortho.shape[:1] + (kv,), jnp.bfloat16),
         ],
-        compiler_params=params(16),
+        scratch_shapes=[
+            pltpu.VMEM((rank, kv), jnp.float32),
+            pltpu.VMEM((rows, kv), jnp.float32),
+            pltpu.VMEM((2 * rank, kv), jnp.bfloat16),
+            pltpu.VMEM((rank, kv), jnp.bfloat16),
+            pltpu.SemaphoreType.DMA((group * CUTS,)),
+        ],
+        compiler_params=params(32),
         name="finish",
     )(who, right_here, right_there, state, ortho, own_ortho, blended)
 
@@ -572,12 +601,15 @@
             arrived[p].append(swap(given[i * PARTS + p], {"dp": offset}))
     for n, offset in enumerate(later):
         places[offset] = (len(offsets) + n) * block
-        blended, given = blend(acts_later, held, basis, momentum_later[n], blended, n, places[offset])
-        if offset == 0:
-            own = list(given)
-        else:
-            for p in range(PARTS):
-                arrived[p].append(swap(given[p], {"dp": offset}))
+    own = [None] * PARTS
+    for calls in CALLS:
+        jobs = tuple((n, p, places[later[n]]) for n, p in calls)
+        blended, given = blend(acts_later, held, basis, momentum_later, blended, jobs)
+        for (n, p), value in zip(calls, given):
+            if later[n] == 0:
+                own[p] = value
+            else:
+                arrived[p].append(swap(value, {"dp": later[n]}))
     sketches = [[None] * PARTS for _ in range(group)]
     for p in range(PARTS):
         for piece in arrived[p]:
@@ -598,32 +630,33 @@
         if p + 1 < PARTS:
             befores += right_terms(who, held, pieces, given, scale)
         else:
-            keep, give, gram = right_terms(who, held, pieces, given, scale, befores)
-
-    blocks = cut(who, keep, swap(give, {"rows": 1}), 1 << len(plane))
-    gram = gram + swap(gram, {"rows": 1})
-    row_masks = bits_of(n_rows)[1:]
-    for mask in row_masks[:-1]:
-        gram = gram + swap(gram, {"rows": mask})
-    gram_other = swap(gram, {"rows": row_masks[-1]})
+            keep, give = right_terms(who, held, pieces, given, scale, befores)
+
+    count = 1 << len(plane)
+    *blocks, gram = cut(who, keep, swap(give, {"rows": 1}), rank, count)
     right = blocks[0]
-    for s in range(len(blocks) - 1, 0, -1):
-        right = right + swap(blocks[s], masks_of([d for b, d in enumerate(plane) if s >> b & 1]))
+    block = right.shape[0]
+    grams = [gram]
+    for s in range(count - 1, 0, -1):
+        piece = swap(blocks[s], masks_of([d for b, d in enumerate(plane) if s >> b & 1]))
+        if s < count // 2:
+            grams.append(piece)
+            piece = piece[:block]
+        right = right + piece
     panels = list(range(0, rank, PANEL))
     middle = len(panels) // 2
-    right, gram, gram_other = lax.optimization_barrier((right, gram, gram_other))
-    state = None
-    for step, mask in enumerate(bits_of(n_dp)[1:]):
-        other = swap(right, {"dp": mask})
-        if step == 0:
-            state = factor(panels[:middle], gram, gram_other)
-        elif step == 1:
-            state = factor(panels[middle:], state)
-        right, state = lax.optimization_barrier((right + other, state))
+    state = factor(panels, rank, grams, len(grams), block)
+    masks = bits_of(n_dp)[1:]
+    for first in range(0, len(masks), 2):
+        pair = masks[first : first + 2]
+        pieces = [swap(right, {"dp": mask}) for mask in ([sum(pair)] + pair[::-1])[: 2 ** len(pair) - 1]]
+        *pieces, state = lax.optimization_barrier((*pieces, state))
+        for piece in pieces:
+            right = right + piece
     flat = [sketches[s][p] for s in range(group) for p in range(PARTS)]
-    ortho, own_ortho, held = orthonormal(who, state, flat, blended, group, n_dp)
-    right, ortho = gather(right, plane, ortho)
+    right, held = gather(right, plane, load(blended, right))
     other = swap(right, {"rows": 1})
+    ortho, own_ortho = orthonormal(who, state, flat, group, n_dp)
 
     new_momentum, new_basis, update = finish(
         who, right, other, state, ortho, own_ortho, held, places, n_rows,

time: 93.1 us -> 89.6 us (0.962)
  starting transfers between devices: 38 us -> 34.8 us
  Pallas kernels: 41.9 us -> 40.3 us
  waiting for transfers between devices: 11.9 us -> 13 us
    pallas_call x1, Pallas kernels: 4.71 us -> 1.13 us  [orthonormal(): pl.pallas_call(functools.partial(ortho_kernel, group), in_specs=[SMEM] +...]
    ppermute x26 -> x25, starting transfers between devices: 38 us -> 34.8 us  [swap(): return lax.ppermute(value, axes, pairs)]
    pallas_call x5, Pallas kernels: 17.5 us -> 19.5 us  [the longest x2 6.71 us: blend(): pl.pallas_call(functools.partial(blend_kernel, jobs, len(momentum)), in_s...]
    ppermute x26 -> x25, waiting for transfers between devices: 11.9 us -> 13 us  [swap(): return lax.ppermute(value, axes, pairs)]
  transfers between devices with their start and end apart: 26 -> 25, of which waited for: 12 -> 10; matrix products, arithmetic and copies ran while one was open for 0% -> 0% of each run, Pallas kernels for 19% -> 19%
where the time goes in v5:
time: 89.6 us; the launch traced here: 89.4 us
  Pallas kernels  40.3 us (45%)
  starting transfers between devices  34.8 us (39%)
  waiting for transfers between devices  13 us (15%)
  between operations  1.04 us (1%)
    ppermute x25, starting transfers between devices, swap(): return lax.ppermute(value, axes, pairs)  34.8 us
    ppermute x25, waiting for transfers between devices, swap(): return lax.ppermute(value, axes, pairs)  13 us
    pallas_call x1, Pallas kernels, first_blend(): pl.pallas_call(functools.partial(first_blend_kernel, group, offsets, late...  11.7 us
    pallas_call x3, Pallas kernels, right_terms(): pl.pallas_call(functools.partial(right_kernel, pieces, first, last, scale...  7.37 us
    pallas_call x2, Pallas kernels, blend(): pl.pallas_call(functools.partial(blend_kernel, jobs, len(momentum)), in_s...  6.71 us
    pallas_call x1, Pallas kernels, finish(): pl.pallas_call(functools.partial(finish_kernel, group, places, scale), in...  5.74 us
    pallas_call x1, Pallas kernels, factor(): pl.pallas_call(functools.partial(factor_kernel, panels, grams, block), in...  3.53 us
    pallas_call x1, Pallas kernels, load(): pl.pallas_call(load_kernel, in_specs=[ANY, ANY], out_specs=VMEM, out_shap...  3.5 us
  transfers between devices with their start and end apart: 25, of which 10 were waited for; matrix products, arithmetic and copies ran while one was open for 0% of the time, Pallas kernels for 19%

profile of v5, /device:TPU:0, one launch (start us, length us, event | category | flops | bytes accessed | tf_op | source)
XLA Modules:
  0.0 89.4 jit_solution(11584479900723306926)
XLA Ops:
  0.6 11.7 %first_blend.1 = (f32[2048,1024]{1,0:T(8,128)}, bf16[2048,1024]{1,0:T(8,128)(2,1)S(1)}, bf16[2,2048,512]{2,1,0:T(8,128)(2,1)S(1)}, f32[512,1024]{1,0:T(8,128)S(1...) custom-call(bf16[2048,2048]{1,0:T(8,128)(2,1)} %acts.1, ...), custom_call_target="tpu_custom_call" | custom-call | tf_op jit(solution)/shard_map/first_blend/pallas_call | solution.py:197
  12.4 3.4 %blend.2 = (f32[2048,1024]{1,0:T(8,128)}, f32[256,128]{1,0:T(8,128)S(1)}, f32[256,128]{1,0:T(8,128)S(1)}) custom-call(bf16[2,2048,512]{2,1,0:T(8,128)(2,1)S(1)} %get-tuple-element.44.acts, bf16[2048,1024]{1,0:T(8,128)(2,1)S(1)} %get-tuple-element.45.grads, f32[1024,128]{1,0:T(8,128)S(1)} %copy-done, ...), custom_call_target="tpu_custom_call", output_to_operand_aliasing={{0}: (5, {})} | custom-call | tf_op jit(solution)/shard_map/blend/pallas_call | solution.py:245
  15.8 3.0 %collective-permute-start.2 = (f32[256,128]{1,0:T(8,128)S(1)}, f32[256,128]{1,0:T(8,128)S(1)}, u32[]{:S(2)}, u32[]{:S(2)}) collective-permute-start(f32[256,128]{1,0:T(8,128)S(1)} %get-tuple-element.54), channel_id=1, source_target_pairs={{0,4},{4,0},{8,12},{12,8},{16,20},{20,16},{24,28},{28,24},{1,5},{5... | collective-permute-start | bytes 393224 | tf_op jit(solution)/shard_map/ppermute | solution.py:49
  18.8 1.5 %collective-permute-start = (f32[256,128]{1,0:T(8,128)S(1)}, f32[256,128]{1,0:T(8,128)S(1)}, u32[]{:S(2)}, u32[]{:S(2)}) collective-permute-start(f32[256,128]{1,0:T(8,128)S(1)} %get-tuple-element.52), channel_id=1, source_target_pairs={{0,12},{4,8},{8,4},{12,0},{16,28},{20,24},{24,20},{28,16},{1,13},{... | collective-permute-start | bytes 393224 | tf_op jit(solution)/shard_map/ppermute | solution.py:49
  20.3 0.0 collective-permute-start.1
  20.3 1.9 %collective-permute-start.6 = (f32[256,128]{1,0:T(8,128)S(1)}, f32[256,128]{1,0:T(8,128)S(1)}, u32[]{:S(2)}, u32[]{:S(2)}) collective-permute-start(f32[256,128]{1,0:T(8,128)S(1)} %get-tuple-element.58), channel_id=1, source_target_pairs={{0,4},{4,0},{8,12},{12,8},{16,20},{20,16},{24,28},{28,24},{1,5},{5... | collective-permute-start | bytes 393224 | tf_op jit(solution)/shard_map/ppermute | solution.py:49
  22.3 1.5 %collective-permute-start.4 = (f32[256,128]{1,0:T(8,128)S(1)}, f32[256,128]{1,0:T(8,128)S(1)}, u32[]{:S(2)}, u32[]{:S(2)}) collective-permute-start(f32[256,128]{1,0:T(8,128)S(1)} %get-tuple-element.56), channel_id=1, source_target_pairs={{0,12},{4,8},{8,4},{12,0},{16,28},{20,24},{24,20},{28,16},{1,13},{... | collective-permute-start | bytes 393224 | tf_op jit(solution)/shard_map/ppermute | solution.py:49
  23.8 3.4 %blend.3 = (f32[2048,1024]{1,0:T(8,128)}, f32[256,128]{1,0:T(8,128)S(1)}, f32[256,128]{1,0:T(8,128)S(1)}) custom-call(bf16[2,2048,512]{2,1,0:T(8,128)(2,1)S(1)} %get-tuple-element.44.acts, bf16[2048,1024]{1,0:T(8,128)(2,1)S(1)} %get-tuple-element.45.grads, f32[1024,128]{1,0:T(8,128)S(1)} %copy-done, ...), custom_call_target="tpu_custom_call", output_to_operand_aliasing={{0}: (5, {})} | custom-call | tf_op jit(solution)/shard_map/blend/pallas_call | solution.py:245
  27.1 0.0 collective-permute-done.2
  27.2 0.8 collective-permute-start.5
  28.0 2.7 %collective-permute-start.3 = (f32[256,128]{1,0:T(8,128)S(1)}, f32[256,128]{1,0:T(8,128)S(1)}, u32[]{:S(2)}, u32[]{:S(2)}) collective-permute-start(f32[256,128]{1,0:T(8,128)S(1)} %add_add_fusion.1), channel_id=1, source_target_pairs={{0,16},{4,20},{8,24},{12,28},{16,0},{20,4},{24,8},{28,12},{1,17},{... | collective-permute-start | bytes 393224 | tf_op jit(solution)/shard_map/ppermute | solution.py:49
  30.6 2.1 %collective-permute-done.4 = f32[256,128]{1,0:T(8,128)S(1)} collective-permute-done((f32[256,128]{1,0:T(8,128)S(1)}, f32[256,128]{1,0:T(8,128)S(1)}, u32[]{:S(2)}, u32[]{:S(2)}) %collective-permute-start.4) | collective-permute-done | bytes 131104 | tf_op jit(solution)/shard_map/ppermute | solution.py:49
  32.7 1.8 %collective-permute-done.5 = f32[256,128]{1,0:T(8,128)S(1)} collective-permute-done((f32[256,128]{1,0:T(8,128)S(1)}, f32[256,128]{1,0:T(8,128)S(1)}, u32[]{:S(2)}, u32[]{:S(2)}) %collective-permute-start.5) | collective-permute-done | bytes 131104 | tf_op jit(solution)/shard_map/ppermute | solution.py:49
  34.6 1.7 %collective-permute-start.7 = (f32[256,128]{1,0:T(8,128)S(1)}, f32[256,128]{1,0:T(8,128)S(1)}, u32[]{:S(2)}, u32[]{:S(2)}) collective-permute-start(f32[256,128]{1,0:T(8,128)S(1)} %add_add_fusion), channel_id=1, source_target_pairs={{0,16},{4,20},{8,24},{12,28},{16,0},{20,4},{24,8},{28,12},{1,17},{... | collective-permute-start | bytes 393224 | tf_op jit(solution)/shard_map/ppermute | solution.py:49
  36.3 4.1 %collective-permute-start.11 = (f32[256,128]{1,0:T(8,128)S(1)}, f32[256,128]{1,0:T(8,128)S(1)}, u32[]{:S(2)}, u32[]{:S(2)}) collective-permute-start(f32[256,128]{1,0:T(8,128)S(1)} %add_multiply_fusion.1.refs_2_.refs_0_), channel_id=1, source_target_pairs={{0,4},{4,0},{8,12},{12,8},{16,20},{20,16},{24,28},{28,24},{1,5},{5... | collective-permute-start | bytes 393224 | tf_op jit(solution)/shard_map/ppermute | solution.py:49
  40.4 0.1 collective-permute-start.12
  40.5 1.5 %collective-permute-start.13 = (f32[256,128]{1,0:T(8,128)S(1)}, f32[256,128]{1,0:T(8,128)S(1)}, u32[]{:S(2)}, u32[]{:S(2)}) collective-permute-start(f32[256,128]{1,0:T(8,128)S(1)} %add_multiply_fusion.1.refs_2_.refs_0_), channel_id=1, source_target_pairs={{0,12},{4,8},{8,4},{12,0},{16,28},{20,24},{24,20},{28,16},{1,13},{... | collective-permute-start | bytes 393224 | tf_op jit(solution)/shard_map/ppermute | solution.py:49
  41.9 0.7 collective-permute-done.7
  42.6 1.7 %collective-permute-start.10 = (f32[256,128]{1,0:T(8,128)S(1)}, f32[256,128]{1,0:T(8,128)S(1)}, u32[]{:S(2)}, u32[]{:S(2)}) collective-permute-start(f32[256,128]{1,0:T(8,128)S(1)} %add_multiply_fusion.refs_3_.refs_1_), channel_id=1, source_target_pairs={{0,12},{4,8},{8,4},{12,0},{16,28},{20,24},{24,20},{28,16},{1,13},{... | collective-permute-start | bytes 393224 | tf_op jit(solution)/shard_map/ppermute | solution.py:49
  44.3 0.2 collective-permute-start.8
  44.5 1.6 %collective-permute-start.9 = (f32[256,128]{1,0:T(8,128)S(1)}, f32[256,128]{1,0:T(8,128)S(1)}, u32[]{:S(2)}, u32[]{:S(2)}) collective-permute-start(f32[256,128]{1,0:T(8,128)S(1)} %add_multiply_fusion.refs_3_.refs_1_), channel_id=1, source_target_pairs={{0,8},{4,12},{8,0},{12,4},{16,24},{20,28},{24,16},{28,20},{1,9},{5... | collective-permute-start | bytes 393224 | tf_op jit(solution)/shard_map/ppermute | solution.py:49
  46.2 0.1 pad_add_fusion.refs_0_.who
  46.3 4.0 %right_terms.3 = (f32[128,1024]{1,0:T(8,128)S(1)}, f32[128,128]{1,0:T(8,128)S(1)}, f32[2048,1024]{1,0:T(8,128)S(1)}) custom-call(s32[4]{0:T(128)S(1)} %pad_add_fusion.refs_0_.who, f32[2048,1024]{1,0:T(8,128)} %get-tuple-element.50.refs_1_.source, f32[256,128]{1,0:T(8,128)S(1)} %add_multiply_fusion.1.refs_2_.refs_0_, ...), custom_call_target="tpu_custom_call" | custom-call | tf_op jit(solution)/shard_map/right_terms/pallas_call | solution.py:341
  50.3 1.7 %right_terms.4 = (f32[128,1024]{1,0:T(8,128)S(1)}, f32[128,128]{1,0:T(8,128)S(1)}) custom-call(s32[4]{0:T(128)S(1)} %pad_add_fusion.refs_0_.who, f32[2048,1024]{1,0:T(8,128)S(1)} %get-tuple-element.59.refs_1_, f32[256,128]{1,0:T(8,128)S(1)} %collective-permute-done.11.refs_2_, f32[256,128]{1,0:T(8,128)S(1)} %collective-permute-done.12.refs_3_.refs_4_, ...), custom_call_target="tpu_custom_call" | custom-call | tf_op jit(solution)/shard_map/right_terms/pallas_call | solution.py:341
  52.1 0.4 collective-permute-done.8.refs_2_.refs_3_
  52.4 0.1 collective-permute-done.9.refs_3_.refs_5_
  52.5 1.6 %right_terms.5 = (f32[80,1024]{1,0:T(8,128)S(1)}, f32[80,1024]{1,0:T(8,128)S(1)}) custom-call(s32[4]{0:T(128)S(1)} %pad_add_fusion.refs_0_.who, f32[2048,1024]{1,0:T(8,128)S(1)} %get-tuple-element.59.refs_1_, f32[256,128]{1,0:T(8,128)S(1)} %collective-permute-done.8.refs_2_.refs_3_, f32[256,128]{1,0:T(8,128)S(1)} %collective-permute-done.9.refs_3_.refs_5_, ...), custom_call_target="tpu_custom_call" | custom-call | tf_op jit(solution)/shard_map/right_terms/pallas_call | solution.py:341
  54.1 0.1 collective-permute-start.14
  54.2 1.6 %collective-permute-done.14.arrived = f32[80,1024]{1,0:T(8,128)S(1)} collective-permute-done((f32[80,1024]{1,0:T(8,128)S(1)}, f32[80,1024]{1,0:T(8,128)S(1)}, u32[]{:S(2)}, u32[]{:S(2)}) %collective-permute-start.14) | collective-permute-done | bytes 327712 | tf_op jit(solution)/shard_map/ppermute | solution.py:49
  55.8 0.6 cut.1
  56.4 1.6 %collective-permute-start.17 = (f32[32,1024]{1,0:T(8,128)S(1)}, f32[32,1024]{1,0:T(8,128)S(1)}, u32[]{:S(2)}, u32[]{:S(2)}) collective-permute-start(f32[32,1024]{1,0:T(8,128)S(1)} %get-tuple-element.69), channel_id=1, source_target_pairs={{0,2},{1,3},{2,0},{3,1},{4,6},{5,7},{6,4},{7,5},{8,10},{9,11},{10,... | collective-permute-start | bytes 393224 | tf_op jit(solution)/shard_map/ppermute | solution.py:49
  58.0 1.4 %collective-permute-start.15 = (f32[16,1024]{1,0:T(8,128)S(1)}, f32[16,1024]{1,0:T(8,128)S(1)}, u32[]{:S(2)}, u32[]{:S(2)}) collective-permute-start(f32[16,1024]{1,0:T(8,128)S(1)} %get-tuple-element.67), channel_id=1, source_target_pairs={{0,6},{1,7},{2,4},{3,5},{4,2},{5,3},{6,0},{7,1},{8,14},{9,15},{10,... | collective-permute-start | bytes 196616 | tf_op jit(solution)/shard_map/ppermute | solution.py:49
  59.4 0.6 collective-permute-start.16
  60.0 3.8 %collective-permute-done.15 = f32[16,1024]{1,0:T(8,128)S(1)} collective-permute-done((f32[16,1024]{1,0:T(8,128)S(1)}, f32[16,1024]{1,0:T(8,128)S(1)}, u32[]{:S(2)}, u32[]{:S(2)}) %collective-permute-start.15) | collective-permute-done | bytes 65568 | tf_op jit(solution)/shard_map/ppermute | solution.py:49
  63.9 4.1 %collective-permute-start.18 = (f32[16,1024]{1,0:T(8,128)S(1)}, f32[16,1024]{1,0:T(8,128)S(1)}, u32[]{:S(2)}, u32[]{:S(2)}) collective-permute-start(f32[16,1024]{1,0:T(8,128)S(1)} %slice_add_fusion), channel_id=1, source_target_pairs={{0,24},{4,28},{8,16},{12,20},{16,8},{20,12},{24,0},{28,4},{1,25},{... | collective-permute-start | bytes 196616 | tf_op jit(solution)/shard_map/ppermute | solution.py:49
  68.0 0.6 collective-permute-start.19
  68.6 0.5 collective-permute-start.20
  69.1 3.5 %factor.1.state = f32[128,256]{1,0:T(8,128)S(1)} custom-call(f32[16,1024]{1,0:T(8,128)S(1)} %get-tuple-element.70.refs_0_, f32[32,1024]{1,0:T(8,128)S(1)} %collective-permute-done.17.refs_1_), custom_call_target="tpu_custom_call" | custom-call | tf_op jit(solution)/shard_map/factor/pallas_call | solution.py:431
  72.6 1.2 %collective-permute-done.19 = f32[16,1024]{1,0:T(8,128)S(1)} collective-permute-done((f32[16,1024]{1,0:T(8,128)S(1)}, f32[16,1024]{1,0:T(8,128)S(1)}, u32[]{:S(2)}, u32[]{:S(2)}) %collective-permute-start.19) | collective-permute-done | bytes 65568 | tf_op jit(solution)/shard_map/ppermute | solution.py:49
  73.8 1.6 %collective-permute-start.21 = (f32[16,1024]{1,0:T(8,128)S(1)}, f32[16,1024]{1,0:T(8,128)S(1)}, u32[]{:S(2)}, u32[]{:S(2)}) collective-permute-start(f32[16,1024]{1,0:T(8,128)S(1)} %add_add_fusion.2.token), channel_id=1, source_target_pairs={{0,2},{1,3},{2,0},{3,1},{4,6},{5,7},{6,4},{7,5},{8,10},{9,11},{10,... | collective-permute-start | bytes 196616 | tf_op jit(solution)/shard_map/ppermute | solution.py:49
  75.5 1.2 %collective-permute-start.22 = (f32[16,1024]{1,0:T(8,128)S(1)}, f32[16,1024]{1,0:T(8,128)S(1)}, u32[]{:S(2)}, u32[]{:S(2)}) collective-permute-start(f32[16,1024]{1,0:T(8,128)S(1)} %add_add_fusion.2.token), channel_id=1, source_target_pairs={{0,4},{4,0},{8,12},{12,8},{16,20},{20,16},{24,28},{28,24},{1,5},{5... | collective-permute-start | bytes 196616 | tf_op jit(solution)/shard_map/ppermute | solution.py:49
  76.7 0.7 collective-permute-start.23
  77.4 3.5 %load.1.refs_0_ = f32[2048,1024]{1,0:T(8,128)S(1)} custom-call(f32[2048,1024]{1,0:T(8,128)} %get-tuple-element.50.refs_1_.source, f32[16,1024]{1,0:T(8,128)S(1)} %add_add_fusion.2.token), custom_call_target="tpu_custom_call" | custom-call | tf_op jit(solution)/shard_map/load/pallas_call | solution.py:456
  80.9 0.9 %collective-permute-done.23 = f32[16,1024]{1,0:T(8,128)S(1)} collective-permute-done((f32[16,1024]{1,0:T(8,128)S(1)}, f32[16,1024]{1,0:T(8,128)S(1)}, u32[]{:S(2)}, u32[]{:S(2)}) %collective-permute-start.23) | collective-permute-done | bytes 65568 | tf_op jit(solution)/shard_map/ppermute | solution.py:49
  81.9 0.1 collective-permute-start.24
  82.0 1.1 %ortho.1 = (bf16[2048,256]{1,0:T(8,128)(2,1)S(1)}, f32[256,128]{1,0:T(8,128)S(1)}) custom-call(s32[4]{0:T(128)S(1)} %pad_add_fusion.refs_0_.who, f32[128,256]{1,0:T(8,128)S(1)} %factor.1.state, f32[256,128]{1,0:T(8,128)S(1)} %add_multiply_fusion.1.refs_2_.refs_0_, f32[256,128]{1,0:T(8,128)S(1)} %add_multiply_fusion.refs_3_.refs_1_, ...), custom_call_target="tpu_custom_call" | custom-call | tf_op jit(solution)/shard_map/ortho/pallas_call | solution.py:491
  83.2 0.4 collective-permute-done.24.right_there
  83.5 5.7 %finish.1 = (f32[2048,1024]{1,0:T(8,128)}, f32[256,128]{1,0:T(8,128)}, bf16[256,1024]{1,0:T(8,128)(2,1)}) custom-call(s32[4]{0:T(128)S(1)} %pad_add_fusion.refs_0_.who, f32[64,1024]{1,0:T(8,128)S(1)} %constant_dynamic-update-slice_fusion.right_here, f32[64,1024]{1,0:T(8,128)S(1)} %collective-permute-done.24.right_there, f32[128,256]{1,0:T(8,128)S(1)} %factor.1.state, ...), custom_call_target="tpu_custom_call" | custom-call | tf_op jit(solution)/shard_map/finish/pallas_call | solution.py:556
  (27 shorter events, 0.2 us)
Async XLA Ops:
  0.6 11.8 %copy-start = (f32[1024,128]{1,0:T(8,128)S(1)}, f32[1024,128]{1,0:T(8,128)}, u32[]{:S(2)}) copy-start(f32[1024,128]{1,0:T(8,128)} %basis.5) | copy-start | bytes 1572868
  15.8 11.4 %collective-permute-start.2 = (f32[256,128]{1,0:T(8,128)S(1)}, f32[256,128]{1,0:T(8,128)S(1)}, u32[]{:S(2)}, u32[]{:S(2)}) collective-permute-start(f32[256,128]{1,0:T(8,128)S(1)} %get-tuple-element.54), channel_id=1, source_target_pairs={{0,4},{4,0},{8,12},{12,8},{16,20},{20,16},{24,28},{28,24},{1,5},{5... | collective-permute-start | bytes 393224 | tf_op jit(solution)/shard_map/ppermute | solution.py:49
  18.8 9.2 %collective-permute-start = (f32[256,128]{1,0:T(8,128)S(1)}, f32[256,128]{1,0:T(8,128)S(1)}, u32[]{:S(2)}, u32[]{:S(2)}) collective-permute-start(f32[256,128]{1,0:T(8,128)S(1)} %get-tuple-element.52), channel_id=1, source_target_pairs={{0,12},{4,8},{8,4},{12,0},{16,28},{20,24},{24,20},{28,16},{1,13},{... | collective-permute-start | bytes 393224 | tf_op jit(solution)/shard_map/ppermute | solution.py:49
  20.3 7.6 %collective-permute-start.1 = (f32[256,128]{1,0:T(8,128)S(1)}, f32[256,128]{1,0:T(8,128)S(1)}, u32[]{:S(2)}, u32[]{:S(2)}) collective-permute-start(f32[256,128]{1,0:T(8,128)S(1)} %get-tuple-element.53), channel_id=1, source_target_pairs={{0,8},{4,12},{8,0},{12,4},{16,24},{20,28},{24,16},{28,20},{1,9},{5... | collective-permute-start | bytes 393224 | tf_op jit(solution)/shard_map/ppermute | solution.py:49
  20.3 10.3 %collective-permute-start.6 = (f32[256,128]{1,0:T(8,128)S(1)}, f32[256,128]{1,0:T(8,128)S(1)}, u32[]{:S(2)}, u32[]{:S(2)}) collective-permute-start(f32[256,128]{1,0:T(8,128)S(1)} %get-tuple-element.58), channel_id=1, source_target_pairs={{0,4},{4,0},{8,12},{12,8},{16,20},{20,16},{24,28},{28,24},{1,5},{5... | collective-permute-start | bytes 393224 | tf_op jit(solution)/shard_map/ppermute | solution.py:49
  22.3 10.5 %collective-permute-start.4 = (f32[256,128]{1,0:T(8,128)S(1)}, f32[256,128]{1,0:T(8,128)S(1)}, u32[]{:S(2)}, u32[]{:S(2)}) collective-permute-start(f32[256,128]{1,0:T(8,128)S(1)} %get-tuple-element.56), channel_id=1, source_target_pairs={{0,12},{4,8},{8,4},{12,0},{16,28},{20,24},{24,20},{28,16},{1,13},{... | collective-permute-start | bytes 393224 | tf_op jit(solution)/shard_map/ppermute | solution.py:49
  27.2 7.4 %collective-permute-start.5 = (f32[256,128]{1,0:T(8,128)S(1)}, f32[256,128]{1,0:T(8,128)S(1)}, u32[]{:S(2)}, u32[]{:S(2)}) collective-permute-start(f32[256,128]{1,0:T(8,128)S(1)} %get-tuple-element.57), channel_id=1, source_target_pairs={{0,8},{4,12},{8,0},{12,4},{16,24},{20,28},{24,16},{28,20},{1,9},{5... | collective-permute-start | bytes 393224 | tf_op jit(solution)/shard_map/ppermute | solution.py:49
  28.0 8.3 %collective-permute-start.3 = (f32[256,128]{1,0:T(8,128)S(1)}, f32[256,128]{1,0:T(8,128)S(1)}, u32[]{:S(2)}, u32[]{:S(2)}) collective-permute-start(f32[256,128]{1,0:T(8,128)S(1)} %add_add_fusion.1), channel_id=1, source_target_pairs={{0,16},{4,20},{8,24},{12,28},{16,0},{20,4},{24,8},{28,12},{1,17},{... | collective-permute-start | bytes 393224 | tf_op jit(solution)/shard_map/ppermute | solution.py:49
  34.6 8.0 %collective-permute-start.7 = (f32[256,128]{1,0:T(8,128)S(1)}, f32[256,128]{1,0:T(8,128)S(1)}, u32[]{:S(2)}, u32[]{:S(2)}) collective-permute-start(f32[256,128]{1,0:T(8,128)S(1)} %add_add_fusion), channel_id=1, source_target_pairs={{0,16},{4,20},{8,24},{12,28},{16,0},{20,4},{24,8},{28,12},{1,17},{... | collective-permute-start | bytes 393224 | tf_op jit(solution)/shard_map/ppermute | solution.py:49
  36.3 8.3 %collective-permute-start.11 = (f32[256,128]{1,0:T(8,128)S(1)}, f32[256,128]{1,0:T(8,128)S(1)}, u32[]{:S(2)}, u32[]{:S(2)}) collective-permute-start(f32[256,128]{1,0:T(8,128)S(1)} %add_multiply_fusion.1.refs_2_.refs_0_), channel_id=1, source_target_pairs={{0,4},{4,0},{8,12},{12,8},{16,20},{20,16},{24,28},{28,24},{1,5},{5... | collective-permute-start | bytes 393224 | tf_op jit(solution)/shard_map/ppermute | solution.py:49
  40.4 9.9 %collective-permute-start.12 = (f32[256,128]{1,0:T(8,128)S(1)}, f32[256,128]{1,0:T(8,128)S(1)}, u32[]{:S(2)}, u32[]{:S(2)}) collective-permute-start(f32[256,128]{1,0:T(8,128)S(1)} %add_multiply_fusion.1.refs_2_.refs_0_), channel_id=1, source_target_pairs={{0,8},{4,12},{8,0},{12,4},{16,24},{20,28},{24,16},{28,20},{1,9},{5... | collective-permute-start | bytes 393224 | tf_op jit(solution)/shard_map/ppermute | solution.py:49
  40.5 9.8 %collective-permute-start.13 = (f32[256,128]{1,0:T(8,128)S(1)}, f32[256,128]{1,0:T(8,128)S(1)}, u32[]{:S(2)}, u32[]{:S(2)}) collective-permute-start(f32[256,128]{1,0:T(8,128)S(1)} %add_multiply_fusion.1.refs_2_.refs_0_), channel_id=1, source_target_pairs={{0,12},{4,8},{8,4},{12,0},{16,28},{20,24},{24,20},{28,16},{1,13},{... | collective-permute-start | bytes 393224 | tf_op jit(solution)/shard_map/ppermute | solution.py:49
  42.6 9.4 %collective-permute-start.10 = (f32[256,128]{1,0:T(8,128)S(1)}, f32[256,128]{1,0:T(8,128)S(1)}, u32[]{:S(2)}, u32[]{:S(2)}) collective-permute-start(f32[256,128]{1,0:T(8,128)S(1)} %add_multiply_fusion.refs_3_.refs_1_), channel_id=1, source_target_pairs={{0,12},{4,8},{8,4},{12,0},{16,28},{20,24},{24,20},{28,16},{1,13},{... | collective-permute-start | bytes 393224 | tf_op jit(solution)/shard_map/ppermute | solution.py:49
  44.3 8.1 %collective-permute-start.8 = (f32[256,128]{1,0:T(8,128)S(1)}, f32[256,128]{1,0:T(8,128)S(1)}, u32[]{:S(2)}, u32[]{:S(2)}) collective-permute-start(f32[256,128]{1,0:T(8,128)S(1)} %add_multiply_fusion.refs_3_.refs_1_), channel_id=1, source_target_pairs={{0,4},{4,0},{8,12},{12,8},{16,20},{20,16},{24,28},{28,24},{1,5},{5... | collective-permute-start | bytes 393224 | tf_op jit(solution)/shard_map/ppermute | solution.py:49
  44.5 8.0 %collective-permute-start.9 = (f32[256,128]{1,0:T(8,128)S(1)}, f32[256,128]{1,0:T(8,128)S(1)}, u32[]{:S(2)}, u32[]{:S(2)}) collective-permute-start(f32[256,128]{1,0:T(8,128)S(1)} %add_multiply_fusion.refs_3_.refs_1_), channel_id=1, source_target_pairs={{0,8},{4,12},{8,0},{12,4},{16,24},{20,28},{24,16},{28,20},{1,9},{5... | collective-permute-start | bytes 393224 | tf_op jit(solution)/shard_map/ppermute | solution.py:49
  54.1 1.7 %collective-permute-start.14 = (f32[80,1024]{1,0:T(8,128)S(1)}, f32[80,1024]{1,0:T(8,128)S(1)}, u32[]{:S(2)}, u32[]{:S(2)}) collective-permute-start(f32[80,1024]{1,0:T(8,128)S(1)} %get-tuple-element.65), channel_id=1, source_target_pairs={{0,1},{1,0},{2,3},{3,2},{4,5},{5,4},{6,7},{7,6},{8,9},{9,8},{10,11... | collective-permute-start | bytes 983048 | tf_op jit(solution)/shard_map/ppermute | solution.py:49
  56.4 7.4 %collective-permute-start.17 = (f32[32,1024]{1,0:T(8,128)S(1)}, f32[32,1024]{1,0:T(8,128)S(1)}, u32[]{:S(2)}, u32[]{:S(2)}) collective-permute-start(f32[32,1024]{1,0:T(8,128)S(1)} %get-tuple-element.69), channel_id=1, source_target_pairs={{0,2},{1,3},{2,0},{3,1},{4,6},{5,7},{6,4},{7,5},{8,10},{9,11},{10,... | collective-permute-start | bytes 393224 | tf_op jit(solution)/shard_map/ppermute | solution.py:49
  58.0 5.8 %collective-permute-start.15 = (f32[16,1024]{1,0:T(8,128)S(1)}, f32[16,1024]{1,0:T(8,128)S(1)}, u32[]{:S(2)}, u32[]{:S(2)}) collective-permute-start(f32[16,1024]{1,0:T(8,128)S(1)} %get-tuple-element.67), channel_id=1, source_target_pairs={{0,6},{1,7},{2,4},{3,5},{4,2},{5,3},{6,0},{7,1},{8,14},{9,15},{10,... | collective-permute-start | bytes 196616 | tf_op jit(solution)/shard_map/ppermute | solution.py:49
  59.4 4.4 %collective-permute-start.16 = (f32[16,1024]{1,0:T(8,128)S(1)}, f32[16,1024]{1,0:T(8,128)S(1)}, u32[]{:S(2)}, u32[]{:S(2)}) collective-permute-start(f32[16,1024]{1,0:T(8,128)S(1)} %get-tuple-element.68), channel_id=1, source_target_pairs={{0,4},{4,0},{8,12},{12,8},{16,20},{20,16},{24,28},{28,24},{1,5},{5... | collective-permute-start | bytes 196616 | tf_op jit(solution)/shard_map/ppermute | solution.py:49
  63.9 8.8 %collective-permute-start.18 = (f32[16,1024]{1,0:T(8,128)S(1)}, f32[16,1024]{1,0:T(8,128)S(1)}, u32[]{:S(2)}, u32[]{:S(2)}) collective-permute-start(f32[16,1024]{1,0:T(8,128)S(1)} %slice_add_fusion), channel_id=1, source_target_pairs={{0,24},{4,28},{8,16},{12,20},{16,8},{20,12},{24,0},{28,4},{1,25},{... | collective-permute-start | bytes 196616 | tf_op jit(solution)/shard_map/ppermute | solution.py:49
  68.0 5.9 %collective-permute-start.19 = (f32[16,1024]{1,0:T(8,128)S(1)}, f32[16,1024]{1,0:T(8,128)S(1)}, u32[]{:S(2)}, u32[]{:S(2)}) collective-permute-start(f32[16,1024]{1,0:T(8,128)S(1)} %slice_add_fusion), channel_id=1, source_target_pairs={{0,16},{4,20},{8,24},{12,28},{16,0},{20,4},{24,8},{28,12},{1,17},{... | collective-permute-start | bytes 196616 | tf_op jit(solution)/shard_map/ppermute | solution.py:49
  68.6 5.2 %collective-permute-start.20 = (f32[16,1024]{1,0:T(8,128)S(1)}, f32[16,1024]{1,0:T(8,128)S(1)}, u32[]{:S(2)}, u32[]{:S(2)}) collective-permute-start(f32[16,1024]{1,0:T(8,128)S(1)} %slice_add_fusion), channel_id=1, source_target_pairs={{0,8},{4,12},{8,0},{12,4},{16,24},{20,28},{24,16},{28,20},{1,9},{5... | collective-permute-start | bytes 196616 | tf_op jit(solution)/shard_map/ppermute | solution.py:49
  73.8 7.1 %collective-permute-start.21 = (f32[16,1024]{1,0:T(8,128)S(1)}, f32[16,1024]{1,0:T(8,128)S(1)}, u32[]{:S(2)}, u32[]{:S(2)}) collective-permute-start(f32[16,1024]{1,0:T(8,128)S(1)} %add_add_fusion.2.token), channel_id=1, source_target_pairs={{0,2},{1,3},{2,0},{3,1},{4,6},{5,7},{6,4},{7,5},{8,10},{9,11},{10,... | collective-permute-start | bytes 196616 | tf_op jit(solution)/shard_map/ppermute | solution.py:49
  75.5 5.5 %collective-permute-start.22 = (f32[16,1024]{1,0:T(8,128)S(1)}, f32[16,1024]{1,0:T(8,128)S(1)}, u32[]{:S(2)}, u32[]{:S(2)}) collective-permute-start(f32[16,1024]{1,0:T(8,128)S(1)} %add_add_fusion.2.token), channel_id=1, source_target_pairs={{0,4},{4,0},{8,12},{12,8},{16,20},{20,16},{24,28},{28,24},{1,5},{5... | collective-permute-start | bytes 196616 | tf_op jit(solution)/shard_map/ppermute | solution.py:49
  76.7 5.2 %collective-permute-start.23 = (f32[16,1024]{1,0:T(8,128)S(1)}, f32[16,1024]{1,0:T(8,128)S(1)}, u32[]{:S(2)}, u32[]{:S(2)}) collective-permute-start(f32[16,1024]{1,0:T(8,128)S(1)} %add_add_fusion.2.token), channel_id=1, source_target_pairs={{0,6},{1,7},{2,4},{3,5},{4,2},{5,3},{6,0},{7,1},{8,14},{9,15},{10,... | collective-permute-start | bytes 196616 | tf_op jit(solution)/shard_map/ppermute | solution.py:49
  81.9 1.6 %collective-permute-start.24 = (f32[64,1024]{1,0:T(8,128)S(1)}, f32[64,1024]{1,0:T(8,128)S(1)}, u32[]{:S(2)}, u32[]{:S(2)}) collective-permute-start(f32[64,1024]{1,0:T(8,128)S(1)} %constant_dynamic-update-slice_fusion.right_here), channel_id=1, source_target_pairs={{0,1},{1,0},{2,3},{3,2},{4,5},{5,4},{6,7},{7,6},{8,9},{9,8},{10,11... | collective-permute-start | bytes 786440 | tf_op jit(solution)/shard_map/ppermute | solution.py:49

commit v6 on v5

--- a/solution.py
+++ b/solution.py
@@ -91,7 +91,7 @@
     return wide[:, :rank] + wide[:, rank:] + dot(low, both[:, :rank], 1, 0)
 
 
-CHUNKS = 4
+CHUNKS = 2
 
 
 def first_blend_kernel(group, offsets, later, acts, grads, momentum, basis, *refs):
@@ -100,7 +100,7 @@
     momentum_later = refs[3 : 3 + extra]
     sketches = refs[3 + extra : 3 + extra + PARTS * count]
     refs = refs[3 + extra + PARTS * count :]
-    acts_held, values, both, acts_sem, grads_sem, momentum_sem, later_sem, out_sem = refs
+    acts_held, values, basis_held, both, acts_sem, grads_sem, momentum_sem, later_sem, out_sem, basis_sem = refs
     low = lax.axis_index("dp") & (group - 1)
     tokens, block = acts_held.shape[1:]
     rank = basis.shape[1]
@@ -141,9 +141,8 @@
     for c in range(CHUNKS):
         acts_copy(0, c).start()
         grads_copy(c).start()
-    basis_high, basis_low = split(basis[...])
-    both[:, :rank] = basis_high
-    both[:, rank:] = basis_low
+    basis_copy = pltpu.make_async_copy(basis, basis_held, basis_sem)
+    basis_copy.start()
     columns = [slice(p * part, (p + 1) * part) for p in range(PARTS)]
     for i in range(count):
         if i == 0:
@@ -173,6 +172,11 @@
             gradient = sums[p] if i == 0 else dot(acts_held[i, :, cols], held[...], 0, 0)
             values[rows, :] = values[rows, :] + gradient
             out_copy(i * PARTS + p).start()
+        if i == 0:
+            basis_copy.wait()
+            basis_high, basis_low = split(basis_held[...])
+            both[:, :rank] = basis_high
+            both[:, rank:] = basis_low
         for index in range(i * PARTS, (i + 1) * PARTS):
             sketches[index][...] = sketch_of(values[index * part : (index + 1) * part, :], both[...], rank)
     for index in range(count * PARTS):
@@ -196,18 +200,20 @@
     outs += [pltpu.VMEM((block // PARTS, rank), jnp.float32)] * (PARTS * count)
     out = pl.pallas_call(
         functools.partial(first_blend_kernel, group, offsets, later),
-        in_specs=[ANY, ANY, ANY, VMEM],
+        in_specs=[ANY, ANY, ANY, ANY],
         out_specs=[ANY] + [VMEM] * (len(outs) - 1),
         out_shape=outs,
         scratch_shapes=[
             pltpu.VMEM((count, tokens, block), jnp.bfloat16),
             pltpu.VMEM((count * block, kv), jnp.float32),
+            pltpu.VMEM((kv, rank), jnp.float32),
             pltpu.VMEM((kv, 2 * rank), jnp.bfloat16),
             pltpu.SemaphoreType.DMA((count, CHUNKS)),
             pltpu.SemaphoreType.DMA((CHUNKS,)),
             pltpu.SemaphoreType.DMA((count,)),
             pltpu.SemaphoreType.DMA((extra, 2)),
             pltpu.SemaphoreType.DMA((count * PARTS,)),
+            pltpu.SemaphoreType.DMA,
         ],
         compiler_params=params(FIRST_MIB),
         name="first_blend",
@@ -506,7 +512,7 @@
 
 
 def finish_kernel(group, places, scale, who, right_here, right_there, state, ortho, own_ortho, *refs):
-    blended, new_momentum, new_basis, update, right, values, coeff_high, coeff_low, sem = refs
+    blended, new_momentum, new_basis, update, right, values, coeff_high, coeff_low, basis_held, update_held, sem = refs
     rank, kv = right.shape
     half = rank // 2
     core = who[2] & 1
@@ -539,12 +545,16 @@
 
         @pl.when(who[2] == j)
         def _(j=j):
-            new_basis[...] = normed[:, j * count : (j + 1) * count].T
-
+            basis_held[...] = normed[:, j * count : (j + 1) * count].T
+
+    copies.append(pltpu.make_async_copy(basis_held, new_basis, sem.at[len(copies)]))
+    copies[-1].start()
     rows_high, rows_low = split(own_ortho[...])
     high, low = split(normed)
     product = dot(jnp.concatenate([rows_high, rows_low], 1), jnp.concatenate([high, high], 0), 1, 0)
-    update[...] = (scale * (product + dot(rows_high, low, 1, 0))).astype(update.dtype)
+    update_held[...] = (scale * (product + dot(rows_high, low, 1, 0))).astype(update.dtype)
+    copies.append(pltpu.make_async_copy(update_held, update, sem.at[len(copies)]))
+    copies[-1].start()
     for copy in copies:
         copy.wait()
 
@@ -556,7 +566,7 @@
     return pl.pallas_call(
         functools.partial(finish_kernel, group, places, scale),
         in_specs=[SMEM] + [VMEM] * 6,
-        out_specs=[ANY, VMEM, VMEM],
+        out_specs=[ANY, ANY, ANY],
         out_shape=[
             jax.ShapeDtypeStruct((rows, kv), jnp.float32),
             jax.ShapeDtypeStruct((kv // n_rows, rank), jnp.float32),
@@ -567,7 +577,9 @@
             pltpu.VMEM((rows, kv), jnp.float32),
             pltpu.VMEM((2 * rank, kv), jnp.bfloat16),
             pltpu.VMEM((rank, kv), jnp.bfloat16),
-            pltpu.SemaphoreType.DMA((group * CUTS,)),
+            pltpu.VMEM((kv // n_rows, rank), jnp.float32),
+            pltpu.VMEM(own_ortho.shape[:1] + (kv,), jnp.bfloat16),
+            pltpu.SemaphoreType.DMA((group * CUTS + 2,)),
         ],
         compiler_params=params(32),
         name="finish",

time: 89.6 us -> 87.7 us (0.979)
  Pallas kernels: 40.3 us -> 38.5 us
    pallas_call x1, Pallas kernels: 11.7 us -> 10.6 us  [first_blend(): pl.pallas_call(functools.partial(first_blend_kernel, group, offsets, late...]
  transfers between devices with their start and end apart: 25 -> 25, of which waited for: 10 -> 10; matrix products, arithmetic and copies ran while one was open for 0% -> 0% of each run, Pallas kernels for 19% -> 20%
where the time goes in v6:
time: 87.7 us; the launch traced here: 87.6 us
  Pallas kernels  38.5 us (44%)
  starting transfers between devices  34.9 us (40%)
  waiting for transfers between devices  12.9 us (15%)
  between operations  1.04 us (1%)
    ppermute x25, starting transfers between devices, swap(): return lax.ppermute(value, axes, pairs)  34.9 us
    ppermute x25, waiting for transfers between devices, swap(): return lax.ppermute(value, axes, pairs)  12.9 us
    pallas_call x1, Pallas kernels, first_blend(): pl.pallas_call(functools.partial(first_blend_kernel, group, offsets, late...  10.6 us
    pallas_call x3, Pallas kernels, right_terms(): pl.pallas_call(functools.partial(right_kernel, pieces, first, last, scale...  7.36 us
    pallas_call x2, Pallas kernels, blend(): pl.pallas_call(functools.partial(blend_kernel, jobs, len(momentum)), in_s...  6.72 us
    pallas_call x1, Pallas kernels, finish(): pl.pallas_call(functools.partial(finish_kernel, group, places, scale), in...  5.1 us
    pallas_call x1, Pallas kernels, factor(): pl.pallas_call(functools.partial(factor_kernel, panels, grams, block), in...  3.52 us
    pallas_call x1, Pallas kernels, load(): pl.pallas_call(load_kernel, in_specs=[ANY, ANY], out_specs=VMEM, out_shap...  3.5 us
  transfers between devices with their start and end apart: 25, of which 10 were waited for; matrix products, arithmetic and copies ran while one was open for 0% of the time, Pallas kernels for 20%

profile of v6, /device:TPU:0, one launch (start us, length us, event | category | flops | bytes accessed | tf_op | source)
XLA Modules:
  0.0 87.6 jit_solution(6065514621047574802)
XLA Ops:
  0.6 10.6 %first_blend.1 = (f32[2048,1024]{1,0:T(8,128)}, bf16[2048,1024]{1,0:T(8,128)(2,1)S(1)}, bf16[2,2048,512]{2,1,0:T(8,128)(2,1)S(1)}, f32[512,1024]{1,0:T(8,128)S(1...) custom-call(bf16[2048,2048]{1,0:T(8,128)(2,1)} %acts.1, ...), custom_call_target="tpu_custom_call" | custom-call | tf_op jit(solution)/shard_map/first_blend/pallas_call | solution.py:201
  11.2 3.4 %blend.2 = (f32[2048,1024]{1,0:T(8,128)}, f32[256,128]{1,0:T(8,128)S(1)}, f32[256,128]{1,0:T(8,128)S(1)}) custom-call(bf16[2,2048,512]{2,1,0:T(8,128)(2,1)S(1)} %get-tuple-element.44.acts, bf16[2048,1024]{1,0:T(8,128)(2,1)S(1)} %get-tuple-element.45.grads, f32[1024,128]{1,0:T(8,128)S(1)} %copy-done, ...), custom_call_target="tpu_custom_call", output_to_operand_aliasing={{0}: (5, {})} | custom-call | tf_op jit(solution)/shard_map/blend/pallas_call | solution.py:251
  14.6 3.0 %collective-permute-start.2 = (f32[256,128]{1,0:T(8,128)S(1)}, f32[256,128]{1,0:T(8,128)S(1)}, u32[]{:S(2)}, u32[]{:S(2)}) collective-permute-start(f32[256,128]{1,0:T(8,128)S(1)} %get-tuple-element.54), channel_id=1, source_target_pairs={{0,4},{4,0},{8,12},{12,8},{16,20},{20,16},{24,28},{28,24},{1,5},{5... | collective-permute-start | bytes 393224 | tf_op jit(solution)/shard_map/ppermute | solution.py:49
  17.6 1.5 %collective-permute-start = (f32[256,128]{1,0:T(8,128)S(1)}, f32[256,128]{1,0:T(8,128)S(1)}, u32[]{:S(2)}, u32[]{:S(2)}) collective-permute-start(f32[256,128]{1,0:T(8,128)S(1)} %get-tuple-element.52), channel_id=1, source_target_pairs={{0,12},{4,8},{8,4},{12,0},{16,28},{20,24},{24,20},{28,16},{1,13},{... | collective-permute-start | bytes 393224 | tf_op jit(solution)/shard_map/ppermute | solution.py:49
  19.1 0.0 collective-permute-start.1
  19.2 1.9 %collective-permute-start.6 = (f32[256,128]{1,0:T(8,128)S(1)}, f32[256,128]{1,0:T(8,128)S(1)}, u32[]{:S(2)}, u32[]{:S(2)}) collective-permute-start(f32[256,128]{1,0:T(8,128)S(1)} %get-tuple-element.58), channel_id=1, source_target_pairs={{0,4},{4,0},{8,12},{12,8},{16,20},{20,16},{24,28},{28,24},{1,5},{5... | collective-permute-start | bytes 393224 | tf_op jit(solution)/shard_map/ppermute | solution.py:49
  21.1 1.5 %collective-permute-start.4 = (f32[256,128]{1,0:T(8,128)S(1)}, f32[256,128]{1,0:T(8,128)S(1)}, u32[]{:S(2)}, u32[]{:S(2)}) collective-permute-start(f32[256,128]{1,0:T(8,128)S(1)} %get-tuple-element.56), channel_id=1, source_target_pairs={{0,12},{4,8},{8,4},{12,0},{16,28},{20,24},{24,20},{28,16},{1,13},{... | collective-permute-start | bytes 393224 | tf_op jit(solution)/shard_map/ppermute | solution.py:49
  22.6 3.4 %blend.3 = (f32[2048,1024]{1,0:T(8,128)}, f32[256,128]{1,0:T(8,128)S(1)}, f32[256,128]{1,0:T(8,128)S(1)}) custom-call(bf16[2,2048,512]{2,1,0:T(8,128)(2,1)S(1)} %get-tuple-element.44.acts, bf16[2048,1024]{1,0:T(8,128)(2,1)S(1)} %get-tuple-element.45.grads, f32[1024,128]{1,0:T(8,128)S(1)} %copy-done, ...), custom_call_target="tpu_custom_call", output_to_operand_aliasing={{0}: (5, {})} | custom-call | tf_op jit(solution)/shard_map/blend/pallas_call | solution.py:251
  26.0 0.0 collective-permute-done.2
  26.0 0.8 collective-permute-start.5
  26.8 2.7 %collective-permute-start.3 = (f32[256,128]{1,0:T(8,128)S(1)}, f32[256,128]{1,0:T(8,128)S(1)}, u32[]{:S(2)}, u32[]{:S(2)}) collective-permute-start(f32[256,128]{1,0:T(8,128)S(1)} %add_add_fusion.1), channel_id=1, source_target_pairs={{0,16},{4,20},{8,24},{12,28},{16,0},{20,4},{24,8},{28,12},{1,17},{... | collective-permute-start | bytes 393224 | tf_op jit(solution)/shard_map/ppermute | solution.py:49
  29.5 2.1 %collective-permute-done.4 = f32[256,128]{1,0:T(8,128)S(1)} collective-permute-done((f32[256,128]{1,0:T(8,128)S(1)}, f32[256,128]{1,0:T(8,128)S(1)}, u32[]{:S(2)}, u32[]{:S(2)}) %collective-permute-start.4) | collective-permute-done | bytes 131104 | tf_op jit(solution)/shard_map/ppermute | solution.py:49
  31.6 1.8 %collective-permute-done.5 = f32[256,128]{1,0:T(8,128)S(1)} collective-permute-done((f32[256,128]{1,0:T(8,128)S(1)}, f32[256,128]{1,0:T(8,128)S(1)}, u32[]{:S(2)}, u32[]{:S(2)}) %collective-permute-start.5) | collective-permute-done | bytes 131104 | tf_op jit(solution)/shard_map/ppermute | solution.py:49
  33.4 1.7 %collective-permute-start.7 = (f32[256,128]{1,0:T(8,128)S(1)}, f32[256,128]{1,0:T(8,128)S(1)}, u32[]{:S(2)}, u32[]{:S(2)}) collective-permute-start(f32[256,128]{1,0:T(8,128)S(1)} %add_add_fusion), channel_id=1, source_target_pairs={{0,16},{4,20},{8,24},{12,28},{16,0},{20,4},{24,8},{28,12},{1,17},{... | collective-permute-start | bytes 393224 | tf_op jit(solution)/shard_map/ppermute | solution.py:49
  35.1 4.1 %collective-permute-start.11 = (f32[256,128]{1,0:T(8,128)S(1)}, f32[256,128]{1,0:T(8,128)S(1)}, u32[]{:S(2)}, u32[]{:S(2)}) collective-permute-start(f32[256,128]{1,0:T(8,128)S(1)} %add_multiply_fusion.1.refs_2_.refs_0_), channel_id=1, source_target_pairs={{0,4},{4,0},{8,12},{12,8},{16,20},{20,16},{24,28},{28,24},{1,5},{5... | collective-permute-start | bytes 393224 | tf_op jit(solution)/shard_map/ppermute | solution.py:49
  39.2 0.1 collective-permute-start.12
  39.3 1.4 %collective-permute-start.13 = (f32[256,128]{1,0:T(8,128)S(1)}, f32[256,128]{1,0:T(8,128)S(1)}, u32[]{:S(2)}, u32[]{:S(2)}) collective-permute-start(f32[256,128]{1,0:T(8,128)S(1)} %add_multiply_fusion.1.refs_2_.refs_0_), channel_id=1, source_target_pairs={{0,12},{4,8},{8,4},{12,0},{16,28},{20,24},{24,20},{28,16},{1,13},{... | collective-permute-start | bytes 393224 | tf_op jit(solution)/shard_map/ppermute | solution.py:49
  40.8 0.7 collective-permute-done.7
  41.5 1.7 %collective-permute-start.10 = (f32[256,128]{1,0:T(8,128)S(1)}, f32[256,128]{1,0:T(8,128)S(1)}, u32[]{:S(2)}, u32[]{:S(2)}) collective-permute-start(f32[256,128]{1,0:T(8,128)S(1)} %add_multiply_fusion.refs_3_.refs_1_), channel_id=1, source_target_pairs={{0,12},{4,8},{8,4},{12,0},{16,28},{20,24},{24,20},{28,16},{1,13},{... | collective-permute-start | bytes 393224 | tf_op jit(solution)/shard_map/ppermute | solution.py:49
  43.2 0.2 collective-permute-start.8
  43.4 1.6 %collective-permute-start.9 = (f32[256,128]{1,0:T(8,128)S(1)}, f32[256,128]{1,0:T(8,128)S(1)}, u32[]{:S(2)}, u32[]{:S(2)}) collective-permute-start(f32[256,128]{1,0:T(8,128)S(1)} %add_multiply_fusion.refs_3_.refs_1_), channel_id=1, source_target_pairs={{0,8},{4,12},{8,0},{12,4},{16,24},{20,28},{24,16},{28,20},{1,9},{5... | collective-permute-start | bytes 393224 | tf_op jit(solution)/shard_map/ppermute | solution.py:49
  45.0 0.1 pad_add_fusion.refs_0_.who
  45.1 4.0 %right_terms.3 = (f32[128,1024]{1,0:T(8,128)S(1)}, f32[128,128]{1,0:T(8,128)S(1)}, f32[2048,1024]{1,0:T(8,128)S(1)}) custom-call(s32[4]{0:T(128)S(1)} %pad_add_fusion.refs_0_.who, f32[2048,1024]{1,0:T(8,128)} %get-tuple-element.50.refs_1_.source, f32[256,128]{1,0:T(8,128)S(1)} %add_multiply_fusion.1.refs_2_.refs_0_, ...), custom_call_target="tpu_custom_call" | custom-call | tf_op jit(solution)/shard_map/right_terms/pallas_call | solution.py:347
  49.1 1.7 %right_terms.4 = (f32[128,1024]{1,0:T(8,128)S(1)}, f32[128,128]{1,0:T(8,128)S(1)}) custom-call(s32[4]{0:T(128)S(1)} %pad_add_fusion.refs_0_.who, f32[2048,1024]{1,0:T(8,128)S(1)} %get-tuple-element.59.refs_1_, f32[256,128]{1,0:T(8,128)S(1)} %collective-permute-done.11.refs_2_, f32[256,128]{1,0:T(8,128)S(1)} %collective-permute-done.12.refs_3_.refs_4_, ...), custom_call_target="tpu_custom_call" | custom-call | tf_op jit(solution)/shard_map/right_terms/pallas_call | solution.py:347
  50.9 0.4 collective-permute-done.8.refs_2_.refs_3_
  51.3 0.1 collective-permute-done.9.refs_3_.refs_5_
  51.3 1.6 %right_terms.5 = (f32[80,1024]{1,0:T(8,128)S(1)}, f32[80,1024]{1,0:T(8,128)S(1)}) custom-call(s32[4]{0:T(128)S(1)} %pad_add_fusion.refs_0_.who, f32[2048,1024]{1,0:T(8,128)S(1)} %get-tuple-element.59.refs_1_, f32[256,128]{1,0:T(8,128)S(1)} %collective-permute-done.8.refs_2_.refs_3_, f32[256,128]{1,0:T(8,128)S(1)} %collective-permute-done.9.refs_3_.refs_5_, ...), custom_call_target="tpu_custom_call" | custom-call | tf_op jit(solution)/shard_map/right_terms/pallas_call | solution.py:347
  53.0 0.1 collective-permute-start.14
  53.1 1.6 %collective-permute-done.14.arrived = f32[80,1024]{1,0:T(8,128)S(1)} collective-permute-done((f32[80,1024]{1,0:T(8,128)S(1)}, f32[80,1024]{1,0:T(8,128)S(1)}, u32[]{:S(2)}, u32[]{:S(2)}) %collective-permute-start.14) | collective-permute-done | bytes 327712 | tf_op jit(solution)/shard_map/ppermute | solution.py:49
  54.7 0.6 cut.1
  55.3 1.6 %collective-permute-start.17 = (f32[32,1024]{1,0:T(8,128)S(1)}, f32[32,1024]{1,0:T(8,128)S(1)}, u32[]{:S(2)}, u32[]{:S(2)}) collective-permute-start(f32[32,1024]{1,0:T(8,128)S(1)} %get-tuple-element.69), channel_id=1, source_target_pairs={{0,2},{1,3},{2,0},{3,1},{4,6},{5,7},{6,4},{7,5},{8,10},{9,11},{10,... | collective-permute-start | bytes 393224 | tf_op jit(solution)/shard_map/ppermute | solution.py:49
  56.9 1.4 %collective-permute-start.15 = (f32[16,1024]{1,0:T(8,128)S(1)}, f32[16,1024]{1,0:T(8,128)S(1)}, u32[]{:S(2)}, u32[]{:S(2)}) collective-permute-start(f32[16,1024]{1,0:T(8,128)S(1)} %get-tuple-element.67), channel_id=1, source_target_pairs={{0,6},{1,7},{2,4},{3,5},{4,2},{5,3},{6,0},{7,1},{8,14},{9,15},{10,... | collective-permute-start | bytes 196616 | tf_op jit(solution)/shard_map/ppermute | solution.py:49
  58.2 0.6 collective-permute-start.16
  58.8 3.8 %collective-permute-done.15 = f32[16,1024]{1,0:T(8,128)S(1)} collective-permute-done((f32[16,1024]{1,0:T(8,128)S(1)}, f32[16,1024]{1,0:T(8,128)S(1)}, u32[]{:S(2)}, u32[]{:S(2)}) %collective-permute-start.15) | collective-permute-done | bytes 65568 | tf_op jit(solution)/shard_map/ppermute | solution.py:49
  62.7 4.2 %collective-permute-start.18 = (f32[16,1024]{1,0:T(8,128)S(1)}, f32[16,1024]{1,0:T(8,128)S(1)}, u32[]{:S(2)}, u32[]{:S(2)}) collective-permute-start(f32[16,1024]{1,0:T(8,128)S(1)} %slice_add_fusion), channel_id=1, source_target_pairs={{0,24},{4,28},{8,16},{12,20},{16,8},{20,12},{24,0},{28,4},{1,25},{... | collective-permute-start | bytes 196616 | tf_op jit(solution)/shard_map/ppermute | solution.py:49
  66.9 0.6 collective-permute-start.19
  67.5 0.5 collective-permute-start.20
  68.0 3.5 %factor.1.state = f32[128,256]{1,0:T(8,128)S(1)} custom-call(f32[16,1024]{1,0:T(8,128)S(1)} %get-tuple-element.70.refs_0_, f32[32,1024]{1,0:T(8,128)S(1)} %collective-permute-done.17.refs_1_), custom_call_target="tpu_custom_call" | custom-call | tf_op jit(solution)/shard_map/factor/pallas_call | solution.py:437
  71.5 1.2 %collective-permute-done.19 = f32[16,1024]{1,0:T(8,128)S(1)} collective-permute-done((f32[16,1024]{1,0:T(8,128)S(1)}, f32[16,1024]{1,0:T(8,128)S(1)}, u32[]{:S(2)}, u32[]{:S(2)}) %collective-permute-start.19) | collective-permute-done | bytes 65568 | tf_op jit(solution)/shard_map/ppermute | solution.py:49
  72.8 1.5 %collective-permute-start.21 = (f32[16,1024]{1,0:T(8,128)S(1)}, f32[16,1024]{1,0:T(8,128)S(1)}, u32[]{:S(2)}, u32[]{:S(2)}) collective-permute-start(f32[16,1024]{1,0:T(8,128)S(1)} %add_add_fusion.2.token), channel_id=1, source_target_pairs={{0,2},{1,3},{2,0},{3,1},{4,6},{5,7},{6,4},{7,5},{8,10},{9,11},{10,... | collective-permute-start | bytes 196616 | tf_op jit(solution)/shard_map/ppermute | solution.py:49
  74.2 1.2 %collective-permute-start.22 = (f32[16,1024]{1,0:T(8,128)S(1)}, f32[16,1024]{1,0:T(8,128)S(1)}, u32[]{:S(2)}, u32[]{:S(2)}) collective-permute-start(f32[16,1024]{1,0:T(8,128)S(1)} %add_add_fusion.2.token), channel_id=1, source_target_pairs={{0,4},{4,0},{8,12},{12,8},{16,20},{20,16},{24,28},{28,24},{1,5},{5... | collective-permute-start | bytes 196616 | tf_op jit(solution)/shard_map/ppermute | solution.py:49
  75.4 0.9 collective-permute-start.23
  76.3 3.5 %load.1.refs_0_ = f32[2048,1024]{1,0:T(8,128)S(1)} custom-call(f32[2048,1024]{1,0:T(8,128)} %get-tuple-element.50.refs_1_.source, f32[16,1024]{1,0:T(8,128)S(1)} %add_add_fusion.2.token), custom_call_target="tpu_custom_call" | custom-call | tf_op jit(solution)/shard_map/load/pallas_call | solution.py:462
  79.8 0.8 collective-permute-done.23
  80.7 0.1 collective-permute-start.24
  80.8 1.1 %ortho.1 = (bf16[2048,256]{1,0:T(8,128)(2,1)S(1)}, f32[256,128]{1,0:T(8,128)S(1)}) custom-call(s32[4]{0:T(128)S(1)} %pad_add_fusion.refs_0_.who, f32[128,256]{1,0:T(8,128)S(1)} %factor.1.state, f32[256,128]{1,0:T(8,128)S(1)} %add_multiply_fusion.1.refs_2_.refs_0_, f32[256,128]{1,0:T(8,128)S(1)} %add_multiply_fusion.refs_3_.refs_1_, ...), custom_call_target="tpu_custom_call" | custom-call | tf_op jit(solution)/shard_map/ortho/pallas_call | solution.py:497
  81.9 0.4 collective-permute-done.24.right_there
  82.3 5.1 %finish.1 = (f32[2048,1024]{1,0:T(8,128)}, f32[256,128]{1,0:T(8,128)}, bf16[256,1024]{1,0:T(8,128)(2,1)}) custom-call(s32[4]{0:T(128)S(1)} %pad_add_fusion.refs_0_.who, f32[64,1024]{1,0:T(8,128)S(1)} %constant_dynamic-update-slice_fusion.right_here, f32[64,1024]{1,0:T(8,128)S(1)} %collective-permute-done.24.right_there, f32[128,256]{1,0:T(8,128)S(1)} %factor.1.state, ...), custom_call_target="tpu_custom_call" | custom-call | tf_op jit(solution)/shard_map/finish/pallas_call | solution.py:566
  (27 shorter events, 0.2 us)
Async XLA Ops:
  0.6 10.6 %copy-start = (f32[1024,128]{1,0:T(8,128)S(1)}, f32[1024,128]{1,0:T(8,128)}, u32[]{:S(2)}) copy-start(f32[1024,128]{1,0:T(8,128)} %basis.5) | copy-start | bytes 1572868
  14.6 11.4 %collective-permute-start.2 = (f32[256,128]{1,0:T(8,128)S(1)}, f32[256,128]{1,0:T(8,128)S(1)}, u32[]{:S(2)}, u32[]{:S(2)}) collective-permute-start(f32[256,128]{1,0:T(8,128)S(1)} %get-tuple-element.54), channel_id=1, source_target_pairs={{0,4},{4,0},{8,12},{12,8},{16,20},{20,16},{24,28},{28,24},{1,5},{5... | collective-permute-start | bytes 393224 | tf_op jit(solution)/shard_map/ppermute | solution.py:49
  17.6 9.2 %collective-permute-start = (f32[256,128]{1,0:T(8,128)S(1)}, f32[256,128]{1,0:T(8,128)S(1)}, u32[]{:S(2)}, u32[]{:S(2)}) collective-permute-start(f32[256,128]{1,0:T(8,128)S(1)} %get-tuple-element.52), channel_id=1, source_target_pairs={{0,12},{4,8},{8,4},{12,0},{16,28},{20,24},{24,20},{28,16},{1,13},{... | collective-permute-start | bytes 393224 | tf_op jit(solution)/shard_map/ppermute | solution.py:49
  19.1 7.6 %collective-permute-start.1 = (f32[256,128]{1,0:T(8,128)S(1)}, f32[256,128]{1,0:T(8,128)S(1)}, u32[]{:S(2)}, u32[]{:S(2)}) collective-permute-start(f32[256,128]{1,0:T(8,128)S(1)} %get-tuple-element.53), channel_id=1, source_target_pairs={{0,8},{4,12},{8,0},{12,4},{16,24},{20,28},{24,16},{28,20},{1,9},{5... | collective-permute-start | bytes 393224 | tf_op jit(solution)/shard_map/ppermute | solution.py:49
  19.2 10.3 %collective-permute-start.6 = (f32[256,128]{1,0:T(8,128)S(1)}, f32[256,128]{1,0:T(8,128)S(1)}, u32[]{:S(2)}, u32[]{:S(2)}) collective-permute-start(f32[256,128]{1,0:T(8,128)S(1)} %get-tuple-element.58), channel_id=1, source_target_pairs={{0,4},{4,0},{8,12},{12,8},{16,20},{20,16},{24,28},{28,24},{1,5},{5... | collective-permute-start | bytes 393224 | tf_op jit(solution)/shard_map/ppermute | solution.py:49
  21.1 10.5 %collective-permute-start.4 = (f32[256,128]{1,0:T(8,128)S(1)}, f32[256,128]{1,0:T(8,128)S(1)}, u32[]{:S(2)}, u32[]{:S(2)}) collective-permute-start(f32[256,128]{1,0:T(8,128)S(1)} %get-tuple-element.56), channel_id=1, source_target_pairs={{0,12},{4,8},{8,4},{12,0},{16,28},{20,24},{24,20},{28,16},{1,13},{... | collective-permute-start | bytes 393224 | tf_op jit(solution)/shard_map/ppermute | solution.py:49
  26.0 7.4 %collective-permute-start.5 = (f32[256,128]{1,0:T(8,128)S(1)}, f32[256,128]{1,0:T(8,128)S(1)}, u32[]{:S(2)}, u32[]{:S(2)}) collective-permute-start(f32[256,128]{1,0:T(8,128)S(1)} %get-tuple-element.57), channel_id=1, source_target_pairs={{0,8},{4,12},{8,0},{12,4},{16,24},{20,28},{24,16},{28,20},{1,9},{5... | collective-permute-start | bytes 393224 | tf_op jit(solution)/shard_map/ppermute | solution.py:49
  26.8 8.3 %collective-permute-start.3 = (f32[256,128]{1,0:T(8,128)S(1)}, f32[256,128]{1,0:T(8,128)S(1)}, u32[]{:S(2)}, u32[]{:S(2)}) collective-permute-start(f32[256,128]{1,0:T(8,128)S(1)} %add_add_fusion.1), channel_id=1, source_target_pairs={{0,16},{4,20},{8,24},{12,28},{16,0},{20,4},{24,8},{28,12},{1,17},{... | collective-permute-start | bytes 393224 | tf_op jit(solution)/shard_map/ppermute | solution.py:49
  33.4 8.0 %collective-permute-start.7 = (f32[256,128]{1,0:T(8,128)S(1)}, f32[256,128]{1,0:T(8,128)S(1)}, u32[]{:S(2)}, u32[]{:S(2)}) collective-permute-start(f32[256,128]{1,0:T(8,128)S(1)} %add_add_fusion), channel_id=1, source_target_pairs={{0,16},{4,20},{8,24},{12,28},{16,0},{20,4},{24,8},{28,12},{1,17},{... | collective-permute-start | bytes 393224 | tf_op jit(solution)/shard_map/ppermute | solution.py:49
  35.1 8.3 %collective-permute-start.11 = (f32[256,128]{1,0:T(8,128)S(1)}, f32[256,128]{1,0:T(8,128)S(1)}, u32[]{:S(2)}, u32[]{:S(2)}) collective-permute-start(f32[256,128]{1,0:T(8,128)S(1)} %add_multiply_fusion.1.refs_2_.refs_0_), channel_id=1, source_target_pairs={{0,4},{4,0},{8,12},{12,8},{16,20},{20,16},{24,28},{28,24},{1,5},{5... | collective-permute-start | bytes 393224 | tf_op jit(solution)/shard_map/ppermute | solution.py:49
  39.2 9.9 %collective-permute-start.12 = (f32[256,128]{1,0:T(8,128)S(1)}, f32[256,128]{1,0:T(8,128)S(1)}, u32[]{:S(2)}, u32[]{:S(2)}) collective-permute-start(f32[256,128]{1,0:T(8,128)S(1)} %add_multiply_fusion.1.refs_2_.refs_0_), channel_id=1, source_target_pairs={{0,8},{4,12},{8,0},{12,4},{16,24},{20,28},{24,16},{28,20},{1,9},{5... | collective-permute-start | bytes 393224 | tf_op jit(solution)/shard_map/ppermute | solution.py:49
  39.3 9.8 %collective-permute-start.13 = (f32[256,128]{1,0:T(8,128)S(1)}, f32[256,128]{1,0:T(8,128)S(1)}, u32[]{:S(2)}, u32[]{:S(2)}) collective-permute-start(f32[256,128]{1,0:T(8,128)S(1)} %add_multiply_fusion.1.refs_2_.refs_0_), channel_id=1, source_target_pairs={{0,12},{4,8},{8,4},{12,0},{16,28},{20,24},{24,20},{28,16},{1,13},{... | collective-permute-start | bytes 393224 | tf_op jit(solution)/shard_map/ppermute | solution.py:49
  41.5 9.4 %collective-permute-start.10 = (f32[256,128]{1,0:T(8,128)S(1)}, f32[256,128]{1,0:T(8,128)S(1)}, u32[]{:S(2)}, u32[]{:S(2)}) collective-permute-start(f32[256,128]{1,0:T(8,128)S(1)} %add_multiply_fusion.refs_3_.refs_1_), channel_id=1, source_target_pairs={{0,12},{4,8},{8,4},{12,0},{16,28},{20,24},{24,20},{28,16},{1,13},{... | collective-permute-start | bytes 393224 | tf_op jit(solution)/shard_map/ppermute | solution.py:49
  43.2 8.1 %collective-permute-start.8 = (f32[256,128]{1,0:T(8,128)S(1)}, f32[256,128]{1,0:T(8,128)S(1)}, u32[]{:S(2)}, u32[]{:S(2)}) collective-permute-start(f32[256,128]{1,0:T(8,128)S(1)} %add_multiply_fusion.refs_3_.refs_1_), channel_id=1, source_target_pairs={{0,4},{4,0},{8,12},{12,8},{16,20},{20,16},{24,28},{28,24},{1,5},{5... | collective-permute-start | bytes 393224 | tf_op jit(solution)/shard_map/ppermute | solution.py:49
  43.4 7.9 %collective-permute-start.9 = (f32[256,128]{1,0:T(8,128)S(1)}, f32[256,128]{1,0:T(8,128)S(1)}, u32[]{:S(2)}, u32[]{:S(2)}) collective-permute-start(f32[256,128]{1,0:T(8,128)S(1)} %add_multiply_fusion.refs_3_.refs_1_), channel_id=1, source_target_pairs={{0,8},{4,12},{8,0},{12,4},{16,24},{20,28},{24,16},{28,20},{1,9},{5... | collective-permute-start | bytes 393224 | tf_op jit(solution)/shard_map/ppermute | solution.py:49
  53.0 1.7 %collective-permute-start.14 = (f32[80,1024]{1,0:T(8,128)S(1)}, f32[80,1024]{1,0:T(8,128)S(1)}, u32[]{:S(2)}, u32[]{:S(2)}) collective-permute-start(f32[80,1024]{1,0:T(8,128)S(1)} %get-tuple-element.65), channel_id=1, source_target_pairs={{0,1},{1,0},{2,3},{3,2},{4,5},{5,4},{6,7},{7,6},{8,9},{9,8},{10,11... | collective-permute-start | bytes 983048 | tf_op jit(solution)/shard_map/ppermute | solution.py:49
  55.3 7.4 %collective-permute-start.17 = (f32[32,1024]{1,0:T(8,128)S(1)}, f32[32,1024]{1,0:T(8,128)S(1)}, u32[]{:S(2)}, u32[]{:S(2)}) collective-permute-start(f32[32,1024]{1,0:T(8,128)S(1)} %get-tuple-element.69), channel_id=1, source_target_pairs={{0,2},{1,3},{2,0},{3,1},{4,6},{5,7},{6,4},{7,5},{8,10},{9,11},{10,... | collective-permute-start | bytes 393224 | tf_op jit(solution)/shard_map/ppermute | solution.py:49
  56.9 5.8 %collective-permute-start.15 = (f32[16,1024]{1,0:T(8,128)S(1)}, f32[16,1024]{1,0:T(8,128)S(1)}, u32[]{:S(2)}, u32[]{:S(2)}) collective-permute-start(f32[16,1024]{1,0:T(8,128)S(1)} %get-tuple-element.67), channel_id=1, source_target_pairs={{0,6},{1,7},{2,4},{3,5},{4,2},{5,3},{6,0},{7,1},{8,14},{9,15},{10,... | collective-permute-start | bytes 196616 | tf_op jit(solution)/shard_map/ppermute | solution.py:49
  58.2 4.4 %collective-permute-start.16 = (f32[16,1024]{1,0:T(8,128)S(1)}, f32[16,1024]{1,0:T(8,128)S(1)}, u32[]{:S(2)}, u32[]{:S(2)}) collective-permute-start(f32[16,1024]{1,0:T(8,128)S(1)} %get-tuple-element.68), channel_id=1, source_target_pairs={{0,4},{4,0},{8,12},{12,8},{16,20},{20,16},{24,28},{28,24},{1,5},{5... | collective-permute-start | bytes 196616 | tf_op jit(solution)/shard_map/ppermute | solution.py:49
  62.7 8.9 %collective-permute-start.18 = (f32[16,1024]{1,0:T(8,128)S(1)}, f32[16,1024]{1,0:T(8,128)S(1)}, u32[]{:S(2)}, u32[]{:S(2)}) collective-permute-start(f32[16,1024]{1,0:T(8,128)S(1)} %slice_add_fusion), channel_id=1, source_target_pairs={{0,24},{4,28},{8,16},{12,20},{16,8},{20,12},{24,0},{28,4},{1,25},{... | collective-permute-start | bytes 196616 | tf_op jit(solution)/shard_map/ppermute | solution.py:49
  66.9 5.9 %collective-permute-start.19 = (f32[16,1024]{1,0:T(8,128)S(1)}, f32[16,1024]{1,0:T(8,128)S(1)}, u32[]{:S(2)}, u32[]{:S(2)}) collective-permute-start(f32[16,1024]{1,0:T(8,128)S(1)} %slice_add_fusion), channel_id=1, source_target_pairs={{0,16},{4,20},{8,24},{12,28},{16,0},{20,4},{24,8},{28,12},{1,17},{... | collective-permute-start | bytes 196616 | tf_op jit(solution)/shard_map/ppermute | solution.py:49
  67.5 5.2 %collective-permute-start.20 = (f32[16,1024]{1,0:T(8,128)S(1)}, f32[16,1024]{1,0:T(8,128)S(1)}, u32[]{:S(2)}, u32[]{:S(2)}) collective-permute-start(f32[16,1024]{1,0:T(8,128)S(1)} %slice_add_fusion), channel_id=1, source_target_pairs={{0,8},{4,12},{8,0},{12,4},{16,24},{20,28},{24,16},{28,20},{1,9},{5... | collective-permute-start | bytes 196616 | tf_op jit(solution)/shard_map/ppermute | solution.py:49
  72.8 7.1 %collective-permute-start.21 = (f32[16,1024]{1,0:T(8,128)S(1)}, f32[16,1024]{1,0:T(8,128)S(1)}, u32[]{:S(2)}, u32[]{:S(2)}) collective-permute-start(f32[16,1024]{1,0:T(8,128)S(1)} %add_add_fusion.2.token), channel_id=1, source_target_pairs={{0,2},{1,3},{2,0},{3,1},{4,6},{5,7},{6,4},{7,5},{8,10},{9,11},{10,... | collective-permute-start | bytes 196616 | tf_op jit(solution)/shard_map/ppermute | solution.py:49
  74.2 5.6 %collective-permute-start.22 = (f32[16,1024]{1,0:T(8,128)S(1)}, f32[16,1024]{1,0:T(8,128)S(1)}, u32[]{:S(2)}, u32[]{:S(2)}) collective-permute-start(f32[16,1024]{1,0:T(8,128)S(1)} %add_add_fusion.2.token), channel_id=1, source_target_pairs={{0,4},{4,0},{8,12},{12,8},{16,20},{20,16},{24,28},{28,24},{1,5},{5... | collective-permute-start | bytes 196616 | tf_op jit(solution)/shard_map/ppermute | solution.py:49
  75.4 5.2 %collective-permute-start.23 = (f32[16,1024]{1,0:T(8,128)S(1)}, f32[16,1024]{1,0:T(8,128)S(1)}, u32[]{:S(2)}, u32[]{:S(2)}) collective-permute-start(f32[16,1024]{1,0:T(8,128)S(1)} %add_add_fusion.2.token), channel_id=1, source_target_pairs={{0,6},{1,7},{2,4},{3,5},{4,2},{5,3},{6,0},{7,1},{8,14},{9,15},{10,... | collective-permute-start | bytes 196616 | tf_op jit(solution)/shard_map/ppermute | solution.py:49
  80.7 1.6 %collective-permute-start.24 = (f32[64,1024]{1,0:T(8,128)S(1)}, f32[64,1024]{1,0:T(8,128)S(1)}, u32[]{:S(2)}, u32[]{:S(2)}) collective-permute-start(f32[64,1024]{1,0:T(8,128)S(1)} %constant_dynamic-update-slice_fusion.right_here), channel_id=1, source_target_pairs={{0,1},{1,0},{2,3},{3,2},{4,5},{5,4},{6,7},{7,6},{8,9},{9,8},{10,11... | collective-permute-start | bytes 786440 | tf_op jit(solution)/shard_map/ppermute | solution.py:49

commit v7 on v6

--- a/solution.py
+++ b/solution.py
@@ -484,7 +484,10 @@
             wide = dot(high, jnp.concatenate([first, second], 0), 1, 1)
             value = wide[:, :rank] + wide[:, rank:] + dot(low, first, 1, 1)
             rows = slice((s * PARTS + p) * part, (s * PARTS + p + 1) * part)
-            ortho[rows, :] = jnp.concatenate(split(value), 1)
+            high, low = split(0.2 * value)
+            wide = dot(high, jnp.concatenate([first, second], 1), 1, 0)
+            turned = wide[:, :rank] + wide[:, rank:] + dot(low, first, 1, 0)
+            ortho[rows, :] = jnp.concatenate(split(turned), 1)
             start = ((who[0] ^ s) * PARTS + p) * part
             total[pl.ds(pl.multiple_of(start, part), part), :] = value
     own = own_ortho.shape[0]
@@ -512,17 +515,16 @@
 
 
 def finish_kernel(group, places, scale, who, right_here, right_there, state, ortho, own_ortho, *refs):
-    blended, new_momentum, new_basis, update, right, values, coeff_high, coeff_low, basis_held, update_held, sem = refs
+    blended, new_momentum, new_basis, update, right, values, right_high, right_low, basis_held, update_held, sem = refs
     rank, kv = right.shape
     half = rank // 2
     core = who[2] & 1
     right[pl.ds(pl.multiple_of(core * half, half), half), :] = right_here[...]
     right[pl.ds(pl.multiple_of((1 - core) * half, half), half), :] = right_there[...]
-    coeff = dot(state[:, rank:], right[...], 1, 0, EXACT)
-    high, low = split(0.2 * coeff)
-    coeff_high[:rank, :] = high
-    coeff_high[rank:, :] = high
-    coeff_low[...] = low
+    high, low = split(right[...])
+    right_high[:rank, :] = high
+    right_high[rank:, :] = high
+    right_low[...] = low
     block = values.shape[0] // group
     rows = block // CUTS
     copies = []
@@ -530,7 +532,7 @@
         for c in range(CUTS):
             here = slice(s * block + c * rows, s * block + (c + 1) * rows)
             part = ortho[here, :]
-            feedback = dot(part, coeff_high[...], 1, 0) + dot(part[:, :rank], coeff_low[...], 1, 0)
+            feedback = dot(part, right_high[...], 1, 0) + dot(part[:, :rank], right_low[...], 1, 0)
             at = places[s] + c * rows
             values[here, :] = blended[at : at + rows, :] - feedback
             there = pl.multiple_of((who[0] ^ s) * block + c * rows, rows)
@@ -538,6 +540,7 @@
                 pltpu.make_async_copy(values.at[here], new_momentum.at[pl.ds(there, rows)], sem.at[len(copies)])
             )
             copies[-1].start()
+    coeff = dot(state[:, rank:], right[...], 1, 0, EXACT)
     norm = jnp.sqrt(jnp.sum(coeff * coeff, axis=1, keepdims=True) + 1e-06)
     normed = coeff / norm
     count = new_basis.shape[0]

time: 87.7 us -> 88.4 us (level)
  Pallas kernels: 38.5 us -> 39.5 us
    pallas_call x1, Pallas kernels: 1.13 us -> 2.28 us  [orthonormal(): pl.pallas_call(functools.partial(ortho_kernel, group), in_specs=[SMEM] +...]
  transfers between devices with their start and end apart: 25 -> 25, of which waited for: 10 -> 9; matrix products, arithmetic and copies ran while one was open for 0% -> 0% of each run, Pallas kernels for 20% -> 21%
where the time goes in v7:
time: 88.4 us; the launch traced here: 88.2 us
  Pallas kernels  39.5 us (45%)
  starting transfers between devices  34.9 us (39%)
  waiting for transfers between devices  12.5 us (14%)
  between operations  1.05 us (1%)
    ppermute x25, starting transfers between devices, swap(): return lax.ppermute(value, axes, pairs)  34.9 us
    ppermute x25, waiting for transfers between devices, swap(): return lax.ppermute(value, axes, pairs)  12.5 us
    pallas_call x1, Pallas kernels, first_blend(): pl.pallas_call(functools.partial(first_blend_kernel, group, offsets, late...  10.6 us
    pallas_call x3, Pallas kernels, right_terms(): pl.pallas_call(functools.partial(right_kernel, pieces, first, last, scale...  7.36 us
    pallas_call x2, Pallas kernels, blend(): pl.pallas_call(functools.partial(blend_kernel, jobs, len(momentum)), in_s...  6.72 us
    pallas_call x1, Pallas kernels, finish(): pl.pallas_call(functools.partial(finish_kernel, group, places, scale), in...  4.96 us
    pallas_call x1, Pallas kernels, factor(): pl.pallas_call(functools.partial(factor_kernel, panels, grams, block), in...  3.52 us
    pallas_call x1, Pallas kernels, load(): pl.pallas_call(load_kernel, in_specs=[ANY, ANY], out_specs=VMEM, out_shap...  3.5 us
  transfers between devices with their start and end apart: 25, of which 9 were waited for; matrix products, arithmetic and copies ran while one was open for 0% of the time, Pallas kernels for 21%

profile of v7, /device:TPU:0, one launch (start us, length us, event | category | flops | bytes accessed | tf_op | source)
XLA Modules:
  0.0 88.2 jit_solution(11746834343088052734)
XLA Ops:
  0.6 10.6 %first_blend.1 = (f32[2048,1024]{1,0:T(8,128)}, bf16[2048,1024]{1,0:T(8,128)(2,1)S(1)}, bf16[2,2048,512]{2,1,0:T(8,128)(2,1)S(1)}, f32[512,1024]{1,0:T(8,128)S(1...) custom-call(bf16[2048,2048]{1,0:T(8,128)(2,1)} %acts.1, ...), custom_call_target="tpu_custom_call" | custom-call | tf_op jit(solution)/shard_map/first_blend/pallas_call | solution.py:201
  11.2 3.4 %blend.2 = (f32[2048,1024]{1,0:T(8,128)}, f32[256,128]{1,0:T(8,128)S(1)}, f32[256,128]{1,0:T(8,128)S(1)}) custom-call(bf16[2,2048,512]{2,1,0:T(8,128)(2,1)S(1)} %get-tuple-element.44.acts, bf16[2048,1024]{1,0:T(8,128)(2,1)S(1)} %get-tuple-element.45.grads, f32[1024,128]{1,0:T(8,128)S(1)} %copy-done, ...), custom_call_target="tpu_custom_call", output_to_operand_aliasing={{0}: (5, {})} | custom-call | tf_op jit(solution)/shard_map/blend/pallas_call | solution.py:251
  14.6 3.0 %collective-permute-start.2 = (f32[256,128]{1,0:T(8,128)S(1)}, f32[256,128]{1,0:T(8,128)S(1)}, u32[]{:S(2)}, u32[]{:S(2)}) collective-permute-start(f32[256,128]{1,0:T(8,128)S(1)} %get-tuple-element.54), channel_id=1, source_target_pairs={{0,4},{4,0},{8,12},{12,8},{16,20},{20,16},{24,28},{28,24},{1,5},{5... | collective-permute-start | bytes 393224 | tf_op jit(solution)/shard_map/ppermute | solution.py:49
  17.6 1.5 %collective-permute-start = (f32[256,128]{1,0:T(8,128)S(1)}, f32[256,128]{1,0:T(8,128)S(1)}, u32[]{:S(2)}, u32[]{:S(2)}) collective-permute-start(f32[256,128]{1,0:T(8,128)S(1)} %get-tuple-element.52), channel_id=1, source_target_pairs={{0,12},{4,8},{8,4},{12,0},{16,28},{20,24},{24,20},{28,16},{1,13},{... | collective-permute-start | bytes 393224 | tf_op jit(solution)/shard_map/ppermute | solution.py:49
  19.1 0.0 collective-permute-start.1
  19.2 1.9 %collective-permute-start.6 = (f32[256,128]{1,0:T(8,128)S(1)}, f32[256,128]{1,0:T(8,128)S(1)}, u32[]{:S(2)}, u32[]{:S(2)}) collective-permute-start(f32[256,128]{1,0:T(8,128)S(1)} %get-tuple-element.58), channel_id=1, source_target_pairs={{0,4},{4,0},{8,12},{12,8},{16,20},{20,16},{24,28},{28,24},{1,5},{5... | collective-permute-start | bytes 393224 | tf_op jit(solution)/shard_map/ppermute | solution.py:49
  21.1 1.5 %collective-permute-start.4 = (f32[256,128]{1,0:T(8,128)S(1)}, f32[256,128]{1,0:T(8,128)S(1)}, u32[]{:S(2)}, u32[]{:S(2)}) collective-permute-start(f32[256,128]{1,0:T(8,128)S(1)} %get-tuple-element.56), channel_id=1, source_target_pairs={{0,12},{4,8},{8,4},{12,0},{16,28},{20,24},{24,20},{28,16},{1,13},{... | collective-permute-start | bytes 393224 | tf_op jit(solution)/shard_map/ppermute | solution.py:49
  22.6 3.4 %blend.3 = (f32[2048,1024]{1,0:T(8,128)}, f32[256,128]{1,0:T(8,128)S(1)}, f32[256,128]{1,0:T(8,128)S(1)}) custom-call(bf16[2,2048,512]{2,1,0:T(8,128)(2,1)S(1)} %get-tuple-element.44.acts, bf16[2048,1024]{1,0:T(8,128)(2,1)S(1)} %get-tuple-element.45.grads, f32[1024,128]{1,0:T(8,128)S(1)} %copy-done, ...), custom_call_target="tpu_custom_call", output_to_operand_aliasing={{0}: (5, {})} | custom-call | tf_op jit(solution)/shard_map/blend/pallas_call | solution.py:251
  26.0 0.0 collective-permute-done.2
  26.0 0.8 collective-permute-start.5
  26.8 2.7 %collective-permute-start.3 = (f32[256,128]{1,0:T(8,128)S(1)}, f32[256,128]{1,0:T(8,128)S(1)}, u32[]{:S(2)}, u32[]{:S(2)}) collective-permute-start(f32[256,128]{1,0:T(8,128)S(1)} %add_add_fusion.1), channel_id=1, source_target_pairs={{0,16},{4,20},{8,24},{12,28},{16,0},{20,4},{24,8},{28,12},{1,17},{... | collective-permute-start | bytes 393224 | tf_op jit(solution)/shard_map/ppermute | solution.py:49
  29.5 2.1 %collective-permute-done.4 = f32[256,128]{1,0:T(8,128)S(1)} collective-permute-done((f32[256,128]{1,0:T(8,128)S(1)}, f32[256,128]{1,0:T(8,128)S(1)}, u32[]{:S(2)}, u32[]{:S(2)}) %collective-permute-start.4) | collective-permute-done | bytes 131104 | tf_op jit(solution)/shard_map/ppermute | solution.py:49
  31.6 1.8 %collective-permute-done.5 = f32[256,128]{1,0:T(8,128)S(1)} collective-permute-done((f32[256,128]{1,0:T(8,128)S(1)}, f32[256,128]{1,0:T(8,128)S(1)}, u32[]{:S(2)}, u32[]{:S(2)}) %collective-permute-start.5) | collective-permute-done | bytes 131104 | tf_op jit(solution)/shard_map/ppermute | solution.py:49
  33.4 1.7 %collective-permute-start.7 = (f32[256,128]{1,0:T(8,128)S(1)}, f32[256,128]{1,0:T(8,128)S(1)}, u32[]{:S(2)}, u32[]{:S(2)}) collective-permute-start(f32[256,128]{1,0:T(8,128)S(1)} %add_add_fusion), channel_id=1, source_target_pairs={{0,16},{4,20},{8,24},{12,28},{16,0},{20,4},{24,8},{28,12},{1,17},{... | collective-permute-start | bytes 393224 | tf_op jit(solution)/shard_map/ppermute | solution.py:49
  35.1 0.0 collective-permute-done.3
  35.1 4.1 %collective-permute-start.11 = (f32[256,128]{1,0:T(8,128)S(1)}, f32[256,128]{1,0:T(8,128)S(1)}, u32[]{:S(2)}, u32[]{:S(2)}) collective-permute-start(f32[256,128]{1,0:T(8,128)S(1)} %add_multiply_fusion.1.refs_2_.refs_0_), channel_id=1, source_target_pairs={{0,4},{4,0},{8,12},{12,8},{16,20},{20,16},{24,28},{28,24},{1,5},{5... | collective-permute-start | bytes 393224 | tf_op jit(solution)/shard_map/ppermute | solution.py:49
  39.2 0.1 collective-permute-start.12
  39.3 1.4 %collective-permute-start.13 = (f32[256,128]{1,0:T(8,128)S(1)}, f32[256,128]{1,0:T(8,128)S(1)}, u32[]{:S(2)}, u32[]{:S(2)}) collective-permute-start(f32[256,128]{1,0:T(8,128)S(1)} %add_multiply_fusion.1.refs_2_.refs_0_), channel_id=1, source_target_pairs={{0,12},{4,8},{8,4},{12,0},{16,28},{20,24},{24,20},{28,16},{1,13},{... | collective-permute-start | bytes 393224 | tf_op jit(solution)/shard_map/ppermute | solution.py:49
  40.8 0.7 collective-permute-done.7
  41.5 1.7 %collective-permute-start.10 = (f32[256,128]{1,0:T(8,128)S(1)}, f32[256,128]{1,0:T(8,128)S(1)}, u32[]{:S(2)}, u32[]{:S(2)}) collective-permute-start(f32[256,128]{1,0:T(8,128)S(1)} %add_multiply_fusion.refs_3_.refs_1_), channel_id=1, source_target_pairs={{0,12},{4,8},{8,4},{12,0},{16,28},{20,24},{24,20},{28,16},{1,13},{... | collective-permute-start | bytes 393224 | tf_op jit(solution)/shard_map/ppermute | solution.py:49
  43.2 0.2 collective-permute-start.8
  43.4 1.6 %collective-permute-start.9 = (f32[256,128]{1,0:T(8,128)S(1)}, f32[256,128]{1,0:T(8,128)S(1)}, u32[]{:S(2)}, u32[]{:S(2)}) collective-permute-start(f32[256,128]{1,0:T(8,128)S(1)} %add_multiply_fusion.refs_3_.refs_1_), channel_id=1, source_target_pairs={{0,8},{4,12},{8,0},{12,4},{16,24},{20,28},{24,16},{28,20},{1,9},{5... | collective-permute-start | bytes 393224 | tf_op jit(solution)/shard_map/ppermute | solution.py:49
  45.0 0.1 pad_add_fusion.refs_0_.who
  45.1 4.0 %right_terms.3 = (f32[128,1024]{1,0:T(8,128)S(1)}, f32[128,128]{1,0:T(8,128)S(1)}, f32[2048,1024]{1,0:T(8,128)S(1)}) custom-call(s32[4]{0:T(128)S(1)} %pad_add_fusion.refs_0_.who, f32[2048,1024]{1,0:T(8,128)} %get-tuple-element.50.refs_1_.source, f32[256,128]{1,0:T(8,128)S(1)} %add_multiply_fusion.1.refs_2_.refs_0_, ...), custom_call_target="tpu_custom_call" | custom-call | tf_op jit(solution)/shard_map/right_terms/pallas_call | solution.py:347
  49.1 1.7 %right_terms.4 = (f32[128,1024]{1,0:T(8,128)S(1)}, f32[128,128]{1,0:T(8,128)S(1)}) custom-call(s32[4]{0:T(128)S(1)} %pad_add_fusion.refs_0_.who, f32[2048,1024]{1,0:T(8,128)S(1)} %get-tuple-element.59.refs_1_, f32[256,128]{1,0:T(8,128)S(1)} %collective-permute-done.11.refs_2_, f32[256,128]{1,0:T(8,128)S(1)} %collective-permute-done.12.refs_3_.refs_4_, ...), custom_call_target="tpu_custom_call" | custom-call | tf_op jit(solution)/shard_map/right_terms/pallas_call | solution.py:347
  50.9 0.4 collective-permute-done.8.refs_2_.refs_3_
  51.3 0.1 collective-permute-done.9.refs_3_.refs_5_
  51.3 1.6 %right_terms.5 = (f32[80,1024]{1,0:T(8,128)S(1)}, f32[80,1024]{1,0:T(8,128)S(1)}) custom-call(s32[4]{0:T(128)S(1)} %pad_add_fusion.refs_0_.who, f32[2048,1024]{1,0:T(8,128)S(1)} %get-tuple-element.59.refs_1_, f32[256,128]{1,0:T(8,128)S(1)} %collective-permute-done.8.refs_2_.refs_3_, f32[256,128]{1,0:T(8,128)S(1)} %collective-permute-done.9.refs_3_.refs_5_, ...), custom_call_target="tpu_custom_call" | custom-call | tf_op jit(solution)/shard_map/right_terms/pallas_call | solution.py:347
  53.0 0.1 collective-permute-start.14
  53.1 1.6 %collective-permute-done.14.arrived = f32[80,1024]{1,0:T(8,128)S(1)} collective-permute-done((f32[80,1024]{1,0:T(8,128)S(1)}, f32[80,1024]{1,0:T(8,128)S(1)}, u32[]{:S(2)}, u32[]{:S(2)}) %collective-permute-start.14) | collective-permute-done | bytes 327712 | tf_op jit(solution)/shard_map/ppermute | solution.py:49
  54.7 0.6 cut.1
  55.3 1.6 %collective-permute-start.17 = (f32[32,1024]{1,0:T(8,128)S(1)}, f32[32,1024]{1,0:T(8,128)S(1)}, u32[]{:S(2)}, u32[]{:S(2)}) collective-permute-start(f32[32,1024]{1,0:T(8,128)S(1)} %get-tuple-element.69), channel_id=1, source_target_pairs={{0,2},{1,3},{2,0},{3,1},{4,6},{5,7},{6,4},{7,5},{8,10},{9,11},{10,... | collective-permute-start | bytes 393224 | tf_op jit(solution)/shard_map/ppermute | solution.py:49
  56.9 1.4 %collective-permute-start.15 = (f32[16,1024]{1,0:T(8,128)S(1)}, f32[16,1024]{1,0:T(8,128)S(1)}, u32[]{:S(2)}, u32[]{:S(2)}) collective-permute-start(f32[16,1024]{1,0:T(8,128)S(1)} %get-tuple-element.67), channel_id=1, source_target_pairs={{0,6},{1,7},{2,4},{3,5},{4,2},{5,3},{6,0},{7,1},{8,14},{9,15},{10,... | collective-permute-start | bytes 196616 | tf_op jit(solution)/shard_map/ppermute | solution.py:49
  58.2 0.6 collective-permute-start.16
  58.8 3.8 %collective-permute-done.15 = f32[16,1024]{1,0:T(8,128)S(1)} collective-permute-done((f32[16,1024]{1,0:T(8,128)S(1)}, f32[16,1024]{1,0:T(8,128)S(1)}, u32[]{:S(2)}, u32[]{:S(2)}) %collective-permute-start.15) | collective-permute-done | bytes 65568 | tf_op jit(solution)/shard_map/ppermute | solution.py:49
  62.7 4.2 %collective-permute-start.18 = (f32[16,1024]{1,0:T(8,128)S(1)}, f32[16,1024]{1,0:T(8,128)S(1)}, u32[]{:S(2)}, u32[]{:S(2)}) collective-permute-start(f32[16,1024]{1,0:T(8,128)S(1)} %slice_add_fusion), channel_id=1, source_target_pairs={{0,24},{4,28},{8,16},{12,20},{16,8},{20,12},{24,0},{28,4},{1,25},{... | collective-permute-start | bytes 196616 | tf_op jit(solution)/shard_map/ppermute | solution.py:49
  66.9 0.6 collective-permute-start.19
  67.5 0.5 collective-permute-start.20
  68.0 3.5 %factor.1.state = f32[128,256]{1,0:T(8,128)S(1)} custom-call(f32[16,1024]{1,0:T(8,128)S(1)} %get-tuple-element.70.refs_0_, f32[32,1024]{1,0:T(8,128)S(1)} %collective-permute-done.17.refs_1_), custom_call_target="tpu_custom_call" | custom-call | tf_op jit(solution)/shard_map/factor/pallas_call | solution.py:437
  71.5 1.2 %collective-permute-done.19 = f32[16,1024]{1,0:T(8,128)S(1)} collective-permute-done((f32[16,1024]{1,0:T(8,128)S(1)}, f32[16,1024]{1,0:T(8,128)S(1)}, u32[]{:S(2)}, u32[]{:S(2)}) %collective-permute-start.19) | collective-permute-done | bytes 65568 | tf_op jit(solution)/shard_map/ppermute | solution.py:49
  72.8 1.5 %collective-permute-start.21 = (f32[16,1024]{1,0:T(8,128)S(1)}, f32[16,1024]{1,0:T(8,128)S(1)}, u32[]{:S(2)}, u32[]{:S(2)}) collective-permute-start(f32[16,1024]{1,0:T(8,128)S(1)} %add_add_fusion.2.token), channel_id=1, source_target_pairs={{0,2},{1,3},{2,0},{3,1},{4,6},{5,7},{6,4},{7,5},{8,10},{9,11},{10,... | collective-permute-start | bytes 196616 | tf_op jit(solution)/shard_map/ppermute | solution.py:49
  74.2 1.2 %collective-permute-start.22 = (f32[16,1024]{1,0:T(8,128)S(1)}, f32[16,1024]{1,0:T(8,128)S(1)}, u32[]{:S(2)}, u32[]{:S(2)}) collective-permute-start(f32[16,1024]{1,0:T(8,128)S(1)} %add_add_fusion.2.token), channel_id=1, source_target_pairs={{0,4},{4,0},{8,12},{12,8},{16,20},{20,16},{24,28},{28,24},{1,5},{5... | collective-permute-start | bytes 196616 | tf_op jit(solution)/shard_map/ppermute | solution.py:49
  75.4 0.9 collective-permute-start.23
  76.3 3.5 %load.1.refs_0_ = f32[2048,1024]{1,0:T(8,128)S(1)} custom-call(f32[2048,1024]{1,0:T(8,128)} %get-tuple-element.50.refs_1_.source, f32[16,1024]{1,0:T(8,128)S(1)} %add_add_fusion.2.token), custom_call_target="tpu_custom_call" | custom-call | tf_op jit(solution)/shard_map/load/pallas_call | solution.py:462
  79.8 0.8 collective-permute-done.23
  80.7 0.1 collective-permute-start.24
  80.8 2.3 %ortho.1 = (bf16[2048,256]{1,0:T(8,128)(2,1)S(1)}, f32[256,128]{1,0:T(8,128)S(1)}) custom-call(s32[4]{0:T(128)S(1)} %pad_add_fusion.refs_0_.who, f32[128,256]{1,0:T(8,128)S(1)} %factor.1.state, f32[256,128]{1,0:T(8,128)S(1)} %add_multiply_fusion.1.refs_2_.refs_0_, f32[256,128]{1,0:T(8,128)S(1)} %add_multiply_fusion.refs_3_.refs_1_, ...), custom_call_target="tpu_custom_call" | custom-call | tf_op jit(solution)/shard_map/ortho/pallas_call | solution.py:500
  83.1 5.0 %finish.1 = (f32[2048,1024]{1,0:T(8,128)}, f32[256,128]{1,0:T(8,128)}, bf16[256,1024]{1,0:T(8,128)(2,1)}) custom-call(s32[4]{0:T(128)S(1)} %pad_add_fusion.refs_0_.who, f32[64,1024]{1,0:T(8,128)S(1)} %constant_dynamic-update-slice_fusion.right_here, f32[64,1024]{1,0:T(8,128)S(1)} %collective-permute-done.24.right_there, f32[128,256]{1,0:T(8,128)S(1)} %factor.1.state, ...), custom_call_target="tpu_custom_call" | custom-call | tf_op jit(solution)/shard_map/finish/pallas_call | solution.py:569
  (27 shorter events, 0.2 us)
Async XLA Ops:
  0.6 10.6 %copy-start = (f32[1024,128]{1,0:T(8,128)S(1)}, f32[1024,128]{1,0:T(8,128)}, u32[]{:S(2)}) copy-start(f32[1024,128]{1,0:T(8,128)} %basis.5) | copy-start | bytes 1572868
  14.6 11.4 %collective-permute-start.2 = (f32[256,128]{1,0:T(8,128)S(1)}, f32[256,128]{1,0:T(8,128)S(1)}, u32[]{:S(2)}, u32[]{:S(2)}) collective-permute-start(f32[256,128]{1,0:T(8,128)S(1)} %get-tuple-element.54), channel_id=1, source_target_pairs={{0,4},{4,0},{8,12},{12,8},{16,20},{20,16},{24,28},{28,24},{1,5},{5... | collective-permute-start | bytes 393224 | tf_op jit(solution)/shard_map/ppermute | solution.py:49
  17.6 9.2 %collective-permute-start = (f32[256,128]{1,0:T(8,128)S(1)}, f32[256,128]{1,0:T(8,128)S(1)}, u32[]{:S(2)}, u32[]{:S(2)}) collective-permute-start(f32[256,128]{1,0:T(8,128)S(1)} %get-tuple-element.52), channel_id=1, source_target_pairs={{0,12},{4,8},{8,4},{12,0},{16,28},{20,24},{24,20},{28,16},{1,13},{... | collective-permute-start | bytes 393224 | tf_op jit(solution)/shard_map/ppermute | solution.py:49
  19.1 7.6 %collective-permute-start.1 = (f32[256,128]{1,0:T(8,128)S(1)}, f32[256,128]{1,0:T(8,128)S(1)}, u32[]{:S(2)}, u32[]{:S(2)}) collective-permute-start(f32[256,128]{1,0:T(8,128)S(1)} %get-tuple-element.53), channel_id=1, source_target_pairs={{0,8},{4,12},{8,0},{12,4},{16,24},{20,28},{24,16},{28,20},{1,9},{5... | collective-permute-start | bytes 393224 | tf_op jit(solution)/shard_map/ppermute | solution.py:49
  19.2 10.3 %collective-permute-start.6 = (f32[256,128]{1,0:T(8,128)S(1)}, f32[256,128]{1,0:T(8,128)S(1)}, u32[]{:S(2)}, u32[]{:S(2)}) collective-permute-start(f32[256,128]{1,0:T(8,128)S(1)} %get-tuple-element.58), channel_id=1, source_target_pairs={{0,4},{4,0},{8,12},{12,8},{16,20},{20,16},{24,28},{28,24},{1,5},{5... | collective-permute-start | bytes 393224 | tf_op jit(solution)/shard_map/ppermute | solution.py:49
  21.1 10.5 %collective-permute-start.4 = (f32[256,128]{1,0:T(8,128)S(1)}, f32[256,128]{1,0:T(8,128)S(1)}, u32[]{:S(2)}, u32[]{:S(2)}) collective-permute-start(f32[256,128]{1,0:T(8,128)S(1)} %get-tuple-element.56), channel_id=1, source_target_pairs={{0,12},{4,8},{8,4},{12,0},{16,28},{20,24},{24,20},{28,16},{1,13},{... | collective-permute-start | bytes 393224 | tf_op jit(solution)/shard_map/ppermute | solution.py:49
  26.0 7.4 %collective-permute-start.5 = (f32[256,128]{1,0:T(8,128)S(1)}, f32[256,128]{1,0:T(8,128)S(1)}, u32[]{:S(2)}, u32[]{:S(2)}) collective-permute-start(f32[256,128]{1,0:T(8,128)S(1)} %get-tuple-element.57), channel_id=1, source_target_pairs={{0,8},{4,12},{8,0},{12,4},{16,24},{20,28},{24,16},{28,20},{1,9},{5... | collective-permute-start | bytes 393224 | tf_op jit(solution)/shard_map/ppermute | solution.py:49
  26.8 8.3 %collective-permute-start.3 = (f32[256,128]{1,0:T(8,128)S(1)}, f32[256,128]{1,0:T(8,128)S(1)}, u32[]{:S(2)}, u32[]{:S(2)}) collective-permute-start(f32[256,128]{1,0:T(8,128)S(1)} %add_add_fusion.1), channel_id=1, source_target_pairs={{0,16},{4,20},{8,24},{12,28},{16,0},{20,4},{24,8},{28,12},{1,17},{... | collective-permute-start | bytes 393224 | tf_op jit(solution)/shard_map/ppermute | solution.py:49
  33.4 8.0 %collective-permute-start.7 = (f32[256,128]{1,0:T(8,128)S(1)}, f32[256,128]{1,0:T(8,128)S(1)}, u32[]{:S(2)}, u32[]{:S(2)}) collective-permute-start(f32[256,128]{1,0:T(8,128)S(1)} %add_add_fusion), channel_id=1, source_target_pairs={{0,16},{4,20},{8,24},{12,28},{16,0},{20,4},{24,8},{28,12},{1,17},{... | collective-permute-start | bytes 393224 | tf_op jit(solution)/shard_map/ppermute | solution.py:49
  35.1 8.3 %collective-permute-start.11 = (f32[256,128]{1,0:T(8,128)S(1)}, f32[256,128]{1,0:T(8,128)S(1)}, u32[]{:S(2)}, u32[]{:S(2)}) collective-permute-start(f32[256,128]{1,0:T(8,128)S(1)} %add_multiply_fusion.1.refs_2_.refs_0_), channel_id=1, source_target_pairs={{0,4},{4,0},{8,12},{12,8},{16,20},{20,16},{24,28},{28,24},{1,5},{5... | collective-permute-start | bytes 393224 | tf_op jit(solution)/shard_map/ppermute | solution.py:49
  39.2 9.9 %collective-permute-start.12 = (f32[256,128]{1,0:T(8,128)S(1)}, f32[256,128]{1,0:T(8,128)S(1)}, u32[]{:S(2)}, u32[]{:S(2)}) collective-permute-start(f32[256,128]{1,0:T(8,128)S(1)} %add_multiply_fusion.1.refs_2_.refs_0_), channel_id=1, source_target_pairs={{0,8},{4,12},{8,0},{12,4},{16,24},{20,28},{24,16},{28,20},{1,9},{5... | collective-permute-start | bytes 393224 | tf_op jit(solution)/shard_map/ppermute | solution.py:49
  39.3 9.8 %collective-permute-start.13 = (f32[256,128]{1,0:T(8,128)S(1)}, f32[256,128]{1,0:T(8,128)S(1)}, u32[]{:S(2)}, u32[]{:S(2)}) collective-permute-start(f32[256,128]{1,0:T(8,128)S(1)} %add_multiply_fusion.1.refs_2_.refs_0_), channel_id=1, source_target_pairs={{0,12},{4,8},{8,4},{12,0},{16,28},{20,24},{24,20},{28,16},{1,13},{... | collective-permute-start | bytes 393224 | tf_op jit(solution)/shard_map/ppermute | solution.py:49
  41.5 9.4 %collective-permute-start.10 = (f32[256,128]{1,0:T(8,128)S(1)}, f32[256,128]{1,0:T(8,128)S(1)}, u32[]{:S(2)}, u32[]{:S(2)}) collective-permute-start(f32[256,128]{1,0:T(8,128)S(1)} %add_multiply_fusion.refs_3_.refs_1_), channel_id=1, source_target_pairs={{0,12},{4,8},{8,4},{12,0},{16,28},{20,24},{24,20},{28,16},{1,13},{... | collective-permute-start | bytes 393224 | tf_op jit(solution)/shard_map/ppermute | solution.py:49
  43.2 8.1 %collective-permute-start.8 = (f32[256,128]{1,0:T(8,128)S(1)}, f32[256,128]{1,0:T(8,128)S(1)}, u32[]{:S(2)}, u32[]{:S(2)}) collective-permute-start(f32[256,128]{1,0:T(8,128)S(1)} %add_multiply_fusion.refs_3_.refs_1_), channel_id=1, source_target_pairs={{0,4},{4,0},{8,12},{12,8},{16,20},{20,16},{24,28},{28,24},{1,5},{5... | collective-permute-start | bytes 393224 | tf_op jit(solution)/shard_map/ppermute | solution.py:49
  43.4 7.9 %collective-permute-start.9 = (f32[256,128]{1,0:T(8,128)S(1)}, f32[256,128]{1,0:T(8,128)S(1)}, u32[]{:S(2)}, u32[]{:S(2)}) collective-permute-start(f32[256,128]{1,0:T(8,128)S(1)} %add_multiply_fusion.refs_3_.refs_1_), channel_id=1, source_target_pairs={{0,8},{4,12},{8,0},{12,4},{16,24},{20,28},{24,16},{28,20},{1,9},{5... | collective-permute-start | bytes 393224 | tf_op jit(solution)/shard_map/ppermute | solution.py:49
  53.0 1.7 %collective-permute-start.14 = (f32[80,1024]{1,0:T(8,128)S(1)}, f32[80,1024]{1,0:T(8,128)S(1)}, u32[]{:S(2)}, u32[]{:S(2)}) collective-permute-start(f32[80,1024]{1,0:T(8,128)S(1)} %get-tuple-element.65), channel_id=1, source_target_pairs={{0,1},{1,0},{2,3},{3,2},{4,5},{5,4},{6,7},{7,6},{8,9},{9,8},{10,11... | collective-permute-start | bytes 983048 | tf_op jit(solution)/shard_map/ppermute | solution.py:49
  55.3 7.4 %collective-permute-start.17 = (f32[32,1024]{1,0:T(8,128)S(1)}, f32[32,1024]{1,0:T(8,128)S(1)}, u32[]{:S(2)}, u32[]{:S(2)}) collective-permute-start(f32[32,1024]{1,0:T(8,128)S(1)} %get-tuple-element.69), channel_id=1, source_target_pairs={{0,2},{1,3},{2,0},{3,1},{4,6},{5,7},{6,4},{7,5},{8,10},{9,11},{10,... | collective-permute-start | bytes 393224 | tf_op jit(solution)/shard_map/ppermute | solution.py:49
  56.9 5.8 %collective-permute-start.15 = (f32[16,1024]{1,0:T(8,128)S(1)}, f32[16,1024]{1,0:T(8,128)S(1)}, u32[]{:S(2)}, u32[]{:S(2)}) collective-permute-start(f32[16,1024]{1,0:T(8,128)S(1)} %get-tuple-element.67), channel_id=1, source_target_pairs={{0,6},{1,7},{2,4},{3,5},{4,2},{5,3},{6,0},{7,1},{8,14},{9,15},{10,... | collective-permute-start | bytes 196616 | tf_op jit(solution)/shard_map/ppermute | solution.py:49
  58.2 4.4 %collective-permute-start.16 = (f32[16,1024]{1,0:T(8,128)S(1)}, f32[16,1024]{1,0:T(8,128)S(1)}, u32[]{:S(2)}, u32[]{:S(2)}) collective-permute-start(f32[16,1024]{1,0:T(8,128)S(1)} %get-tuple-element.68), channel_id=1, source_target_pairs={{0,4},{4,0},{8,12},{12,8},{16,20},{20,16},{24,28},{28,24},{1,5},{5... | collective-permute-start | bytes 196616 | tf_op jit(solution)/shard_map/ppermute | solution.py:49
  62.7 8.9 %collective-permute-start.18 = (f32[16,1024]{1,0:T(8,128)S(1)}, f32[16,1024]{1,0:T(8,128)S(1)}, u32[]{:S(2)}, u32[]{:S(2)}) collective-permute-start(f32[16,1024]{1,0:T(8,128)S(1)} %slice_add_fusion), channel_id=1, source_target_pairs={{0,24},{4,28},{8,16},{12,20},{16,8},{20,12},{24,0},{28,4},{1,25},{... | collective-permute-start | bytes 196616 | tf_op jit(solution)/shard_map/ppermute | solution.py:49
  66.9 5.9 %collective-permute-start.19 = (f32[16,1024]{1,0:T(8,128)S(1)}, f32[16,1024]{1,0:T(8,128)S(1)}, u32[]{:S(2)}, u32[]{:S(2)}) collective-permute-start(f32[16,1024]{1,0:T(8,128)S(1)} %slice_add_fusion), channel_id=1, source_target_pairs={{0,16},{4,20},{8,24},{12,28},{16,0},{20,4},{24,8},{28,12},{1,17},{... | collective-permute-start | bytes 196616 | tf_op jit(solution)/shard_map/ppermute | solution.py:49
  67.5 5.2 %collective-permute-start.20 = (f32[16,1024]{1,0:T(8,128)S(1)}, f32[16,1024]{1,0:T(8,128)S(1)}, u32[]{:S(2)}, u32[]{:S(2)}) collective-permute-start(f32[16,1024]{1,0:T(8,128)S(1)} %slice_add_fusion), channel_id=1, source_target_pairs={{0,8},{4,12},{8,0},{12,4},{16,24},{20,28},{24,16},{28,20},{1,9},{5... | collective-permute-start | bytes 196616 | tf_op jit(solution)/shard_map/ppermute | solution.py:49
  72.8 7.1 %collective-permute-start.21 = (f32[16,1024]{1,0:T(8,128)S(1)}, f32[16,1024]{1,0:T(8,128)S(1)}, u32[]{:S(2)}, u32[]{:S(2)}) collective-permute-start(f32[16,1024]{1,0:T(8,128)S(1)} %add_add_fusion.2.token), channel_id=1, source_target_pairs={{0,2},{1,3},{2,0},{3,1},{4,6},{5,7},{6,4},{7,5},{8,10},{9,11},{10,... | collective-permute-start | bytes 196616 | tf_op jit(solution)/shard_map/ppermute | solution.py:49
  74.2 5.6 %collective-permute-start.22 = (f32[16,1024]{1,0:T(8,128)S(1)}, f32[16,1024]{1,0:T(8,128)S(1)}, u32[]{:S(2)}, u32[]{:S(2)}) collective-permute-start(f32[16,1024]{1,0:T(8,128)S(1)} %add_add_fusion.2.token), channel_id=1, source_target_pairs={{0,4},{4,0},{8,12},{12,8},{16,20},{20,16},{24,28},{28,24},{1,5},{5... | collective-permute-start | bytes 196616 | tf_op jit(solution)/shard_map/ppermute | solution.py:49
  75.4 5.2 %collective-permute-start.23 = (f32[16,1024]{1,0:T(8,128)S(1)}, f32[16,1024]{1,0:T(8,128)S(1)}, u32[]{:S(2)}, u32[]{:S(2)}) collective-permute-start(f32[16,1024]{1,0:T(8,128)S(1)} %add_add_fusion.2.token), channel_id=1, source_target_pairs={{0,6},{1,7},{2,4},{3,5},{4,2},{5,3},{6,0},{7,1},{8,14},{9,15},{10,... | collective-permute-start | bytes 196616 | tf_op jit(solution)/shard_map/ppermute | solution.py:49
  80.7 2.4 %collective-permute-start.24 = (f32[64,1024]{1,0:T(8,128)S(1)}, f32[64,1024]{1,0:T(8,128)S(1)}, u32[]{:S(2)}, u32[]{:S(2)}) collective-permute-start(f32[64,1024]{1,0:T(8,128)S(1)} %constant_dynamic-update-slice_fusion.right_here), channel_id=1, source_target_pairs={{0,1},{1,0},{2,3},{3,2},{4,5},{5,4},{6,7},{7,6},{8,9},{9,8},{10,11... | collective-permute-start | bytes 786440 | tf_op jit(solution)/shard_map/ppermute | solution.py:49
